TPU v7x, 128 devices: a whole 4x4x4 slice. The times are simulated.
128 devices in a mesh: leaf: 32 (over z, y, core), sub: 4 (over x).
Axes of the slice: x: 4, y: 4, z: 4, core: 2. Of those that a mesh axis runs over, the one named last changes fastest.
Arguments:
- volume_fraction: float32 [256, 64, 1024], P('leaf', 'sub'), may hold values from 0 to 1
- interface_mask: int32 [256, 64, 1024], P('leaf', 'sub'), may hold values 0 or 1
Outputs:
- pressure: float32 [256, 64, 1024], P('leaf', 'sub')
- residual: float32 [256, 64, 1024], P('leaf', 'sub')
All inputs are finite; a program needn't handle non-finite values. No bound on the sum of `interface_mask` on one device may be relied on, other than what follows from the above.
Results may differ from a plain program's by a relative error of at most 0.0003.
Values sent between devices are 32-bit elements; how exact they have to be, the bound alone decides.
No kernel may reach another device: no remote copies, remote signals or barrier semaphores. Data moves between devices by JAX's collectives and lax.ppermute only.
A program may use at most 128 MiB of HBM per device.

v0:
```python
import jax
import jax.numpy as jnp
from jax import lax
from jax.sharding import PartitionSpec as P

LEV = 3
NU = 2
COARSE = 8


damping = 0.8 / 6.0


def extended(shard, sides, width):
    for axis, dim in sides:
        devices, length = (lax.axis_size(axis), shard.shape[dim])
        up = [(i, (i + 1) % devices) for i in range(devices - 1)]
        down = [(j, i) for i, j in up]
        last = lax.slice_in_dim(shard, length - width, length, axis=dim)
        first = lax.slice_in_dim(shard, 0, width, axis=dim)
        before = lax.ppermute(last, axis, up)
        after = lax.ppermute(first, axis, down)
        shard = jnp.concatenate([before, shard, after], axis=dim)
    return shard


def neighbours(padded):
    total = padded[2:, 1:-1, 1:-1] + padded[:-2, 1:-1, 1:-1]
    total = total + padded[1:-1, 2:, 1:-1] + padded[1:-1, :-2, 1:-1]
    total = total + padded[1:-1, 1:-1, 2:] + padded[1:-1, 1:-1, :-2]
    return total


def apply_op(field):
    padded = extended(field, (("leaf", 0), ("sub", 1)), 1)
    padded = jnp.pad(padded, ((0, 0), (0, 0), (1, 1)))
    return 6.0 * field - neighbours(padded)


def sweep(field, rhs):
    return field + damping * (rhs - apply_op(field))


def apply_column(field):
    padded = extended(field, (("leaf", 0),), 1)
    padded = jnp.pad(padded, ((0, 0), (1, 1), (1, 1)))
    return 6.0 * field - neighbours(padded)


def restrict(field):
    nx, ny, nz = field.shape
    return 0.5 * field.reshape(nx // 2, 2, ny // 2, 2, nz // 2, 2).sum(axis=(1, 3, 5))


def prolong(field):
    return jnp.repeat(jnp.repeat(jnp.repeat(field, 2, 0), 2, 1), 2, 2)


def curvature_source(volume_fraction, interface_mask):
    depth = volume_fraction.shape[2]
    column = jnp.pad(volume_fraction, ((0, 0), (0, 0), (3, 3)))
    heights = column[:, :, 0:depth]
    for shift in range(1, 7):
        heights = heights + column[:, :, shift : shift + depth]
    padded = extended(heights, (("leaf", 0), ("sub", 1)), 1)
    upper_x = padded[2:, 1:-1]
    lower_x = padded[:-2, 1:-1]
    upper_y = padded[1:-1, 2:]
    lower_y = padded[1:-1, :-2]
    slope_x = 0.5 * (upper_x - lower_x)
    slope_y = 0.5 * (upper_y - lower_y)
    bend = upper_x - 2.0 * heights + lower_x + (upper_y - 2.0 * heights + lower_y)
    factor = 1.0 + slope_x * slope_x + slope_y * slope_y
    curvature = bend / (factor * jnp.sqrt(factor))
    grad_z = 0.5 * (column[:, :, 4 : depth + 4] - column[:, :, 2 : depth + 2])
    return interface_mask.astype(jnp.float32) * curvature * grad_z


def shards(volume_fraction, interface_mask):
    source = curvature_source(volume_fraction, interface_mask)
    rhs = source
    stored = []
    rights = []
    for level in range(LEV):
        field = jnp.zeros_like(rhs)
        for step in range(NU):
            field = sweep(field, rhs)
        remain = rhs - apply_op(field)
        stored.append(field)
        rights.append(rhs)
        rhs = restrict(remain)
    local_y = rhs.shape[1]
    row_rhs = lax.all_gather(rhs, "sub", axis=1, tiled=True)
    field = jnp.zeros_like(row_rhs)
    for step in range(COARSE):
        field = field + damping * (row_rhs - apply_column(field))
    field = lax.dynamic_slice_in_dim(field, lax.axis_index("sub") * local_y, local_y, 1)
    for level in range(LEV - 1, -1, -1):
        field = stored[level] + prolong(field)
        for step in range(NU):
            field = sweep(field, rights[level])
    return (field, source - apply_op(field))


def solution(mesh):
    in_specs = (P("leaf", "sub", None), P("leaf", "sub", None))
    out_specs = (P("leaf", "sub", None), P("leaf", "sub", None))
    return jax.shard_map(shards, mesh=mesh, in_specs=in_specs, out_specs=out_specs, check_vma=False)
```

profile of v0, /device:TPU:102, one launch (start us, length us, event | category | flops | bytes accessed | tf_op | source)
XLA Modules:
  0.0 423.4 jit_solution(5792530443309748026)
XLA Ops:
  0.6 4.2 collective-permute-start.4
  6.8 3.8 fusion.6
  10.6 5.8 %collective-permute-start = (f32[1,16,1024]{2,1,0:T(8,128)S(1)}, f32[1,16,1024]{2,1,0:T(8,128)S(1)}, u32[]{:S(2)}, u32[]{:S(2)}) collective-permute-start(f32[1,16,1024]{2,1,0:T(8,128)S(1)} %get-tuple-element.44), channel_id=1, source_target_pairs={{4,0},{8,4},{12,8},{16,12},{20,16},{24,20},{28,24},{32,28},{36,32}... | collective-permute-start | bytes 196616 | tf_op jit(solution)/shard_map/ppermute | solution.py:22
  18.4 2.7 collective-permute-start.6
  24.1 3.1 collective-permute-start.2
  29.2 4.0 collective-permute-done.3
  34.3 3.8 collective-permute-start.8
  40.0 5.8 %collective-permute-done.9 = f32[1,16,1024]{2,1,0:T(8,128)S(1)} collective-permute-done((f32[1,16,1024]{2,1,0:T(8,128)S(1)}, f32[1,16,1024]{2,1,0:T(8,128)S(1)}, u32[]{:S(2)}, u32[]{:S(2)}) %collective-permute-start.9) | collective-permute-done | bytes 65568 | tf_op jit(solution)/shard_map/ppermute | solution.py:21
  45.8 2.4 collective-permute-start.10
  55.2 5.0 %collective-permute-start.12 = (f32[1,16,1024]{2,1,0:T(8,128)S(1)}, f32[1,16,1024]{2,1,0:T(8,128)S(1)}, u32[]{:S(2)}, u32[]{:S(2)}) collective-permute-start(f32[1,16,1024]{2,1,0:T(8,128)S(1)} %get-tuple-element.40), channel_id=1, source_target_pairs={{4,0},{8,4},{12,8},{16,12},{20,16},{24,20},{28,24},{32,28},{36,32}... | collective-permute-start | bytes 196616 | tf_op jit(solution)/shard_map/ppermute | solution.py:22
  62.3 4.5 %collective-permute-start.18 = (f32[6,1,512]{2,1,0:T(1,128)S(1)}, f32[6,1,512]{2,1,0:T(1,128)S(1)}, u32[]{:S(2)}, u32[]{:S(2)}) collective-permute-start(f32[6,1,512]{2,1,0:T(1,128)S(1)} %get-tuple-element.54), channel_id=1, source_target_pairs={{1,0},{2,1},{3,2},{5,4},{6,5},{7,6},{9,8},{10,9},{11,10},{13,12},{... | collective-permute-start | bytes 36872 | tf_op jit(solution)/shard_map/ppermute | solution.py:22
  68.2 4.5 %collective-permute-start.14 = (f32[10,1,1024]{2,1,0:T(1,128)S(1)}, f32[10,1,1024]{2,1,0:T(1,128)S(1)}, u32[]{:S(2)}, u32[]{:S(2)}) collective-permute-start(f32[10,1,1024]{2,1,0:T(1,128)S(1)} %get-tuple-element.26), channel_id=1, source_target_pairs={{1,0},{2,1},{3,2},{5,4},{6,5},{7,6},{9,8},{10,9},{11,10},{13,12},{... | collective-permute-start | bytes 122888 | tf_op jit(solution)/shard_map/ppermute | solution.py:22
  74.4 4.2 %collective-permute-done.15 = f32[10,1,1024]{2,1,0:T(1,128)S(1)} collective-permute-done((f32[10,1,1024]{2,1,0:T(1,128)S(1)}, f32[10,1,1024]{2,1,0:T(1,128)S(1)}, u32[]{:S(2)}, u32[]{:S(2)}) %collective-permute-start.15) | collective-permute-done | bytes 40992 | tf_op jit(solution)/shard_map/ppermute | solution.py:21
  79.6 34.8 %reshape.47 = f32[4,2,8,2,512,2]{5,4,3,2,1,0:T(8,128)} reshape(f32[8,16,1024]{2,1,0:T(8,128)S(1)} %fusion.37) | data formatting | bytes 1048576 | tf_op jit(solution)/shard_map/reshape | solution.py:52
  114.4 12.2 %reduce_sum.34 = f32[4,8,512]{2,1,0:T(8,128)S(1)} reduce(f32[4,2,8,2,512,2]{5,4,3,2,1,0:T(8,128)} %reshape.47, f32[]{:T(128)} %constant.11.clone.1), dimensions={1,3,5}, to_apply=%region_0.1 | reduce | flops 114688 | bytes 589828 | tf_op jit(solution)/shard_map/reduce_sum | solution.py:52
  126.8 3.8 collective-permute-start.20
  132.5 5.2 %collective-permute-done.21 = f32[1,8,512]{2,1,0:T(8,128)S(1)} collective-permute-done((f32[1,8,512]{2,1,0:T(8,128)S(1)}, f32[1,8,512]{2,1,0:T(8,128)S(1)}, u32[]{:S(2)}, u32[]{:S(2)}) %collective-permute-start.21) | collective-permute-done | bytes 16416 | tf_op jit(solution)/shard_map/ppermute | solution.py:21
  137.7 2.4 collective-permute-start.22
  143.4 2.4 collective-permute-start.29
  146.2 5.3 %collective-permute-start.24 = (f32[1,8,512]{2,1,0:T(8,128)S(1)}, f32[1,8,512]{2,1,0:T(8,128)S(1)}, u32[]{:S(2)}, u32[]{:S(2)}) collective-permute-start(f32[1,8,512]{2,1,0:T(8,128)S(1)} %get-tuple-element.60), channel_id=1, source_target_pairs={{4,0},{8,4},{12,8},{16,12},{20,16},{24,20},{28,24},{32,28},{36,32}... | collective-permute-start | bytes 49160 | tf_op jit(solution)/shard_map/ppermute | solution.py:22
  153.4 4.5 %collective-permute-start.30 = (f32[4,1,256]{2,1,0:T(1,128)S(1)}, f32[4,1,256]{2,1,0:T(1,128)S(1)}, u32[]{:S(2)}, u32[]{:S(2)}) collective-permute-start(f32[4,1,256]{2,1,0:T(1,128)S(1)} %get-tuple-element.72), channel_id=1, source_target_pairs={{1,0},{2,1},{3,2},{5,4},{6,5},{7,6},{9,8},{10,9},{11,10},{13,12},{... | collective-permute-start | bytes 12296 | tf_op jit(solution)/shard_map/ppermute | solution.py:22
  159.3 4.5 %collective-permute-start.26 = (f32[6,1,512]{2,1,0:T(1,128)S(1)}, f32[6,1,512]{2,1,0:T(1,128)S(1)}, u32[]{:S(2)}, u32[]{:S(2)}) collective-permute-start(f32[6,1,512]{2,1,0:T(1,128)S(1)} %get-tuple-element.50), channel_id=1, source_target_pairs={{1,0},{2,1},{3,2},{5,4},{6,5},{7,6},{9,8},{10,9},{11,10},{13,12},{... | collective-permute-start | bytes 36872 | tf_op jit(solution)/shard_map/ppermute | solution.py:22
  165.3 4.1 collective-permute-done.27
  169.8 5.6 %reshape.48 = f32[2,2,4,2,256,2]{5,4,3,2,1,0:T(8,128)} reshape(f32[4,8,512]{2,1,0:T(8,128)S(1)} %fusion.71) | data formatting | bytes 131072 | tf_op jit(solution)/shard_map/reshape | solution.py:52
  175.3 2.5 reduce_sum.35
  178.0 3.8 collective-permute-start.32
  183.7 5.1 %collective-permute-done.33 = f32[1,4,256]{2,1,0:T(4,128)S(1)} collective-permute-done((f32[1,4,256]{2,1,0:T(4,128)S(1)}, f32[1,4,256]{2,1,0:T(4,128)S(1)}, u32[]{:S(2)}, u32[]{:S(2)}) %collective-permute-start.33) | collective-permute-done | bytes 4128 | tf_op jit(solution)/shard_map/ppermute | solution.py:21
  192.3 4.2 collective-permute-done.35
  201.1 5.3 %collective-permute-start.40 = (f32[1,8,128]{2,1,0:T(8,128)S(1)}, f32[1,8,128]{2,1,0:T(8,128)S(1)}, u32[]{:S(2)}, u32[]{:S(2)}) collective-permute-start(f32[1,8,128]{2,1,0:T(8,128)S(1)} %broadcast.149), channel_id=1, source_target_pairs={{4,0},{8,4},{12,8},{16,12},{20,16},{24,20},{28,24},{32,28},{36,32}... | collective-permute-start | bytes 12296 | tf_op jit(solution)/shard_map/ppermute | solution.py:22
  213.5 2.5 collective-permute-done.39
  216.6 6.7 %all-gather.1 = f32[4,2,128]{2,1,0:T(2,128)S(1)} all-gather(f32[1,2,128]{2,1,0:T(2,128)S(1)} %multiply_bitcast_fusion), channel_id=2, replica_groups=mesh['leaf'=32,'sub'=4] {'sub'}, dimensions={0}, use_global_device_ids=true | all-gather | bytes 5120 | tf_op jit(solution)/shard_map/all_gather | solution.py:93
  223.4 2.6 collective-permute-start.42
  227.9 5.1 %collective-permute-done.43 = f32[1,8,128]{2,1,0:T(8,128)S(1)} collective-permute-done((f32[1,8,128]{2,1,0:T(8,128)S(1)}, f32[1,8,128]{2,1,0:T(8,128)S(1)}, u32[]{:S(2)}, u32[]{:S(2)}) %collective-permute-start.43) | collective-permute-done | bytes 4128 | tf_op jit(solution)/shard_map/ppermute | solution.py:21
  235.1 2.4 collective-permute-start.45
  237.5 4.6 %collective-permute-done.45 = f32[1,8,128]{2,1,0:T(8,128)S(1)} collective-permute-done((f32[1,8,128]{2,1,0:T(8,128)S(1)}, f32[1,8,128]{2,1,0:T(8,128)S(1)}, u32[]{:S(2)}, u32[]{:S(2)}) %collective-permute-start.45) | collective-permute-done | bytes 4128 | tf_op jit(solution)/shard_map/ppermute | solution.py:21
  244.2 2.4 collective-permute-start.47
  246.6 4.6 %collective-permute-done.47 = f32[1,8,128]{2,1,0:T(8,128)S(1)} collective-permute-done((f32[1,8,128]{2,1,0:T(8,128)S(1)}, f32[1,8,128]{2,1,0:T(8,128)S(1)}, u32[]{:S(2)}, u32[]{:S(2)}) %collective-permute-start.47) | collective-permute-done | bytes 4128 | tf_op jit(solution)/shard_map/ppermute | solution.py:21
  253.3 2.4 collective-permute-start.49
  255.8 4.6 %collective-permute-done.49 = f32[1,8,128]{2,1,0:T(8,128)S(1)} collective-permute-done((f32[1,8,128]{2,1,0:T(8,128)S(1)}, f32[1,8,128]{2,1,0:T(8,128)S(1)}, u32[]{:S(2)}, u32[]{:S(2)}) %collective-permute-start.49) | collective-permute-done | bytes 4128 | tf_op jit(solution)/shard_map/ppermute | solution.py:21
  262.5 2.4 collective-permute-start.51
  264.9 4.6 %collective-permute-done.51 = f32[1,8,128]{2,1,0:T(8,128)S(1)} collective-permute-done((f32[1,8,128]{2,1,0:T(8,128)S(1)}, f32[1,8,128]{2,1,0:T(8,128)S(1)}, u32[]{:S(2)}, u32[]{:S(2)}) %collective-permute-start.51) | collective-permute-done | bytes 4128 | tf_op jit(solution)/shard_map/ppermute | solution.py:21
  271.6 2.4 collective-permute-start.53
  274.0 4.6 %collective-permute-done.53 = f32[1,8,128]{2,1,0:T(8,128)S(1)} collective-permute-done((f32[1,8,128]{2,1,0:T(8,128)S(1)}, f32[1,8,128]{2,1,0:T(8,128)S(1)}, u32[]{:S(2)}, u32[]{:S(2)}) %collective-permute-start.53) | collective-permute-done | bytes 4128 | tf_op jit(solution)/shard_map/ppermute | solution.py:21
  280.7 2.4 collective-permute-start.55
  283.1 4.6 %collective-permute-done.55 = f32[1,8,128]{2,1,0:T(8,128)S(1)} collective-permute-done((f32[1,8,128]{2,1,0:T(8,128)S(1)}, f32[1,8,128]{2,1,0:T(8,128)S(1)}, u32[]{:S(2)}, u32[]{:S(2)}) %collective-permute-start.55) | collective-permute-done | bytes 4128 | tf_op jit(solution)/shard_map/ppermute | solution.py:21
  290.1 2.4 collective-permute-start.57
  292.5 4.6 %collective-permute-done.57 = f32[1,4,256]{2,1,0:T(4,128)S(1)} collective-permute-done((f32[1,4,256]{2,1,0:T(4,128)S(1)}, f32[1,4,256]{2,1,0:T(4,128)S(1)}, u32[]{:S(2)}, u32[]{:S(2)}) %collective-permute-start.57) | collective-permute-done | bytes 4128 | tf_op jit(solution)/shard_map/ppermute | solution.py:21
  297.2 3.3 collective-permute-start.58
  301.8 4.2 collective-permute-done.59
  310.5 4.6 %collective-permute-done.61 = f32[1,4,256]{2,1,0:T(4,128)S(1)} collective-permute-done((f32[1,4,256]{2,1,0:T(4,128)S(1)}, f32[1,4,256]{2,1,0:T(4,128)S(1)}, u32[]{:S(2)}, u32[]{:S(2)}) %collective-permute-start.61) | collective-permute-done | bytes 4128 | tf_op jit(solution)/shard_map/ppermute | solution.py:21
  315.1 3.1 collective-permute-start.62
  319.6 4.2 collective-permute-done.63
  329.3 4.7 %collective-permute-done.65 = f32[1,8,512]{2,1,0:T(8,128)S(1)} collective-permute-done((f32[1,8,512]{2,1,0:T(8,128)S(1)}, f32[1,8,512]{2,1,0:T(8,128)S(1)}, u32[]{:S(2)}, u32[]{:S(2)}) %collective-permute-start.65) | collective-permute-done | bytes 16416 | tf_op jit(solution)/shard_map/ppermute | solution.py:21
  334.1 3.9 collective-permute-start.66
  339.4 4.2 collective-permute-done.67
  348.3 4.7 %collective-permute-done.69 = f32[1,8,512]{2,1,0:T(8,128)S(1)} collective-permute-done((f32[1,8,512]{2,1,0:T(8,128)S(1)}, f32[1,8,512]{2,1,0:T(8,128)S(1)}, u32[]{:S(2)}, u32[]{:S(2)}) %collective-permute-start.69) | collective-permute-done | bytes 16416 | tf_op jit(solution)/shard_map/ppermute | solution.py:21
  356.3 4.2 collective-permute-done.71
  364.2 2.8 copy.255
  371.4 5.3 %collective-permute-done.73 = f32[1,16,1024]{2,1,0:T(8,128)S(1)} collective-permute-done((f32[1,16,1024]{2,1,0:T(8,128)S(1)}, f32[1,16,1024]{2,1,0:T(8,128)S(1)}, u32[]{:S(2)}, u32[]{:S(2)}) %collective-permute-start.73) | collective-permute-done | bytes 65568 | tf_op jit(solution)/shard_map/ppermute | solution.py:21
  380.3 4.2 %collective-permute-done.75 = f32[10,1,1024]{2,1,0:T(1,128)S(1)} collective-permute-done((f32[10,1,1024]{2,1,0:T(1,128)S(1)}, f32[10,1,1024]{2,1,0:T(1,128)S(1)}, u32[]{:S(2)}, u32[]{:S(2)}) %collective-permute-start.75) | collective-permute-done | bytes 40992 | tf_op jit(solution)/shard_map/ppermute | solution.py:21
  390.0 5.3 %collective-permute-done.77 = f32[1,16,1024]{2,1,0:T(8,128)S(1)} collective-permute-done((f32[1,16,1024]{2,1,0:T(8,128)S(1)}, f32[1,16,1024]{2,1,0:T(8,128)S(1)}, u32[]{:S(2)}, u32[]{:S(2)}) %collective-permute-start.77) | collective-permute-done | bytes 65568 | tf_op jit(solution)/shard_map/ppermute | solution.py:21
  398.9 4.2 %collective-permute-done.79 = f32[10,1,1024]{2,1,0:T(1,128)S(1)} collective-permute-done((f32[10,1,1024]{2,1,0:T(1,128)S(1)}, f32[10,1,1024]{2,1,0:T(1,128)S(1)}, u32[]{:S(2)}, u32[]{:S(2)}) %collective-permute-start.79) | collective-permute-done | bytes 40992 | tf_op jit(solution)/shard_map/ppermute | solution.py:21
  408.5 5.3 %collective-permute-done.81 = f32[1,16,1024]{2,1,0:T(8,128)S(1)} collective-permute-done((f32[1,16,1024]{2,1,0:T(8,128)S(1)}, f32[1,16,1024]{2,1,0:T(8,128)S(1)}, u32[]{:S(2)}, u32[]{:S(2)}) %collective-permute-start.81) | collective-permute-done | bytes 65568 | tf_op jit(solution)/shard_map/ppermute | solution.py:21
  417.4 4.2 %collective-permute-done.83 = f32[10,1,1024]{2,1,0:T(1,128)S(1)} collective-permute-done((f32[10,1,1024]{2,1,0:T(1,128)S(1)}, f32[10,1,1024]{2,1,0:T(1,128)S(1)}, u32[]{:S(2)}, u32[]{:S(2)}) %collective-permute-start.83) | collective-permute-done | bytes 40992 | tf_op jit(solution)/shard_map/ppermute | solution.py:21
  (228 shorter events, 122.8 us)
Async XLA Ops:
  0.6 17.6 %collective-permute-start.4 = (f32[1,16,1024]{2,1,0:T(8,128)S(1)}, f32[1,16,1024]{2,1,0:T(8,128)S(1)}, u32[]{:S(2)}, u32[]{:S(2)}) collective-permute-start(f32[1,16,1024]{2,1,0:T(8,128)S(1)} %broadcast.138), channel_id=1, source_target_pairs={{4,0},{8,4},{12,8},{16,12},{20,16},{24,20},{28,24},{32,28},{36,32}... | collective-permute-start | bytes 196616 | tf_op jit(solution)/shard_map/ppermute | solution.py:22
  4.9 13.4 %collective-permute-start.5 = (f32[1,16,1024]{2,1,0:T(8,128)S(1)}, f32[1,16,1024]{2,1,0:T(8,128)S(1)}, u32[]{:S(2)}, u32[]{:S(2)}) collective-permute-start(f32[1,16,1024]{2,1,0:T(8,128)S(1)} %broadcast.138), channel_id=1, source_target_pairs={{0,4},{4,8},{8,12},{12,16},{16,20},{20,24},{24,28},{28,32},{32,36}... | collective-permute-start | bytes 196616 | tf_op jit(solution)/shard_map/ppermute | solution.py:21
  10.6 11.9 %collective-permute-start = (f32[1,16,1024]{2,1,0:T(8,128)S(1)}, f32[1,16,1024]{2,1,0:T(8,128)S(1)}, u32[]{:S(2)}, u32[]{:S(2)}) collective-permute-start(f32[1,16,1024]{2,1,0:T(8,128)S(1)} %get-tuple-element.44), channel_id=1, source_target_pairs={{4,0},{8,4},{12,8},{16,12},{20,16},{24,20},{28,24},{32,28},{36,32}... | collective-permute-start | bytes 196616 | tf_op jit(solution)/shard_map/ppermute | solution.py:22
  16.4 7.7 %collective-permute-start.1 = (f32[1,16,1024]{2,1,0:T(8,128)S(1)}, f32[1,16,1024]{2,1,0:T(8,128)S(1)}, u32[]{:S(2)}, u32[]{:S(2)}) collective-permute-start(f32[1,16,1024]{2,1,0:T(8,128)S(1)} %get-tuple-element.43), channel_id=1, source_target_pairs={{0,4},{4,8},{8,12},{12,16},{16,20},{20,24},{24,28},{28,32},{32,36}... | collective-permute-start | bytes 196616 | tf_op jit(solution)/shard_map/ppermute | solution.py:21
  18.4 10.1 %collective-permute-start.6 = (f32[10,1,1024]{2,1,0:T(1,128)S(1)}, f32[10,1,1024]{2,1,0:T(1,128)S(1)}, u32[]{:S(2)}, u32[]{:S(2)}) collective-permute-start(f32[10,1,1024]{2,1,0:T(1,128)S(1)} %get-tuple-element.32), channel_id=1, source_target_pairs={{1,0},{2,1},{3,2},{5,4},{6,5},{7,6},{9,8},{10,9},{11,10},{13,12},{... | collective-permute-start | bytes 122888 | tf_op jit(solution)/shard_map/ppermute | solution.py:22
  21.2 7.4 %collective-permute-start.7 = (f32[10,1,1024]{2,1,0:T(1,128)S(1)}, f32[10,1,1024]{2,1,0:T(1,128)S(1)}, u32[]{:S(2)}, u32[]{:S(2)}) collective-permute-start(f32[10,1,1024]{2,1,0:T(1,128)S(1)} %get-tuple-element.31), channel_id=1, source_target_pairs={{0,1},{1,2},{2,3},{4,5},{5,6},{6,7},{8,9},{9,10},{10,11},{12,13},{... | collective-permute-start | bytes 122888 | tf_op jit(solution)/shard_map/ppermute | solution.py:21
  24.1 5.0 %collective-permute-start.2 = (f32[10,1,1024]{2,1,0:T(1,128)S(1)}, f32[10,1,1024]{2,1,0:T(1,128)S(1)}, u32[]{:S(2)}, u32[]{:S(2)}) collective-permute-start(f32[10,1,1024]{2,1,0:T(1,128)S(1)} %get-tuple-element.29), channel_id=1, source_target_pairs={{1,0},{2,1},{3,2},{5,4},{6,5},{7,6},{9,8},{10,9},{11,10},{13,12},{... | collective-permute-start | bytes 122888 | tf_op jit(solution)/shard_map/ppermute | solution.py:22
  27.3 5.9 %collective-permute-start.3 = (f32[10,1,1024]{2,1,0:T(1,128)S(1)}, f32[10,1,1024]{2,1,0:T(1,128)S(1)}, u32[]{:S(2)}, u32[]{:S(2)}) collective-permute-start(f32[10,1,1024]{2,1,0:T(1,128)S(1)} %get-tuple-element.30), channel_id=1, source_target_pairs={{0,1},{1,2},{2,3},{4,5},{5,6},{6,7},{8,9},{9,10},{10,11},{12,13},{... | collective-permute-start | bytes 122888 | tf_op jit(solution)/shard_map/ppermute | solution.py:21
  34.3 5.7 %collective-permute-start.8 = (f32[1,16,1024]{2,1,0:T(8,128)S(1)}, f32[1,16,1024]{2,1,0:T(8,128)S(1)}, u32[]{:S(2)}, u32[]{:S(2)}) collective-permute-start(f32[1,16,1024]{2,1,0:T(8,128)S(1)} %get-tuple-element.42), channel_id=1, source_target_pairs={{4,0},{8,4},{12,8},{16,12},{20,16},{24,20},{28,24},{32,28},{36,32}... | collective-permute-start | bytes 196616 | tf_op jit(solution)/shard_map/ppermute | solution.py:22
  38.1 7.7 %collective-permute-start.9 = (f32[1,16,1024]{2,1,0:T(8,128)S(1)}, f32[1,16,1024]{2,1,0:T(8,128)S(1)}, u32[]{:S(2)}, u32[]{:S(2)}) collective-permute-start(f32[1,16,1024]{2,1,0:T(8,128)S(1)} %get-tuple-element.41), channel_id=1, source_target_pairs={{0,4},{4,8},{8,12},{12,16},{16,20},{20,24},{24,28},{28,32},{32,36}... | collective-permute-start | bytes 196616 | tf_op jit(solution)/shard_map/ppermute | solution.py:21
  45.8 8.1 %collective-permute-start.10 = (f32[10,1,1024]{2,1,0:T(1,128)S(1)}, f32[10,1,1024]{2,1,0:T(1,128)S(1)}, u32[]{:S(2)}, u32[]{:S(2)}) collective-permute-start(f32[10,1,1024]{2,1,0:T(1,128)S(1)} %get-tuple-element.28), channel_id=1, source_target_pairs={{1,0},{2,1},{3,2},{5,4},{6,5},{7,6},{9,8},{10,9},{11,10},{13,12},{... | collective-permute-start | bytes 122888 | tf_op jit(solution)/shard_map/ppermute | solution.py:22
  48.3 5.9 %collective-permute-start.11 = (f32[10,1,1024]{2,1,0:T(1,128)S(1)}, f32[10,1,1024]{2,1,0:T(1,128)S(1)}, u32[]{:S(2)}, u32[]{:S(2)}) collective-permute-start(f32[10,1,1024]{2,1,0:T(1,128)S(1)} %get-tuple-element.27), channel_id=1, source_target_pairs={{0,1},{1,2},{2,3},{4,5},{5,6},{6,7},{8,9},{9,10},{10,11},{12,13},{... | collective-permute-start | bytes 122888 | tf_op jit(solution)/shard_map/ppermute | solution.py:21
  49.6 12.6 %collective-permute-start.16 = (f32[1,8,512]{2,1,0:T(8,128)S(1)}, f32[1,8,512]{2,1,0:T(8,128)S(1)}, u32[]{:S(2)}, u32[]{:S(2)}) collective-permute-start(f32[1,8,512]{2,1,0:T(8,128)S(1)} %broadcast.142), channel_id=1, source_target_pairs={{4,0},{8,4},{12,8},{16,12},{20,16},{24,20},{28,24},{32,28},{36,32}... | collective-permute-start | bytes 49160 | tf_op jit(solution)/shard_map/ppermute | solution.py:22
  51.5 10.7 %collective-permute-start.17 = (f32[1,8,512]{2,1,0:T(8,128)S(1)}, f32[1,8,512]{2,1,0:T(8,128)S(1)}, u32[]{:S(2)}, u32[]{:S(2)}) collective-permute-start(f32[1,8,512]{2,1,0:T(8,128)S(1)} %broadcast.142), channel_id=1, source_target_pairs={{0,4},{4,8},{8,12},{12,16},{16,20},{20,24},{24,28},{28,32},{32,36}... | collective-permute-start | bytes 49160 | tf_op jit(solution)/shard_map/ppermute | solution.py:21
  55.2 12.9 %collective-permute-start.12 = (f32[1,16,1024]{2,1,0:T(8,128)S(1)}, f32[1,16,1024]{2,1,0:T(8,128)S(1)}, u32[]{:S(2)}, u32[]{:S(2)}) collective-permute-start(f32[1,16,1024]{2,1,0:T(8,128)S(1)} %get-tuple-element.40), channel_id=1, source_target_pairs={{4,0},{8,4},{12,8},{16,12},{20,16},{24,20},{28,24},{32,28},{36,32}... | collective-permute-start | bytes 196616 | tf_op jit(solution)/shard_map/ppermute | solution.py:22
  60.3 7.9 %collective-permute-start.13 = (f32[1,16,1024]{2,1,0:T(8,128)S(1)}, f32[1,16,1024]{2,1,0:T(8,128)S(1)}, u32[]{:S(2)}, u32[]{:S(2)}) collective-permute-start(f32[1,16,1024]{2,1,0:T(8,128)S(1)} %get-tuple-element.39), channel_id=1, source_target_pairs={{0,4},{4,8},{8,12},{12,16},{16,20},{20,24},{24,28},{28,32},{32,36}... | collective-permute-start | bytes 196616 | tf_op jit(solution)/shard_map/ppermute | solution.py:21
  62.3 11.8 %collective-permute-start.18 = (f32[6,1,512]{2,1,0:T(1,128)S(1)}, f32[6,1,512]{2,1,0:T(1,128)S(1)}, u32[]{:S(2)}, u32[]{:S(2)}) collective-permute-start(f32[6,1,512]{2,1,0:T(1,128)S(1)} %get-tuple-element.54), channel_id=1, source_target_pairs={{1,0},{2,1},{3,2},{5,4},{6,5},{7,6},{9,8},{10,9},{11,10},{13,12},{... | collective-permute-start | bytes 36872 | tf_op jit(solution)/shard_map/ppermute | solution.py:22
  66.8 7.3 %collective-permute-start.19 = (f32[6,1,512]{2,1,0:T(1,128)S(1)}, f32[6,1,512]{2,1,0:T(1,128)S(1)}, u32[]{:S(2)}, u32[]{:S(2)}) collective-permute-start(f32[6,1,512]{2,1,0:T(1,128)S(1)} %get-tuple-element.53), channel_id=1, source_target_pairs={{0,1},{1,2},{2,3},{4,5},{5,6},{6,7},{8,9},{9,10},{10,11},{12,13},{... | collective-permute-start | bytes 36872 | tf_op jit(solution)/shard_map/ppermute | solution.py:21
  68.2 6.2 %collective-permute-start.14 = (f32[10,1,1024]{2,1,0:T(1,128)S(1)}, f32[10,1,1024]{2,1,0:T(1,128)S(1)}, u32[]{:S(2)}, u32[]{:S(2)}) collective-permute-start(f32[10,1,1024]{2,1,0:T(1,128)S(1)} %get-tuple-element.26), channel_id=1, source_target_pairs={{1,0},{2,1},{3,2},{5,4},{6,5},{7,6},{9,8},{10,9},{11,10},{13,12},{... | collective-permute-start | bytes 122888 | tf_op jit(solution)/shard_map/ppermute | solution.py:22
  72.8 5.9 %collective-permute-start.15 = (f32[10,1,1024]{2,1,0:T(1,128)S(1)}, f32[10,1,1024]{2,1,0:T(1,128)S(1)}, u32[]{:S(2)}, u32[]{:S(2)}) collective-permute-start(f32[10,1,1024]{2,1,0:T(1,128)S(1)} %get-tuple-element.25), channel_id=1, source_target_pairs={{0,1},{1,2},{2,3},{4,5},{5,6},{6,7},{8,9},{9,10},{10,11},{12,13},{... | collective-permute-start | bytes 122888 | tf_op jit(solution)/shard_map/ppermute | solution.py:21
  126.8 5.7 %collective-permute-start.20 = (f32[1,8,512]{2,1,0:T(8,128)S(1)}, f32[1,8,512]{2,1,0:T(8,128)S(1)}, u32[]{:S(2)}, u32[]{:S(2)}) collective-permute-start(f32[1,8,512]{2,1,0:T(8,128)S(1)} %get-tuple-element.62), channel_id=1, source_target_pairs={{4,0},{8,4},{12,8},{16,12},{20,16},{24,20},{28,24},{32,28},{36,32}... | collective-permute-start | bytes 49160 | tf_op jit(solution)/shard_map/ppermute | solution.py:22
  130.6 7.2 %collective-permute-start.21 = (f32[1,8,512]{2,1,0:T(8,128)S(1)}, f32[1,8,512]{2,1,0:T(8,128)S(1)}, u32[]{:S(2)}, u32[]{:S(2)}) collective-permute-start(f32[1,8,512]{2,1,0:T(8,128)S(1)} %get-tuple-element.61), channel_id=1, source_target_pairs={{0,4},{4,8},{8,12},{12,16},{16,20},{20,24},{24,28},{28,32},{32,36}... | collective-permute-start | bytes 49160 | tf_op jit(solution)/shard_map/ppermute | solution.py:21
  137.7 8.1 %collective-permute-start.22 = (f32[6,1,512]{2,1,0:T(1,128)S(1)}, f32[6,1,512]{2,1,0:T(1,128)S(1)}, u32[]{:S(2)}, u32[]{:S(2)}) collective-permute-start(f32[6,1,512]{2,1,0:T(1,128)S(1)} %get-tuple-element.52), channel_id=1, source_target_pairs={{1,0},{2,1},{3,2},{5,4},{6,5},{7,6},{9,8},{10,9},{11,10},{13,12},{... | collective-permute-start | bytes 36872 | tf_op jit(solution)/shard_map/ppermute | solution.py:22
  140.2 5.7 %collective-permute-start.23 = (f32[6,1,512]{2,1,0:T(1,128)S(1)}, f32[6,1,512]{2,1,0:T(1,128)S(1)}, u32[]{:S(2)}, u32[]{:S(2)}) collective-permute-start(f32[6,1,512]{2,1,0:T(1,128)S(1)} %get-tuple-element.51), channel_id=1, source_target_pairs={{0,1},{1,2},{2,3},{4,5},{5,6},{6,7},{8,9},{9,10},{10,11},{12,13},{... | collective-permute-start | bytes 36872 | tf_op jit(solution)/shard_map/ppermute | solution.py:21
  141.5 11.9 %collective-permute-start.28 = (f32[1,4,256]{2,1,0:T(4,128)S(1)}, f32[1,4,256]{2,1,0:T(4,128)S(1)}, u32[]{:S(2)}, u32[]{:S(2)}) collective-permute-start(f32[1,4,256]{2,1,0:T(4,128)S(1)} %broadcast.146), channel_id=1, source_target_pairs={{4,0},{8,4},{12,8},{16,12},{20,16},{24,20},{28,24},{32,28},{36,32}... | collective-permute-start | bytes 12296 | tf_op jit(solution)/shard_map/ppermute | solution.py:22
  143.4 10.0 %collective-permute-start.29 = (f32[1,4,256]{2,1,0:T(4,128)S(1)}, f32[1,4,256]{2,1,0:T(4,128)S(1)}, u32[]{:S(2)}, u32[]{:S(2)}) collective-permute-start(f32[1,4,256]{2,1,0:T(4,128)S(1)} %broadcast.146), channel_id=1, source_target_pairs={{0,4},{4,8},{8,12},{12,16},{16,20},{20,24},{24,28},{28,32},{32,36}... | collective-permute-start | bytes 12296 | tf_op jit(solution)/shard_map/ppermute | solution.py:21
  146.2 13.1 %collective-permute-start.24 = (f32[1,8,512]{2,1,0:T(8,128)S(1)}, f32[1,8,512]{2,1,0:T(8,128)S(1)}, u32[]{:S(2)}, u32[]{:S(2)}) collective-permute-start(f32[1,8,512]{2,1,0:T(8,128)S(1)} %get-tuple-element.60), channel_id=1, source_target_pairs={{4,0},{8,4},{12,8},{16,12},{20,16},{24,20},{28,24},{32,28},{36,32}... | collective-permute-start | bytes 49160 | tf_op jit(solution)/shard_map/ppermute | solution.py:22
  151.5 7.8 %collective-permute-start.25 = (f32[1,8,512]{2,1,0:T(8,128)S(1)}, f32[1,8,512]{2,1,0:T(8,128)S(1)}, u32[]{:S(2)}, u32[]{:S(2)}) collective-permute-start(f32[1,8,512]{2,1,0:T(8,128)S(1)} %get-tuple-element.59), channel_id=1, source_target_pairs={{0,4},{4,8},{8,12},{12,16},{16,20},{20,24},{24,28},{28,32},{32,36}... | collective-permute-start | bytes 49160 | tf_op jit(solution)/shard_map/ppermute | solution.py:21
  153.4 11.8 %collective-permute-start.30 = (f32[4,1,256]{2,1,0:T(1,128)S(1)}, f32[4,1,256]{2,1,0:T(1,128)S(1)}, u32[]{:S(2)}, u32[]{:S(2)}) collective-permute-start(f32[4,1,256]{2,1,0:T(1,128)S(1)} %get-tuple-element.72), channel_id=1, source_target_pairs={{1,0},{2,1},{3,2},{5,4},{6,5},{7,6},{9,8},{10,9},{11,10},{13,12},{... | collective-permute-start | bytes 12296 | tf_op jit(solution)/shard_map/ppermute | solution.py:22
  158.0 7.2 %collective-permute-start.31 = (f32[4,1,256]{2,1,0:T(1,128)S(1)}, f32[4,1,256]{2,1,0:T(1,128)S(1)}, u32[]{:S(2)}, u32[]{:S(2)}) collective-permute-start(f32[4,1,256]{2,1,0:T(1,128)S(1)} %get-tuple-element.71), channel_id=1, source_target_pairs={{0,1},{1,2},{2,3},{4,5},{5,6},{6,7},{8,9},{9,10},{10,11},{12,13},{... | collective-permute-start | bytes 12296 | tf_op jit(solution)/shard_map/ppermute | solution.py:21
  159.3 6.0 %collective-permute-start.26 = (f32[6,1,512]{2,1,0:T(1,128)S(1)}, f32[6,1,512]{2,1,0:T(1,128)S(1)}, u32[]{:S(2)}, u32[]{:S(2)}) collective-permute-start(f32[6,1,512]{2,1,0:T(1,128)S(1)} %get-tuple-element.50), channel_id=1, source_target_pairs={{1,0},{2,1},{3,2},{5,4},{6,5},{7,6},{9,8},{10,9},{11,10},{13,12},{... | collective-permute-start | bytes 36872 | tf_op jit(solution)/shard_map/ppermute | solution.py:22
  163.9 5.6 %collective-permute-start.27 = (f32[6,1,512]{2,1,0:T(1,128)S(1)}, f32[6,1,512]{2,1,0:T(1,128)S(1)}, u32[]{:S(2)}, u32[]{:S(2)}) collective-permute-start(f32[6,1,512]{2,1,0:T(1,128)S(1)} %get-tuple-element.49), channel_id=1, source_target_pairs={{0,1},{1,2},{2,3},{4,5},{5,6},{6,7},{8,9},{9,10},{10,11},{12,13},{... | collective-permute-start | bytes 36872 | tf_op jit(solution)/shard_map/ppermute | solution.py:21
  178.0 5.7 %collective-permute-start.32 = (f32[1,4,256]{2,1,0:T(4,128)S(1)}, f32[1,4,256]{2,1,0:T(4,128)S(1)}, u32[]{:S(2)}, u32[]{:S(2)}) collective-permute-start(f32[1,4,256]{2,1,0:T(4,128)S(1)} %get-tuple-element.80), channel_id=1, source_target_pairs={{4,0},{8,4},{12,8},{16,12},{20,16},{24,20},{28,24},{32,28},{36,32}... | collective-permute-start | bytes 12296 | tf_op jit(solution)/shard_map/ppermute | solution.py:22
  181.7 7.0 %collective-permute-start.33 = (f32[1,4,256]{2,1,0:T(4,128)S(1)}, f32[1,4,256]{2,1,0:T(4,128)S(1)}, u32[]{:S(2)}, u32[]{:S(2)}) collective-permute-start(f32[1,4,256]{2,1,0:T(4,128)S(1)} %get-tuple-element.79), channel_id=1, source_target_pairs={{0,4},{4,8},{8,12},{12,16},{16,20},{20,24},{24,28},{28,32},{32,36}... | collective-permute-start | bytes 12296 | tf_op jit(solution)/shard_map/ppermute | solution.py:21
  191.0 5.5 %collective-permute-start.35 = (f32[4,1,256]{2,1,0:T(1,128)S(1)}, f32[4,1,256]{2,1,0:T(1,128)S(1)}, u32[]{:S(2)}, u32[]{:S(2)}) collective-permute-start(f32[4,1,256]{2,1,0:T(1,128)S(1)} %get-tuple-element.69), channel_id=1, source_target_pairs={{0,1},{1,2},{2,3},{4,5},{5,6},{6,7},{8,9},{9,10},{10,11},{12,13},{... | collective-permute-start | bytes 12296 | tf_op jit(solution)/shard_map/ppermute | solution.py:21
  196.7 11.6 %collective-permute-start.36 = (f32[1,4,256]{2,1,0:T(4,128)S(1)}, f32[1,4,256]{2,1,0:T(4,128)S(1)}, u32[]{:S(2)}, u32[]{:S(2)}) collective-permute-start(f32[1,4,256]{2,1,0:T(4,128)S(1)} %get-tuple-element.78), channel_id=1, source_target_pairs={{4,0},{8,4},{12,8},{16,12},{20,16},{24,20},{28,24},{32,28},{36,32}... | collective-permute-start | bytes 12296 | tf_op jit(solution)/shard_map/ppermute | solution.py:22
  198.6 9.6 %collective-permute-start.37 = (f32[1,4,256]{2,1,0:T(4,128)S(1)}, f32[1,4,256]{2,1,0:T(4,128)S(1)}, u32[]{:S(2)}, u32[]{:S(2)}) collective-permute-start(f32[1,4,256]{2,1,0:T(4,128)S(1)} %get-tuple-element.77), channel_id=1, source_target_pairs={{0,4},{4,8},{8,12},{12,16},{16,20},{20,24},{24,28},{28,32},{32,36}... | collective-permute-start | bytes 12296 | tf_op jit(solution)/shard_map/ppermute | solution.py:21
  201.1 10.9 %collective-permute-start.40 = (f32[1,8,128]{2,1,0:T(8,128)S(1)}, f32[1,8,128]{2,1,0:T(8,128)S(1)}, u32[]{:S(2)}, u32[]{:S(2)}) collective-permute-start(f32[1,8,128]{2,1,0:T(8,128)S(1)} %broadcast.149), channel_id=1, source_target_pairs={{4,0},{8,4},{12,8},{16,12},{20,16},{24,20},{28,24},{32,28},{36,32}... | collective-permute-start | bytes 12296 | tf_op jit(solution)/shard_map/ppermute | solution.py:22
  206.3 7.0 %collective-permute-start.41 = (f32[1,8,128]{2,1,0:T(8,128)S(1)}, f32[1,8,128]{2,1,0:T(8,128)S(1)}, u32[]{:S(2)}, u32[]{:S(2)}) collective-permute-start(f32[1,8,128]{2,1,0:T(8,128)S(1)} %broadcast.149), channel_id=1, source_target_pairs={{0,4},{4,8},{8,12},{12,16},{16,20},{20,24},{24,28},{28,32},{32,36}... | collective-permute-start | bytes 12296 | tf_op jit(solution)/shard_map/ppermute | solution.py:21
  208.3 5.2 %collective-permute-start.38 = (f32[4,1,256]{2,1,0:T(1,128)S(1)}, f32[4,1,256]{2,1,0:T(1,128)S(1)}, u32[]{:S(2)}, u32[]{:S(2)}) collective-permute-start(f32[4,1,256]{2,1,0:T(1,128)S(1)} %get-tuple-element.68), channel_id=1, source_target_pairs={{1,0},{2,1},{3,2},{5,4},{6,5},{7,6},{9,8},{10,9},{11,10},{13,12},{... | collective-permute-start | bytes 12296 | tf_op jit(solution)/shard_map/ppermute | solution.py:22
  210.5 5.5 %collective-permute-start.39 = (f32[4,1,256]{2,1,0:T(1,128)S(1)}, f32[4,1,256]{2,1,0:T(1,128)S(1)}, u32[]{:S(2)}, u32[]{:S(2)}) collective-permute-start(f32[4,1,256]{2,1,0:T(1,128)S(1)} %get-tuple-element.67), channel_id=1, source_target_pairs={{0,1},{1,2},{2,3},{4,5},{5,6},{6,7},{8,9},{9,10},{10,11},{12,13},{... | collective-permute-start | bytes 12296 | tf_op jit(solution)/shard_map/ppermute | solution.py:21
  226.0 7.0 %collective-permute-start.43 = (f32[1,8,128]{2,1,0:T(8,128)S(1)}, f32[1,8,128]{2,1,0:T(8,128)S(1)}, u32[]{:S(2)}, u32[]{:S(2)}) collective-permute-start(f32[1,8,128]{2,1,0:T(8,128)S(1)} %get-tuple-element.10), channel_id=1, source_target_pairs={{0,4},{4,8},{8,12},{12,16},{16,20},{20,24},{24,28},{28,32},{32,36}... | collective-permute-start | bytes 12296 | tf_op jit(solution)/shard_map/ppermute | solution.py:21
  235.1 7.0 %collective-permute-start.45 = (f32[1,8,128]{2,1,0:T(8,128)S(1)}, f32[1,8,128]{2,1,0:T(8,128)S(1)}, u32[]{:S(2)}, u32[]{:S(2)}) collective-permute-start(f32[1,8,128]{2,1,0:T(8,128)S(1)} %fusion.147), channel_id=1, source_target_pairs={{0,4},{4,8},{8,12},{12,16},{16,20},{20,24},{24,28},{28,32},{32,36}... | collective-permute-start | bytes 12296 | tf_op jit(solution)/shard_map/ppermute | solution.py:21
  244.2 7.0 %collective-permute-start.47 = (f32[1,8,128]{2,1,0:T(8,128)S(1)}, f32[1,8,128]{2,1,0:T(8,128)S(1)}, u32[]{:S(2)}, u32[]{:S(2)}) collective-permute-start(f32[1,8,128]{2,1,0:T(8,128)S(1)} %fusion.143), channel_id=1, source_target_pairs={{0,4},{4,8},{8,12},{12,16},{16,20},{20,24},{24,28},{28,32},{32,36}... | collective-permute-start | bytes 12296 | tf_op jit(solution)/shard_map/ppermute | solution.py:21
  253.3 7.0 %collective-permute-start.49 = (f32[1,8,128]{2,1,0:T(8,128)S(1)}, f32[1,8,128]{2,1,0:T(8,128)S(1)}, u32[]{:S(2)}, u32[]{:S(2)}) collective-permute-start(f32[1,8,128]{2,1,0:T(8,128)S(1)} %fusion.139), channel_id=1, source_target_pairs={{0,4},{4,8},{8,12},{12,16},{16,20},{20,24},{24,28},{28,32},{32,36}... | collective-permute-start | bytes 12296 | tf_op jit(solution)/shard_map/ppermute | solution.py:21
  262.5 7.0 %collective-permute-start.51 = (f32[1,8,128]{2,1,0:T(8,128)S(1)}, f32[1,8,128]{2,1,0:T(8,128)S(1)}, u32[]{:S(2)}, u32[]{:S(2)}) collective-permute-start(f32[1,8,128]{2,1,0:T(8,128)S(1)} %fusion.135), channel_id=1, source_target_pairs={{0,4},{4,8},{8,12},{12,16},{16,20},{20,24},{24,28},{28,32},{32,36}... | collective-permute-start | bytes 12296 | tf_op jit(solution)/shard_map/ppermute | solution.py:21
  271.6 7.0 %collective-permute-start.53 = (f32[1,8,128]{2,1,0:T(8,128)S(1)}, f32[1,8,128]{2,1,0:T(8,128)S(1)}, u32[]{:S(2)}, u32[]{:S(2)}) collective-permute-start(f32[1,8,128]{2,1,0:T(8,128)S(1)} %fusion.131), channel_id=1, source_target_pairs={{0,4},{4,8},{8,12},{12,16},{16,20},{20,24},{24,28},{28,32},{32,36}... | collective-permute-start | bytes 12296 | tf_op jit(solution)/shard_map/ppermute | solution.py:21
  280.7 7.0 %collective-permute-start.55 = (f32[1,8,128]{2,1,0:T(8,128)S(1)}, f32[1,8,128]{2,1,0:T(8,128)S(1)}, u32[]{:S(2)}, u32[]{:S(2)}) collective-permute-start(f32[1,8,128]{2,1,0:T(8,128)S(1)} %fusion.127), channel_id=1, source_target_pairs={{0,4},{4,8},{8,12},{12,16},{16,20},{20,24},{24,28},{28,32},{32,36}... | collective-permute-start | bytes 12296 | tf_op jit(solution)/shard_map/ppermute | solution.py:21
  290.1 7.0 %collective-permute-start.57 = (f32[1,4,256]{2,1,0:T(4,128)S(1)}, f32[1,4,256]{2,1,0:T(4,128)S(1)}, u32[]{:S(2)}, u32[]{:S(2)}) collective-permute-start(f32[1,4,256]{2,1,0:T(4,128)S(1)} %get-tuple-element.75), channel_id=1, source_target_pairs={{0,4},{4,8},{8,12},{12,16},{16,20},{20,24},{24,28},{28,32},{32,36}... | collective-permute-start | bytes 12296 | tf_op jit(solution)/shard_map/ppermute | solution.py:21
  297.2 4.6 %collective-permute-start.58 = (f32[4,1,256]{2,1,0:T(1,128)S(1)}, f32[4,1,256]{2,1,0:T(1,128)S(1)}, u32[]{:S(2)}, u32[]{:S(2)}) collective-permute-start(f32[4,1,256]{2,1,0:T(1,128)S(1)} %get-tuple-element.66), channel_id=1, source_target_pairs={{1,0},{2,1},{3,2},{5,4},{6,5},{7,6},{9,8},{10,9},{11,10},{13,12},{... | collective-permute-start | bytes 12296 | tf_op jit(solution)/shard_map/ppermute | solution.py:22
  300.4 5.5 %collective-permute-start.59 = (f32[4,1,256]{2,1,0:T(1,128)S(1)}, f32[4,1,256]{2,1,0:T(1,128)S(1)}, u32[]{:S(2)}, u32[]{:S(2)}) collective-permute-start(f32[4,1,256]{2,1,0:T(1,128)S(1)} %get-tuple-element.65), channel_id=1, source_target_pairs={{0,1},{1,2},{2,3},{4,5},{5,6},{6,7},{8,9},{9,10},{10,11},{12,13},{... | collective-permute-start | bytes 12296 | tf_op jit(solution)/shard_map/ppermute | solution.py:21
  308.1 7.0 %collective-permute-start.61 = (f32[1,4,256]{2,1,0:T(4,128)S(1)}, f32[1,4,256]{2,1,0:T(4,128)S(1)}, u32[]{:S(2)}, u32[]{:S(2)}) collective-permute-start(f32[1,4,256]{2,1,0:T(4,128)S(1)} %get-tuple-element.73), channel_id=1, source_target_pairs={{0,4},{4,8},{8,12},{12,16},{16,20},{20,24},{24,28},{28,32},{32,36}... | collective-permute-start | bytes 12296 | tf_op jit(solution)/shard_map/ppermute | solution.py:21
  318.3 5.5 %collective-permute-start.63 = (f32[4,1,256]{2,1,0:T(1,128)S(1)}, f32[4,1,256]{2,1,0:T(1,128)S(1)}, u32[]{:S(2)}, u32[]{:S(2)}) collective-permute-start(f32[4,1,256]{2,1,0:T(1,128)S(1)} %get-tuple-element.63), channel_id=1, source_target_pairs={{0,1},{1,2},{2,3},{4,5},{5,6},{6,7},{8,9},{9,10},{10,11},{12,13},{... | collective-permute-start | bytes 12296 | tf_op jit(solution)/shard_map/ppermute | solution.py:21
  326.9 7.2 %collective-permute-start.65 = (f32[1,8,512]{2,1,0:T(8,128)S(1)}, f32[1,8,512]{2,1,0:T(8,128)S(1)}, u32[]{:S(2)}, u32[]{:S(2)}) collective-permute-start(f32[1,8,512]{2,1,0:T(8,128)S(1)} %get-tuple-element.57), channel_id=1, source_target_pairs={{0,4},{4,8},{8,12},{12,16},{16,20},{20,24},{24,28},{28,32},{32,36}... | collective-permute-start | bytes 49160 | tf_op jit(solution)/shard_map/ppermute | solution.py:21
  334.1 5.3 %collective-permute-start.66 = (f32[6,1,512]{2,1,0:T(1,128)S(1)}, f32[6,1,512]{2,1,0:T(1,128)S(1)}, u32[]{:S(2)}, u32[]{:S(2)}) collective-permute-start(f32[6,1,512]{2,1,0:T(1,128)S(1)} %get-tuple-element.48), channel_id=1, source_target_pairs={{1,0},{2,1},{3,2},{5,4},{6,5},{7,6},{9,8},{10,9},{11,10},{13,12},{... | collective-permute-start | bytes 36872 | tf_op jit(solution)/shard_map/ppermute | solution.py:22
  338.0 5.6 %collective-permute-start.67 = (f32[6,1,512]{2,1,0:T(1,128)S(1)}, f32[6,1,512]{2,1,0:T(1,128)S(1)}, u32[]{:S(2)}, u32[]{:S(2)}) collective-permute-start(f32[6,1,512]{2,1,0:T(1,128)S(1)} %get-tuple-element.47), channel_id=1, source_target_pairs={{0,1},{1,2},{2,3},{4,5},{5,6},{6,7},{8,9},{9,10},{10,11},{12,13},{... | collective-permute-start | bytes 36872 | tf_op jit(solution)/shard_map/ppermute | solution.py:21
  345.8 7.2 %collective-permute-start.69 = (f32[1,8,512]{2,1,0:T(8,128)S(1)}, f32[1,8,512]{2,1,0:T(8,128)S(1)}, u32[]{:S(2)}, u32[]{:S(2)}) collective-permute-start(f32[1,8,512]{2,1,0:T(8,128)S(1)} %get-tuple-element.55), channel_id=1, source_target_pairs={{0,4},{4,8},{8,12},{12,16},{16,20},{20,24},{24,28},{28,32},{32,36}... | collective-permute-start | bytes 49160 | tf_op jit(solution)/shard_map/ppermute | solution.py:21
  354.9 5.6 %collective-permute-start.71 = (f32[6,1,512]{2,1,0:T(1,128)S(1)}, f32[6,1,512]{2,1,0:T(1,128)S(1)}, u32[]{:S(2)}, u32[]{:S(2)}) collective-permute-start(f32[6,1,512]{2,1,0:T(1,128)S(1)} %get-tuple-element.45), channel_id=1, source_target_pairs={{0,1},{1,2},{2,3},{4,5},{5,6},{6,7},{8,9},{9,10},{10,11},{12,13},{... | collective-permute-start | bytes 36872 | tf_op jit(solution)/shard_map/ppermute | solution.py:21
  369.0 7.7 %collective-permute-start.73 = (f32[1,16,1024]{2,1,0:T(8,128)S(1)}, f32[1,16,1024]{2,1,0:T(8,128)S(1)}, u32[]{:S(2)}, u32[]{:S(2)}) collective-permute-start(f32[1,16,1024]{2,1,0:T(8,128)S(1)} %get-tuple-element.37), channel_id=1, source_target_pairs={{0,4},{4,8},{8,12},{12,16},{16,20},{20,24},{24,28},{28,32},{32,36}... | collective-permute-start | bytes 196616 | tf_op jit(solution)/shard_map/ppermute | solution.py:21
  378.7 5.9 %collective-permute-start.75 = (f32[10,1,1024]{2,1,0:T(1,128)S(1)}, f32[10,1,1024]{2,1,0:T(1,128)S(1)}, u32[]{:S(2)}, u32[]{:S(2)}) collective-permute-start(f32[10,1,1024]{2,1,0:T(1,128)S(1)} %get-tuple-element.23), channel_id=1, source_target_pairs={{0,1},{1,2},{2,3},{4,5},{5,6},{6,7},{8,9},{9,10},{10,11},{12,13},{... | collective-permute-start | bytes 122888 | tf_op jit(solution)/shard_map/ppermute | solution.py:21
  387.5 7.7 %collective-permute-start.77 = (f32[1,16,1024]{2,1,0:T(8,128)S(1)}, f32[1,16,1024]{2,1,0:T(8,128)S(1)}, u32[]{:S(2)}, u32[]{:S(2)}) collective-permute-start(f32[1,16,1024]{2,1,0:T(8,128)S(1)} %get-tuple-element.35), channel_id=1, source_target_pairs={{0,4},{4,8},{8,12},{12,16},{16,20},{20,24},{24,28},{28,32},{32,36}... | collective-permute-start | bytes 196616 | tf_op jit(solution)/shard_map/ppermute | solution.py:21
  397.2 5.9 %collective-permute-start.79 = (f32[10,1,1024]{2,1,0:T(1,128)S(1)}, f32[10,1,1024]{2,1,0:T(1,128)S(1)}, u32[]{:S(2)}, u32[]{:S(2)}) collective-permute-start(f32[10,1,1024]{2,1,0:T(1,128)S(1)} %get-tuple-element.21), channel_id=1, source_target_pairs={{0,1},{1,2},{2,3},{4,5},{5,6},{6,7},{8,9},{9,10},{10,11},{12,13},{... | collective-permute-start | bytes 122888 | tf_op jit(solution)/shard_map/ppermute | solution.py:21
  406.1 7.7 %collective-permute-start.81 = (f32[1,16,1024]{2,1,0:T(8,128)S(1)}, f32[1,16,1024]{2,1,0:T(8,128)S(1)}, u32[]{:S(2)}, u32[]{:S(2)}) collective-permute-start(f32[1,16,1024]{2,1,0:T(8,128)S(1)} %get-tuple-element.33), channel_id=1, source_target_pairs={{0,4},{4,8},{8,12},{12,16},{16,20},{20,24},{24,28},{28,32},{32,36}... | collective-permute-start | bytes 196616 | tf_op jit(solution)/shard_map/ppermute | solution.py:21
  415.8 5.9 %collective-permute-start.83 = (f32[10,1,1024]{2,1,0:T(1,128)S(1)}, f32[10,1,1024]{2,1,0:T(1,128)S(1)}, u32[]{:S(2)}, u32[]{:S(2)}) collective-permute-start(f32[10,1,1024]{2,1,0:T(1,128)S(1)} %get-tuple-element.19), channel_id=1, source_target_pairs={{0,1},{1,2},{2,3},{4,5},{5,6},{6,7},{8,9},{9,10},{10,11},{12,13},{... | collective-permute-start | bytes 122888 | tf_op jit(solution)/shard_map/ppermute | solution.py:21
  (23 other events, 119.2 us)
where the time goes:
time: 426 us; the launch traced here: 423 us
  starting transfers between devices  199 us (47%)
  waiting for transfers between devices  137 us (32%)
  local copies, waits for them, and re-layouts  48 us (11%)
  other arithmetic  30.4 us (7%)
  blocking collectives  6.72 us (2%)
    ppermute x42, waiting for transfers between devices, extended(): before = lax.ppermute(last, axis, up)  135 us
    ppermute x42, starting transfers between devices, extended(): after = lax.ppermute(first, axis, down)  121 us
    ppermute x42, starting transfers between devices, extended(): before = lax.ppermute(last, axis, up)  77.9 us
    reshape x2, local copies, waits for them, and re-layouts, restrict(): field.reshape(nx // 2, 2, ny // 2, 2, nz // 2, 2).sum(axis=(1, 3, 5))  40.4 us
    reduce_sum x4, other arithmetic, restrict(): field.reshape(nx // 2, 2, ny // 2, 2, nz // 2, 2).sum(axis=(1, 3, 5))  15 us
  transfers between devices with their start and end apart: 84, of which 38 were waited for; matrix products, arithmetic and copies ran while one was open for 2% of the time, Pallas kernels for 0%

commit v1 on v0

v1 whole, which is shorter than its diff:
```python
import functools

import jax
import jax.numpy as jnp
from jax import lax
from jax.experimental import pallas as pl
from jax.experimental.pallas import tpu as pltpu
from jax.sharding import PartitionSpec as P

D = 0.8 / 6.0
C1 = 2.0 * D - 6.0 * D * D
C2 = D * D
C0 = 1.0 - 6.0 * D
NX, NY = 8, 16
LANES = 128
AXES = ("leaf", "sub")
f32 = jnp.float32


def lanes(rows):
    return lax.broadcasted_iota(jnp.int32, (rows, LANES), 1)


def rows_of(rows):
    return lax.broadcasted_iota(jnp.int32, (rows, LANES), 0)


def along_z(cols):
    lane = lanes(cols[0].shape[0])
    first, last = lane == 0, lane == LANES - 1
    right = [pltpu.roll(c, 1, 1) for c in cols]
    left = [pltpu.roll(c, LANES - 1, 1) for c in cols]
    n = len(cols)
    before = [jnp.where(first, right[k - 1] if k else 0.0, right[k]) for k in range(n)]
    after = [jnp.where(last, left[k + 1] if k < n - 1 else 0.0, left[k]) for k in range(n)]
    return before, after


def around(ref, x, whole=False):
    n, rows = ref.shape[1], ref.shape[2]
    cols = [ref[x, k] for k in range(n)]
    before, after = along_z(cols)
    out = []
    for k, c in enumerate(cols):
        up, down = pltpu.roll(c, rows - 1, 0), pltpu.roll(c, 1, 0)
        if whole:
            row = rows_of(rows)
            up, down = jnp.where(row == rows - 1, 0.0, up), jnp.where(row == 0, 0.0, down)
        out.append((ref[x + 1, k] + ref[x - 1, k]) + (up + down) + (before[k] + after[k]))
    return cols, out


def pairs_z(even, odd):
    lane = lanes(even.shape[0])
    take = (lane * 2) % LANES
    got = [
        jnp.take_along_axis(c + pltpu.roll(c, LANES - 1, 1), take, axis=1, mode="promise_in_bounds") for c in (even, odd)
    ]
    return jnp.where(lane < LANES // 2, got[0], got[1])


def twice_z(col):
    lane = lanes(col.shape[0])
    return [jnp.take_along_axis(col, lane // 2 + h * (LANES // 2), axis=1, mode="promise_in_bounds") for h in (0, 1)]


def restricted(tmp, rows):
    sums = [tmp[k, pl.ds(0, rows, 2), :] + tmp[k, pl.ds(1, rows, 2), :] for k in range(tmp.shape[0])]
    return [0.5 * pairs_z(sums[2 * m], sums[2 * m + 1]) for m in range(tmp.shape[0] // 2)]


def prolonged(tmp, cols, rows, at=0):
    for m, c in enumerate(cols):
        for h, e in enumerate(twice_z(c)):
            tmp[2 * m + h, pl.ds(at, rows, 2), :] = e
            tmp[2 * m + h, pl.ds(at + 1, rows, 2), :] = e


def inside(pos, count):
    return jnp.logical_and(pos >= 0, pos < count)


def row_mask(rows, start, count):
    pos = rows_of(rows) + start
    return jnp.where(inside(pos, count), 1.0, 0.0).astype(f32)


def plane_mask(mask, x, count):
    return mask * jnp.where(inside(x, count), 1.0, 0.0).astype(f32)


def each(lo, hi, body):
    def step(x, carry):
        body(x)
        return carry

    lax.fori_loop(lo, hi, step, 0)


def taps(cols):
    lane = lanes(cols[0].shape[0])
    before, after = along_z(cols)
    n = len(cols)
    three = [before[k] + cols[k] + after[k] for k in range(n)]
    right = [pltpu.roll(c, 2, 1) for c in three]
    left = [pltpu.roll(c, LANES - 2, 1) for c in three]
    out = []
    for k in range(n):
        lo = right[k - 1] if k else jnp.where(lane == 1, before[0], 0.0)
        hi = left[k + 1] if k < n - 1 else jnp.where(lane == LANES - 2, after[n - 1], 0.0)
        out.append(cols[k] + jnp.where(lane < 2, lo, right[k]) + jnp.where(lane >= LANES - 2, hi, left[k]))
    return out, before, after


def split(value):
    return [value[:, k * LANES : (k + 1) * LANES] for k in range(value.shape[1] // LANES)]


def place(leaves, subs):
    i, j = lax.axis_index("leaf"), lax.axis_index("sub")
    odd_i, odd_j = i % 2 == 1, j % 2 == 1
    far_i = jnp.where(odd_i, i < leaves - 1, i > 0)
    far_j = jnp.where(odd_j, j < subs - 1, j > 0)
    return i, j, odd_i, odd_j, far_i, far_j


def descent(dims, vf, mask, ra, rb, rs1, rs2, src, big_a, big_b, c1_out, c2_out, m2a, m2b, own2, F1c, H, F0, U0, T0, F1, U1, T1):
    leaves, subs = dims
    i, j, odd_i, odd_j, far_i, far_j = place(leaves, subs)
    nz = vf.shape[2] // LANES
    zero = jnp.zeros((16, LANES), f32)

    def level0(x):
        h, before, after = taps(split(vf[x]))
        m = mask[x].astype(f32)
        for k in range(nz):
            H[x + 1, k] = h[k]
            U0[x, k, 0:16, :] = (after[k] - before[k]) * (0.5 * m[:, k * LANES : (k + 1) * LANES])

    each(0, NX, level0)
    far_x = jnp.where(far_i, 1.0, 0.0).astype(f32)
    far_y = jnp.where(far_j, 1.0, 0.0).astype(f32)
    ha, _, _ = taps(split(ra[0]))
    hb, _, _ = taps(split(rb[0]))
    hs1, _, _ = taps(split(rs1[...]))
    hs2, _, _ = taps(split(rs2[...]))
    for k in range(nz):
        b = hb[k] * far_x
        H[0, k] = jnp.where(odd_i, ha[k], b)
        H[NX + 1, k] = jnp.where(odd_i, b, ha[k])
    row = rows_of(16)
    low = [jnp.where(odd_j, hs1[k], hs2[k] * far_y) for k in range(nz)]
    high = [jnp.where(odd_j, hs2[k] * far_y, hs1[k]) for k in range(nz)]

    zero24 = jnp.zeros((24, LANES), f32)
    for x in (0, 1, 2, 3, 12, 13, 14, 15):
        for k in range(nz):
            F0[x, k] = zero24
    for x in range(NX):
        for k in range(nz):
            h = H[x + 1, k]
            up = jnp.where(row == 15, high[k][x : x + 1, :], pltpu.roll(h, 15, 0))
            down = jnp.where(row == 0, low[k][x : x + 1, :], pltpu.roll(h, 1, 0))
            ahead, behind = H[x + 2, k], H[x, k]
            sx, sy = 0.5 * (ahead - behind), 0.5 * (up - down)
            bend = ahead - 2.0 * h + behind + (up - 2.0 * h + down)
            inv = lax.rsqrt(1.0 + sx * sx + sy * sy)
            f = U0[x, k, 0:16, :] * (bend * (inv * inv * inv))
            src[x, :, k * LANES : (k + 1) * LANES] = f
            F0[x + 4, k, 0:4, :] = zero24[0:4]
            F0[x + 4, k, 4:20, :] = f
            F0[x + 4, k, 20:24, :] = zero24[0:4]

    count_x, count_y = leaves * NX, subs * NY
    my0 = row_mask(24, j * NY - 4, count_y)
    for x in (1, 2, 13, 14):
        for k in range(nz):
            U0[x, k] = zero24

    def smooth0(x):
        m = plane_mask(my0, i * NX + x - 4, count_x)
        f, around_f = around(F0, x)
        for k in range(nz):
            U0[x, k] = (C1 * f[k] + C2 * around_f[k]) * m

    each(3, 13, smooth0)

    for x in range(0, 14):
        if x < 4 or x >= 10:
            for k in range(nz // 2):
                F1[x, k] = zero

    def restrict0(c):
        total = [zero24] * nz
        for p in (0, 1):
            x = 2 * c + p
            m = plane_mask(my0, i * NX + x - 4, count_x)
            u, around_u = around(U0, x)
            total = [total[k] + (F0[x, k] - 6.0 * u[k] + around_u[k]) * m for k in range(nz)]
        for k in range(nz):
            T0[k] = total[k]
        for k, v in enumerate(restricted(T0, 12)):
            F1[c + 3, k, 0:2, :] = zero[0:2]
            F1[c + 3, k, 2:14, :] = v
            F1[c + 3, k, 14:16, :] = zero[0:2]

    each(1, 7, restrict0)

    n1 = nz // 2
    my1 = row_mask(16, j * (NY // 2) - 4, count_y // 2)
    for x in (0, 1, 2, 11, 12, 13):
        for k in range(n1):
            U1[x, k] = zero

    def smooth1(x):
        m = plane_mask(my1, i * (NX // 2) + x - 5, count_x // 2)
        f, around_f = around(F1, x)
        for k in range(n1):
            U1[x, k] = (C1 * f[k] + C2 * around_f[k]) * m

    each(3, 11, smooth1)

    def restrict1(c):
        total = [zero] * n1
        for p in (0, 1):
            x = 2 * c + 1 + p
            m = plane_mask(my1, i * (NX // 2) + x - 5, count_x // 2)
            u, around_u = around(U1, x)
            total = [total[k] + (F1[x, k] - 6.0 * u[k] + around_u[k]) * m for k in range(n1)]
        for k in range(n1):
            T1[k] = total[k]
        for k, v in enumerate(restricted(T1, 8)):
            F1c[c, :, k * LANES : (k + 1) * LANES] = v

    each(0, 6, restrict1)

    at = jnp.where(odd_i, 0, 4)
    m2a[...] = F1c[pl.ds(at, 2)]
    m2b[...] = F1c[pl.ds(4 - at, 2)]
    own2[...] = F1c[2:4]
    for x in range(4):
        big_a[x] = src[at + x]
        big_b[x] = src[4 - at + x]
    for p in range(3):
        for k in range(n1):
            for h in (0, 1):
                v = F1[4 + p + 3 * h, k]
                big_a[4 + p, :, (h * n1 + k) * LANES : (h * n1 + k + 1) * LANES] = v
                big_b[4 + p, :, (h * n1 + k) * LANES : (h * n1 + k + 1) * LANES] = v
    odd_c = (i // 2) % 2 == 1
    first = jnp.where(odd_c, 4, 8)
    for k in range(n1):
        for h in (0, 1):
            s = slice((h * n1 + k) * LANES, (h * n1 + k + 1) * LANES)
            c1_out[0, :, s] = F1[first + h, k]
            c2_out[0, :, s] = F1[12 - first + h, k]


def sum2(dims, own2, ra, rb, out):
    far = place(*dims)[4]
    v = own2[...] + ra[...] + jnp.where(far, rb[...], 0.0)
    for k in range(out.shape[0]):
        out[k] = v


def chip2(dims, got, out):
    odd_i = place(*dims)[2]
    half = got.shape[3] // 2
    row = lax.broadcasted_iota(jnp.int32, (8, half), 0)
    for c in (0, 1):
        for x in (0, 1):
            t = [jnp.where(odd_i, got[4 * c + j, x, :, half:], got[4 * c + j, x, :, :half]) for j in range(4)]
            one, two = pltpu.roll(t[1], 2, 0), pltpu.roll(t[2], 6, 0)
            lo = jnp.where(row < 6, pltpu.roll(t[0], 6, 0), two) + jnp.where(row >= 2, one, 0.0)
            hi = jnp.where(row >= 2, pltpu.roll(t[3], 2, 0), one) + jnp.where(row < 6, two, 0.0)
            for k in range(out.shape[0]):
                out[k, 2 * c + x, 0:8, :] = lo
                out[k, 2 * c + x, 8:16, :] = hi


def rows_out(dims, src, F1own, ra, rb, rc1, rc2, f1x, s1, s2):
    leaves, subs = dims
    i, j, odd_i, odd_j, far_i, far_j = place(leaves, subs)
    odd_c = (i // 2) % 2 == 1
    chips = leaves // 2
    c = i // 2
    far_c = jnp.where(odd_c, c < chips - 1, c > 0)
    n = src.shape[2] // 2

    def halves(ref, at, p):
        return ref[at + p % 3, :, (p // 3) * n : (p // 3 + 1) * n]

    a = [halves(ra, 4, p) for p in range(6)]
    b = [jnp.where(far_i, halves(rb, 4, p), 0.0) for p in range(6)]
    before = [jnp.where(odd_i, a[p], b[p]) for p in range(6)]
    after = [jnp.where(odd_i, b[p], a[p]) for p in range(6)]
    d1 = [rc1[0, :, h * n : (h + 1) * n] for h in (0, 1)]
    d2 = [jnp.where(far_c, rc2[0, :, h * n : (h + 1) * n], 0.0) for h in (0, 1)]
    before2 = [jnp.where(odd_c, d1[h], d2[h]) for h in (0, 1)]
    after2 = [jnp.where(odd_c, d2[h], d1[h]) for h in (0, 1)]
    own = [halves(F1own, 4, p) for p in range(6)]
    planes = {}

    def add(x, v):
        planes[x] = planes[x] + v if x in planes else v

    for p in range(6):
        add(p - 1, own[p])
        add(p - 5, before[p])
        add(p + 3, after[p])
    for h in (0, 1):
        add(-5 + h, before2[h])
        add(7 + h, after2[h])
    for x in range(14):
        f1x[x] = planes[x - 5]

    def fine(x):
        if 4 <= x < 12:
            return src[x - 4]
        if x < 4:
            return jnp.where(odd_i, ra[x], jnp.where(far_i, rb[x], 0.0))
        return jnp.where(odd_i, jnp.where(far_i, rb[x - 12], 0.0), ra[x - 12])

    for x in range(8):
        u, v = fine(x), fine(x + 8)
        for out, up in ((s1, odd_j == False), (s2, odd_j)):
            out[x, 0:4, :] = jnp.where(up, u[12:16], u[0:4])
            out[x, 4:8, :] = jnp.where(up, v[12:16], v[0:4])
    for x in range(14):
        v = planes[x - 5]
        s = slice((x // 7) * n, (x // 7 + 1) * n)
        last, first = v[5:13], v[3:11]
        s1[8 + x % 7, :, s] = jnp.where(odd_j, first, last)
        s2[8 + x % 7, :, s] = jnp.where(odd_j, last, first)


def ascent(dims, mine, other, src, ra, rb, f1x, rs1, rs2, press, resid, F2, U2, T2, G3, U3, V3, W2, X2, T1, F1, V1, X1, T0, F0, V0, X0):
    leaves, subs = dims
    i, j, odd_i, odd_j, far_i, far_j = place(leaves, subs)
    count_x, count_y = leaves * NX, subs * NY
    nz = src.shape[2] // LANES
    n1, n2 = nz // 2, nz // 4
    x2 = count_x // 4
    zero = jnp.zeros((24, LANES), f32)

    for x in list(range(5)) + list(range(x2 + 5, x2 + 10)):
        for k in range(n2):
            F2[x, k] = zero[0:16]
            U2[x, k] = zero[0:16]
    h2 = n2 // 2

    def fill2(x):
        a, b = mine[x], other[x]
        for k in range(h2):
            s = slice(k * LANES, (k + 1) * LANES)
            F2[x + 5, k] = jnp.where(odd_i, b[:, s], a[:, s])
            F2[x + 5, h2 + k] = jnp.where(odd_i, a[:, s], b[:, s])

    each(0, x2, fill2)

    def smooth2(x):
        f, around_f = around(F2, x, True)
        for k in range(n2):
            U2[x, k] = C1 * f[k] + C2 * around_f[k]

    each(5, x2 + 5, smooth2)

    x3 = x2 // 2

    def restrict2(c):
        total = [zero[0:16]] * n2
        for p in (0, 1):
            x = 5 + 2 * c + p
            u, around_u = around(U2, x, True)
            total = [total[k] + (F2[x, k] - 6.0 * u[k] + around_u[k]) for k in range(n2)]
        for k in range(n2):
            T2[k] = total[k]
        for k, v in enumerate(restricted(T2, 8)):
            G3[c + 2, k] = v
            U3[c + 2, k] = D * v

    each(0, x3, restrict2)
    n3 = n2 // 2
    for x in (0, 1, x3 + 2, x3 + 3):
        for k in range(n3):
            G3[x, k] = zero[0:8]
            U3[x, k] = zero[0:8]
            V3[x, k] = zero[0:8]

    def sweep3(old, new):
        def body(x):
            u, around_u = around(old, x, True)
            for k in range(n3):
                new[x, k] = C0 * u[k] + D * (G3[x, k] + around_u[k])

        each(2, x3 + 2, body)

    for _ in range(3):
        sweep3(U3, V3)
        sweep3(V3, U3)
    sweep3(U3, V3)

    def window2(c):
        x = c // 2
        prolonged(T2, [V3[i + x, k] for k in range(n3)], 8)
        for p in (0, 1):
            w = c + p
            for k in range(n2):
                W2[w, k] = U2[2 * i + 1 + w, k] + T2[k]

    for c in range(0, 10, 2):
        window2(c)
    m2 = jnp.ones((16, LANES), f32)

    def sweep2(old, new, lo, hi):
        for w in range(lo, hi):
            m = plane_mask(m2, 2 * i + w - 4, x2)
            u, around_u = around(old, w, True)
            for k in range(n2):
                new[w, k] = (C0 * u[k] + D * (F2[2 * i + 1 + w, k] + around_u[k])) * m

    for w in range(10):
        m = plane_mask(m2, 2 * i + w - 4, x2)
        for k in range(n2):
            W2[w, k] = W2[w, k] * m
    sweep2(W2, X2, 1, 9)
    sweep2(X2, W2, 2, 8)

    for k in range(n1):
        T1[k] = zero
    low_j = jnp.where(j > 0, 1.0, 0.0).astype(f32)
    high_j = jnp.where(j < subs - 1, 1.0, 0.0).astype(f32)

    def fill1(x):
        part, at = x // 7, 8 + x % 7
        for k in range(n1):
            s = slice(k * LANES, (k + 1) * LANES)
            F1[x, k] = zero
            F1[x, k, 4:20, :] = f1x[x, :, s]
            s = slice((part * n1 + k) * LANES, (part * n1 + k + 1) * LANES)
            lo = jnp.where(odd_j, rs1[at, :, s], rs2[at, :, s]) * low_j
            hi = jnp.where(odd_j, rs2[at, :, s], rs1[at, :, s]) * high_j
            F1[x, k, 1:9, :] = F1[x, k, 1:9, :] + lo
            F1[x, k, 15:23, :] = F1[x, k, 15:23, :] + hi

    for x in range(14):
        fill1(x)
    my1 = row_mask(24, j * (NY // 2) - 8, count_y // 2)

    for c in range(6):
        cols = [pltpu.roll(W2[c + 2, k], (18 - 4 * j) % 16, 0)[0:8] for k in range(n2)]
        prolonged(T1, cols, 8, 4)
        for p in (0, 1):
            x = 2 * c + p + 1
            m = plane_mask(my1, i * (NX // 2) + x - 5, count_x // 2)
            f, around_f = around(F1, x)
            for k in range(n1):
                V1[x, k] = (C1 * f[k] + C2 * around_f[k] + T1[k]) * m

    def sweep1(old, new, lo, hi):
        def body(x):
            m = plane_mask(my1, i * (NX // 2) + x - 5, count_x // 2)
            u, around_u = around(old, x)
            for k in range(n1):
                new[x, k] = (C0 * u[k] + D * (F1[x, k] + around_u[k])) * m

        each(lo, hi, body)

    sweep1(V1, X1, 2, 12)
    sweep1(X1, V1, 3, 11)

    far_x = jnp.where(far_i, 1.0, 0.0).astype(f32)

    def fill0(x):
        if 4 <= x < 12:
            v = src[x - 4]
        elif x < 4:
            v = jnp.where(odd_i, ra[x], rb[x] * far_x)
        else:
            v = jnp.where(odd_i, rb[x - 12] * far_x, ra[x - 12])
        a, b = rs1[x % 8], rs2[x % 8]
        h = 4 * (x // 8)
        lo = jnp.where(odd_j, a[h : h + 4], b[h : h + 4]) * low_j
        hi = jnp.where(odd_j, b[h : h + 4], a[h : h + 4]) * high_j
        for k in range(nz):
            s = slice(k * LANES, (k + 1) * LANES)
            F0[x, k, 0:4, :] = lo[:, s]
            F0[x, k, 4:20, :] = v[:, s]
            F0[x, k, 20:24, :] = hi[:, s]

    for x in range(16):
        fill0(x)
    my0 = row_mask(24, j * NY - 4, count_y)

    def start0(c):
        prolonged(T0, [V1[c + 3, k, 6:18, :] for k in range(n1)], 12)
        for p in (0, 1):
            x = 2 * c + p

            @pl.when(jnp.logical_and(x > 0, x < 15))
            def _():
                m = plane_mask(my0, i * NX + x - 4, count_x)
                f, around_f = around(F0, x)
                for k in range(nz):
                    V0[x, k] = (C1 * f[k] + C2 * around_f[k] + T0[k]) * m

    each(0, 8, start0)

    def sweep0(old, new, lo, hi):
        def body(x):
            m = plane_mask(my0, i * NX + x - 4, count_x)
            u, around_u = around(old, x)
            for k in range(nz):
                new[x, k] = (C0 * u[k] + D * (F0[x, k] + around_u[k])) * m

        each(lo, hi, body)

    sweep0(V0, X0, 2, 14)
    sweep0(X0, V0, 3, 13)

    def finish(x):
        u, around_u = around(V0, x + 4)
        for k in range(nz):
            s = slice(k * LANES, (k + 1) * LANES)
            press[x, :, s] = u[k][4:20]
            resid[x, :, s] = (F0[x + 4, k] - 6.0 * u[k] + around_u[k])[4:20]

    each(0, NX, finish)


def call(kernel, outs, scratch, *args):
    return pl.pallas_call(
        kernel,
        out_shape=[jax.ShapeDtypeStruct(s, f32) for s in outs],
        scratch_shapes=[pltpu.VMEM(s, f32) for s in scratch],
        compiler_params=pltpu.CompilerParams(vmem_limit_bytes=48 * 1024 * 1024),
    )(*args)


def swaps(leaves, subs):
    def table(partner):
        return [(i * subs + j, (lambda t: t[0] * subs + t[1])(partner(i, j))) for i in range(leaves) for j in range(subs)]

    def odd(n):
        return ((n + 1) ^ 1) - 1

    def inner(n, count):
        return 0 <= n < count

    a = table(lambda i, j: (i ^ 1, j))
    b = table(lambda i, j: (odd(i), j) if inner(odd(i), leaves) else (i, j ^ 1))
    s1 = table(lambda i, j: (i, j ^ 1))
    s2 = table(lambda i, j: (i, odd(j)) if inner(odd(j), subs) else (i ^ 1, j))
    c1 = table(lambda i, j: (i ^ 2, j))
    c2 = table(lambda i, j: (2 * odd(i // 2) + i % 2, j) if inner(odd(i // 2), leaves // 2) else (i, j ^ 1))
    return a, b, s1, s2, c1, c2


def shards(dims, volume_fraction, interface_mask):
    leaves, subs = dims
    depth = volume_fraction.shape[2]
    nz = depth // LANES
    pa, pb, ps1, ps2, pc1, pc2 = swaps(leaves, subs)
    move = lambda v, table: lax.ppermute(v, AXES, table)
    i, j = lax.axis_index("leaf"), lax.axis_index("sub")
    odd_i, odd_j = i % 2, j % 2

    vf = volume_fraction
    at_x, at_y = (1 - odd_i) * (NX - 1), (1 - odd_j) * (NY - 1)
    plane = lambda x: lax.dynamic_slice_in_dim(vf, x, 1, 0)
    rows = lambda y: lax.dynamic_slice_in_dim(vf, y, 1, 1).reshape(NX, depth)
    ha, hb = move(plane(at_x), pa), move(plane(NX - 1 - at_x), pb)
    hs1, hs2 = move(rows(at_y), ps1), move(rows(NY - 1 - at_y), ps2)

    n1 = nz // 2
    src, big_a, big_b, m1, m2, m2a, m2b, own2 = call(
        functools.partial(descent, dims),
        [
            (NX, NY, depth),
            (7, 16, depth),
            (7, 16, depth),
            (1, 16, depth),
            (1, 16, depth),
            (2, 8, depth // 4),
            (2, 8, depth // 4),
            (2, 8, depth // 4),
        ],
        [
            (6, 8, depth // 4),
            (NX + 2, nz, 16, LANES),
            (16, nz, 24, LANES),
            (16, nz, 24, LANES),
            (nz, 24, LANES),
            (14, n1, 16, LANES),
            (14, n1, 16, LANES),
            (n1, 16, LANES),
        ],
        vf,
        interface_mask,
        ha,
        hb,
        hs1,
        hs2,
    )
    r2a, r2b = move(m2a, pa), move(m2b, pb)
    ra, rb = move(big_a, pa), move(big_b, pb)
    rc1, rc2 = move(m1, pc1), move(m2, pc2)

    (out,) = call(functools.partial(sum2, dims), [(2 * subs, 2, 8, depth // 4)], [], own2, r2a, r2b)
    group = [list(range(k, k + 2 * subs)) for k in range(0, leaves * subs, 2 * subs)]
    got = lax.all_to_all(out, AXES, 0, 0, axis_index_groups=group)
    chips = leaves // 2
    (out,) = call(functools.partial(chip2, dims), [(chips, 4, 16, depth // 8)], [], got)
    f1x, s1, s2 = call(
        functools.partial(rows_out, dims),
        [(14, 16, depth // 2), (15, 8, depth), (15, 8, depth)],
        [],
        src,
        big_a,
        ra,
        rb,
        rc1,
        rc2,
    )
    rs1, rs2 = move(s1, ps1), move(s2, ps2)
    group = [[(2 * c + k) * subs + s for c in range(chips)] for k in (0, 1) for s in range(subs)]
    mine = lax.all_to_all(out, AXES, 0, 0, axis_index_groups=group).reshape(4 * chips, 16, depth // 8)
    other = move(mine, pa)
    x2 = 2 * leaves
    press, resid = call(
        functools.partial(ascent, dims),
        [(NX, NY, depth), (NX, NY, depth)],
        [
            (x2 + 10, nz // 4, 16, LANES),
            (x2 + 10, nz // 4, 16, LANES),
            (nz // 4, 16, LANES),
            (x2 // 2 + 4, nz // 8, 8, LANES),
            (x2 // 2 + 4, nz // 8, 8, LANES),
            (x2 // 2 + 4, nz // 8, 8, LANES),
            (10, nz // 4, 16, LANES),
            (10, nz // 4, 16, LANES),
            (n1, 24, LANES),
            (14, n1, 24, LANES),
            (14, n1, 24, LANES),
            (14, n1, 24, LANES),
            (nz, 24, LANES),
            (16, nz, 24, LANES),
            (16, nz, 24, LANES),
            (16, nz, 24, LANES),
        ],
        mine,
        other,
        src,
        ra,
        rb,
        f1x,
        rs1,
        rs2,
    )
    return press, resid


def solution(mesh):
    spec = P("leaf", "sub", None)
    dims = (mesh.shape["leaf"], mesh.shape["sub"])
    body = functools.partial(shards, dims)
    return jax.shard_map(body, mesh=mesh, in_specs=(spec, spec), out_specs=(spec, spec), check_vma=False)
```

time: 426 us -> 112 us (0.26)
  the two profiles are of different devices: /device:TPU:102 before, /device:TPU:2 now
where the time goes in v1:
time: 112 us; the launch traced here: 110 us
  Pallas kernels  49.6 us (44%)
  waiting for transfers between devices  26.9 us (24%)
  starting transfers between devices  20.1 us (18%)
  blocking collectives  9.66 us (9%)
  local copies, waits for them, and re-layouts  3.07 us (3%)
    pallas_call x5, Pallas kernels, call(): pl.pallas_call(kernel, out_shape=[jax.ShapeDtypeStruct(s, f32) for s in o...  49.6 us
    ppermute x13, waiting for transfers between devices, shards(): move = lambda v, table: lax.ppermute(v, AXES, table)  18.5 us
    ppermute x13, starting transfers between devices, shards(): move = lambda v, table: lax.ppermute(v, AXES, table)  11.2 us
    all_to_all x1, blocking collectives, shards(): got = lax.all_to_all(out, AXES, 0, 0, axis_index_groups=group)  9.66 us
    all_to_all x1, starting transfers between devices, shards(): lax.all_to_all(out, AXES, 0, 0, axis_index_groups=group)  8.97 us
    all_to_all x1, waiting for transfers between devices, shards(): lax.all_to_all(out, AXES, 0, 0, axis_index_groups=group)  8.35 us
  transfers between devices with their start and end apart: 14, of which 8 were waited for; matrix products, arithmetic and copies ran while one was open for 1% of the time, Pallas kernels for 0%

profile of v1, /device:TPU:2, one launch (start us, length us, event | category | flops | bytes accessed | tf_op | source)
XLA Modules:
  0.0 110.1 jit_solution(1951648497713474934)
XLA Ops:
  0.6 0.0 copy-start
  0.7 0.9 constant_dynamic-slice_fusion.2
  1.6 0.5 collective-permute-start.1
  2.1 1.2 %collective-permute-start = (f32[1,16,1024]{2,1,0:T(8,128)S(1)}, f32[1,16,1024]{2,1,0:T(8,128)S(1)}, u32[]{:S(2)}, u32[]{:S(2)}) collective-permute-start(f32[1,16,1024]{2,1,0:T(8,128)S(1)} %get-tuple-element.27), channel_id=1, source_target_pairs={{0,4},{1,5},{2,6},{3,7},{4,0},{5,1},{6,2},{7,3},{8,12},{9,13},{10,... | collective-permute-start | bytes 196616 | tf_op jit(solution)/shard_map/ppermute | solution.py:564
  3.4 1.1 constant_dynamic-slice_fusion
  4.5 0.6 collective-permute-start.2
  5.1 2.2 %collective-permute-start.3 = (f32[8,1024]{1,0:T(8,128)S(1)}, f32[8,1024]{1,0:T(8,128)S(1)}, u32[]{:S(2)}, u32[]{:S(2)}) collective-permute-start(f32[8,1024]{1,0:T(8,128)S(1)} %bitcast.10), channel_id=1, source_target_pairs={{0,4},{1,2},{2,1},{3,7},{4,0},{5,6},{6,5},{7,3},{8,12},{9,10},{10,... | collective-permute-start | bytes 98312 | tf_op jit(solution)/shard_map/ppermute | solution.py:564
  7.3 1.1 %collective-permute-done.2.rs1 = f32[8,1024]{1,0:T(8,128)S(1)} collective-permute-done((f32[8,1024]{1,0:T(8,128)S(1)}, f32[8,1024]{1,0:T(8,128)S(1)}, u32[]{:S(2)}, u32[]{:S(2)}) %collective-permute-start.2) | collective-permute-done | bytes 32800 | tf_op jit(solution)/shard_map/ppermute | solution.py:564
  8.5 0.8 collective-permute-done.3.rs2
  9.2 0.0 collective-permute-done.1.rb
  9.2 0.0 collective-permute-done.ra
  9.2 0.0 copy-done
  9.2 0.0 copy-start.1
  9.2 1.0 copy-done.1
  10.3 8.0 %shard_map.41 = (f32[8,16,1024]{2,1,0:T(8,128)S(1)}, f32[7,16,1024]{2,1,0:T(8,128)S(1)}, f32[7,16,1024]{2,1,0:T(8,128)S(1)}, f32[1,16,1024]{2,1,0:T(8,128)S(1)},...) custom-call(f32[8,16,1024]{2,1,0:T(8,128)S(1)} %copy-done, ...), custom_call_target="tpu_custom_call" | custom-call | tf_op jit(solution)/shard_map/pallas_call | solution.py:532
  18.3 0.1 collective-permute-start.4
  18.4 0.1 collective-permute-start.5
  18.5 1.1 collective-permute-done.4.ra
  19.5 2.6 %collective-permute-done.5.rb = f32[2,8,256]{2,1,0:T(8,128)S(1)} collective-permute-done((f32[2,8,256]{2,1,0:T(8,128)S(1)}, f32[2,8,256]{2,1,0:T(8,128)S(1)}, u32[]{:S(2)}, u32[]{:S(2)}) %collective-permute-start.5) | collective-permute-done | bytes 16416 | tf_op jit(solution)/shard_map/ppermute | solution.py:564
  22.2 9.7 %all_to_all.10.got = f32[8,2,8,256]{3,2,1,0:T(8,128)S(1)} all-to-all(f32[8,2,8,256]{3,2,1,0:T(8,128)S(1)} %shard_map.42), channel_id=1, replica_groups={{0,1,2,3,4,5,6,7},{8,9,10,11,12,13,14,15},{16,17,18,19,20,21,22,23},{24..., dimensions={0} | all-to-all | bytes 262144 | tf_op jit(solution)/shard_map/all_to_all | solution.py:611
  31.9 0.9 shard_map.43
  32.7 9.0 %all-to-all-start.1 = ((f32[16,4,16,128]{3,2,1,0:T(8,128)}), f32[16,4,16,128]{3,2,1,0:T(8,128)S(1)}, u32[]{:S(2)}, u32[]{:S(2)}) async-start(f32[16,4,16,128]{3,2,1,0:T(8,128)} %shard_map.43), calls=%async_computation.1 | async-start | bytes 1048576 | tf_op jit(solution)/shard_map/all_to_all | solution.py:627
  41.7 1.1 %collective-permute-start.8 = (f32[7,16,1024]{2,1,0:T(8,128)S(1)}, f32[7,16,1024]{2,1,0:T(8,128)S(1)}, u32[]{:S(2)}, u32[]{:S(2)}) collective-permute-start(f32[7,16,1024]{2,1,0:T(8,128)S(1)} %get-tuple-element.18), channel_id=1, source_target_pairs={{0,1},{1,0},{2,3},{3,2},{4,8},{5,9},{6,10},{7,11},{8,4},{9,5},{10,... | collective-permute-start | bytes 1376264 | tf_op jit(solution)/shard_map/ppermute | solution.py:564
  42.8 0.9 collective-permute-start.7
  43.7 1.5 %collective-permute-start.9 = (f32[1,16,1024]{2,1,0:T(8,128)S(1)}, f32[1,16,1024]{2,1,0:T(8,128)S(1)}, u32[]{:S(2)}, u32[]{:S(2)}) collective-permute-start(f32[1,16,1024]{2,1,0:T(8,128)S(1)} %get-tuple-element.19), channel_id=1, source_target_pairs={{0,8},{1,9},{2,10},{3,11},{4,12},{5,13},{6,14},{7,15},{8,0},{9,1},... | collective-permute-start | bytes 196616 | tf_op jit(solution)/shard_map/ppermute | solution.py:564
  45.2 1.1 collective-permute-start.10
  46.3 8.3 %all-to-all-done.1 = f32[16,4,16,128]{3,2,1,0:T(8,128)S(1)} async-done(((f32[16,4,16,128]{3,2,1,0:T(8,128)}), f32[16,4,16,128]{3,2,1,0:T(8,128)S(1)}, u32[]{:S(2)}, u32[]{:S(2)}) %all-to-all-start.1) | async-done | bytes 524320 | tf_op jit(solution)/shard_map/all_to_all | solution.py:627
  54.6 0.0 collective-permute-start.6
  54.6 1.6 %collective-permute-done.9.rc1 = f32[1,16,1024]{2,1,0:T(8,128)S(1)} collective-permute-done((f32[1,16,1024]{2,1,0:T(8,128)S(1)}, f32[1,16,1024]{2,1,0:T(8,128)S(1)}, u32[]{:S(2)}, u32[]{:S(2)}) %collective-permute-start.9) | collective-permute-done | bytes 65568 | tf_op jit(solution)/shard_map/ppermute | solution.py:564
  56.2 0.0 collective-permute-done.10.rc2
  56.2 0.0 collective-permute-done.8.rb
  56.2 0.0 collective-permute-done.7.ra
  56.2 0.3 shard_map.44
  56.5 1.1 %collective-permute-start.11 = (f32[15,8,1024]{2,1,0:T(8,128)S(1)}, f32[15,8,1024]{2,1,0:T(8,128)S(1)}, u32[]{:S(2)}, u32[]{:S(2)}) collective-permute-start(f32[15,8,1024]{2,1,0:T(8,128)S(1)} %get-tuple-element.22), channel_id=1, source_target_pairs={{0,1},{1,0},{2,3},{3,2},{4,5},{5,4},{6,7},{7,6},{8,9},{9,8},{10,11... | collective-permute-start | bytes 1474568 | tf_op jit(solution)/shard_map/ppermute | solution.py:564
  57.7 0.7 collective-permute-start.12
  58.3 10.5 %collective-permute-done.11.rs1 = f32[15,8,1024]{2,1,0:T(8,128)S(1)} collective-permute-done((f32[15,8,1024]{2,1,0:T(8,128)S(1)}, f32[15,8,1024]{2,1,0:T(8,128)S(1)}, u32[]{:S(2)}, u32[]{:S(2)}) %collective-permute-start.11) | collective-permute-done | bytes 491552 | tf_op jit(solution)/shard_map/ppermute | solution.py:564
  68.8 0.8 collective-permute-done.12.rs2
  69.6 0.0 collective-permute-done.6.other
  69.6 40.4 %shard_map.45 = (f32[8,16,1024]{2,1,0:T(8,128)}, f32[8,16,1024]{2,1,0:T(8,128)}) custom-call(f32[64,16,128]{2,1,0:T(8,128)S(1)} %bitcast.8, f32[64,16,128]{2,1,0:T(8,128)S(1)} %collective-permute-done.6.other, f32[8,16,1024]{2,1,0:T(8,128)S(1)} %get-tuple-element.16.src, f32[7,16,1024]{2,1,0:T(8,128)S(1)} %collective-permute-done.7.ra, ...), custom_call_target="tpu_custom_call" | custom-call | tf_op jit(solution)/shard_map/pallas_call | solution.py:532
  (3 shorter events, 0.0 us)
Async XLA Ops:
  0.6 8.6 %copy-start = (f32[8,16,1024]{2,1,0:T(8,128)S(1)}, f32[8,16,1024]{2,1,0:T(8,128)}, u32[]{:S(2)}) copy-start(f32[8,16,1024]{2,1,0:T(8,128)} %vf.1) | copy-start | bytes 1572868
  1.6 7.6 %collective-permute-start.1 = (f32[1,16,1024]{2,1,0:T(8,128)S(1)}, f32[1,16,1024]{2,1,0:T(8,128)S(1)}, u32[]{:S(2)}, u32[]{:S(2)}) collective-permute-start(f32[1,16,1024]{2,1,0:T(8,128)S(1)} %get-tuple-element.26), channel_id=1, source_target_pairs={{0,1},{1,0},{2,3},{3,2},{4,8},{5,9},{6,10},{7,11},{8,4},{9,5},{10,... | collective-permute-start | bytes 196616 | tf_op jit(solution)/shard_map/ppermute | solution.py:564
  2.1 7.1 %collective-permute-start = (f32[1,16,1024]{2,1,0:T(8,128)S(1)}, f32[1,16,1024]{2,1,0:T(8,128)S(1)}, u32[]{:S(2)}, u32[]{:S(2)}) collective-permute-start(f32[1,16,1024]{2,1,0:T(8,128)S(1)} %get-tuple-element.27), channel_id=1, source_target_pairs={{0,4},{1,5},{2,6},{3,7},{4,0},{5,1},{6,2},{7,3},{8,12},{9,13},{10,... | collective-permute-start | bytes 196616 | tf_op jit(solution)/shard_map/ppermute | solution.py:564
  4.5 4.0 %collective-permute-start.2 = (f32[8,1024]{1,0:T(8,128)S(1)}, f32[8,1024]{1,0:T(8,128)S(1)}, u32[]{:S(2)}, u32[]{:S(2)}) collective-permute-start(f32[8,1024]{1,0:T(8,128)S(1)} %bitcast.9), channel_id=1, source_target_pairs={{0,1},{1,0},{2,3},{3,2},{4,5},{5,4},{6,7},{7,6},{8,9},{9,8},{10,11... | collective-permute-start | bytes 98312 | tf_op jit(solution)/shard_map/ppermute | solution.py:564
  5.1 4.1 %collective-permute-start.3 = (f32[8,1024]{1,0:T(8,128)S(1)}, f32[8,1024]{1,0:T(8,128)S(1)}, u32[]{:S(2)}, u32[]{:S(2)}) collective-permute-start(f32[8,1024]{1,0:T(8,128)S(1)} %bitcast.10), channel_id=1, source_target_pairs={{0,4},{1,2},{2,1},{3,7},{4,0},{5,6},{6,5},{7,3},{8,12},{9,10},{10,... | collective-permute-start | bytes 98312 | tf_op jit(solution)/shard_map/ppermute | solution.py:564
  9.2 1.0 copy-start.1
  18.3 1.3 %collective-permute-start.4 = (f32[2,8,256]{2,1,0:T(8,128)S(1)}, f32[2,8,256]{2,1,0:T(8,128)S(1)}, u32[]{:S(2)}, u32[]{:S(2)}) collective-permute-start(f32[2,8,256]{2,1,0:T(8,128)S(1)} %get-tuple-element.14), channel_id=1, source_target_pairs={{0,4},{1,5},{2,6},{3,7},{4,0},{5,1},{6,2},{7,3},{8,12},{9,13},{10,... | collective-permute-start | bytes 49160 | tf_op jit(solution)/shard_map/ppermute | solution.py:564
  18.4 3.8 %collective-permute-start.5 = (f32[2,8,256]{2,1,0:T(8,128)S(1)}, f32[2,8,256]{2,1,0:T(8,128)S(1)}, u32[]{:S(2)}, u32[]{:S(2)}) collective-permute-start(f32[2,8,256]{2,1,0:T(8,128)S(1)} %get-tuple-element.15), channel_id=1, source_target_pairs={{0,1},{1,0},{2,3},{3,2},{4,8},{5,9},{6,10},{7,11},{8,4},{9,5},{10,... | collective-permute-start | bytes 49160 | tf_op jit(solution)/shard_map/ppermute | solution.py:564
  32.7 21.9 %all-to-all-start.1 = ((f32[16,4,16,128]{3,2,1,0:T(8,128)}), f32[16,4,16,128]{3,2,1,0:T(8,128)S(1)}, u32[]{:S(2)}, u32[]{:S(2)}) async-start(f32[16,4,16,128]{3,2,1,0:T(8,128)} %shard_map.43), calls=%async_computation.1 | async-start | bytes 1048576 | tf_op jit(solution)/shard_map/all_to_all | solution.py:627
  41.7 14.5 %collective-permute-start.8 = (f32[7,16,1024]{2,1,0:T(8,128)S(1)}, f32[7,16,1024]{2,1,0:T(8,128)S(1)}, u32[]{:S(2)}, u32[]{:S(2)}) collective-permute-start(f32[7,16,1024]{2,1,0:T(8,128)S(1)} %get-tuple-element.18), channel_id=1, source_target_pairs={{0,1},{1,0},{2,3},{3,2},{4,8},{5,9},{6,10},{7,11},{8,4},{9,5},{10,... | collective-permute-start | bytes 1376264 | tf_op jit(solution)/shard_map/ppermute | solution.py:564
  42.8 13.4 %collective-permute-start.7 = (f32[7,16,1024]{2,1,0:T(8,128)S(1)}, f32[7,16,1024]{2,1,0:T(8,128)S(1)}, u32[]{:S(2)}, u32[]{:S(2)}) collective-permute-start(f32[7,16,1024]{2,1,0:T(8,128)S(1)} %get-tuple-element.17.F1own), channel_id=1, source_target_pairs={{0,4},{1,5},{2,6},{3,7},{4,0},{5,1},{6,2},{7,3},{8,12},{9,13},{10,... | collective-permute-start | bytes 1376264 | tf_op jit(solution)/shard_map/ppermute | solution.py:564
  43.7 12.5 %collective-permute-start.9 = (f32[1,16,1024]{2,1,0:T(8,128)S(1)}, f32[1,16,1024]{2,1,0:T(8,128)S(1)}, u32[]{:S(2)}, u32[]{:S(2)}) collective-permute-start(f32[1,16,1024]{2,1,0:T(8,128)S(1)} %get-tuple-element.19), channel_id=1, source_target_pairs={{0,8},{1,9},{2,10},{3,11},{4,12},{5,13},{6,14},{7,15},{8,0},{9,1},... | collective-permute-start | bytes 196616 | tf_op jit(solution)/shard_map/ppermute | solution.py:564
  45.2 11.0 %collective-permute-start.10 = (f32[1,16,1024]{2,1,0:T(8,128)S(1)}, f32[1,16,1024]{2,1,0:T(8,128)S(1)}, u32[]{:S(2)}, u32[]{:S(2)}) collective-permute-start(f32[1,16,1024]{2,1,0:T(8,128)S(1)} %get-tuple-element.20), channel_id=1, source_target_pairs={{0,1},{1,0},{2,3},{3,2},{4,5},{5,4},{6,7},{7,6},{8,16},{9,17},{10,... | collective-permute-start | bytes 196616 | tf_op jit(solution)/shard_map/ppermute | solution.py:564
  54.6 15.0 %collective-permute-start.6 = (f32[64,16,128]{2,1,0:T(8,128)S(1)}, f32[64,16,128]{2,1,0:T(8,128)S(1)}, u32[]{:S(2)}, u32[]{:S(2)}) collective-permute-start(f32[64,16,128]{2,1,0:T(8,128)S(1)} %bitcast.7), channel_id=1, source_target_pairs={{0,4},{1,5},{2,6},{3,7},{4,0},{5,1},{6,2},{7,3},{8,12},{9,13},{10,... | collective-permute-start | bytes 1572872 | tf_op jit(solution)/shard_map/ppermute | solution.py:564
  56.5 12.3 %collective-permute-start.11 = (f32[15,8,1024]{2,1,0:T(8,128)S(1)}, f32[15,8,1024]{2,1,0:T(8,128)S(1)}, u32[]{:S(2)}, u32[]{:S(2)}) collective-permute-start(f32[15,8,1024]{2,1,0:T(8,128)S(1)} %get-tuple-element.22), channel_id=1, source_target_pairs={{0,1},{1,0},{2,3},{3,2},{4,5},{5,4},{6,7},{7,6},{8,9},{9,8},{10,11... | collective-permute-start | bytes 1474568 | tf_op jit(solution)/shard_map/ppermute | solution.py:564
  57.7 11.9 %collective-permute-start.12 = (f32[15,8,1024]{2,1,0:T(8,128)S(1)}, f32[15,8,1024]{2,1,0:T(8,128)S(1)}, u32[]{:S(2)}, u32[]{:S(2)}) collective-permute-start(f32[15,8,1024]{2,1,0:T(8,128)S(1)} %get-tuple-element.23), channel_id=1, source_target_pairs={{0,4},{1,2},{2,1},{3,7},{4,0},{5,6},{6,5},{7,3},{8,12},{9,10},{10,... | collective-permute-start | bytes 1474568 | tf_op jit(solution)/shard_map/ppermute | solution.py:564

commit v2 on v1

--- a/solution.py
+++ b/solution.py
@@ -89,12 +89,17 @@
     return mask * jnp.where(inside(x, count), 1.0, 0.0).astype(f32)
 
 
-def each(lo, hi, body):
-    def step(x, carry):
+def each(lo, hi, body, together=1):
+    steps = (hi - lo) // together
+
+    def step(s, carry):
+        for t in range(together):
+            body(lo + s * together + t)
+        return carry
+
+    lax.fori_loop(0, steps, step, 0)
+    for x in range(lo + steps * together, hi):
         body(x)
-        return carry
-
-    lax.fori_loop(lo, hi, step, 0)
 
 
 def taps(cols):
@@ -124,20 +129,19 @@
     return i, j, odd_i, odd_j, far_i, far_j
 
 
-def descent(dims, vf, mask, ra, rb, rs1, rs2, src, big_a, big_b, c1_out, c2_out, m2a, m2b, own2, F1c, H, F0, U0, T0, F1, U1, T1):
+def source(dims, vf, mask, ra, rb, rs1, rs2, src, out_a, out_b, H, G):
     leaves, subs = dims
     i, j, odd_i, odd_j, far_i, far_j = place(leaves, subs)
     nz = vf.shape[2] // LANES
-    zero = jnp.zeros((16, LANES), f32)
 
     def level0(x):
         h, before, after = taps(split(vf[x]))
         m = mask[x].astype(f32)
         for k in range(nz):
             H[x + 1, k] = h[k]
-            U0[x, k, 0:16, :] = (after[k] - before[k]) * (0.5 * m[:, k * LANES : (k + 1) * LANES])
-
-    each(0, NX, level0)
+            G[x, k] = (after[k] - before[k]) * (0.5 * m[:, k * LANES : (k + 1) * LANES])
+
+    each(0, NX, level0, 2)
     far_x = jnp.where(far_i, 1.0, 0.0).astype(f32)
     far_y = jnp.where(far_j, 1.0, 0.0).astype(f32)
     ha, _, _ = taps(split(ra[0]))
@@ -152,10 +156,6 @@
     low = [jnp.where(odd_j, hs1[k], hs2[k] * far_y) for k in range(nz)]
     high = [jnp.where(odd_j, hs2[k] * far_y, hs1[k]) for k in range(nz)]
 
-    zero24 = jnp.zeros((24, LANES), f32)
-    for x in (0, 1, 2, 3, 12, 13, 14, 15):
-        for k in range(nz):
-            F0[x, k] = zero24
     for x in range(NX):
         for k in range(nz):
             h = H[x + 1, k]
@@ -165,11 +165,26 @@
             sx, sy = 0.5 * (ahead - behind), 0.5 * (up - down)
             bend = ahead - 2.0 * h + behind + (up - 2.0 * h + down)
             inv = lax.rsqrt(1.0 + sx * sx + sy * sy)
-            f = U0[x, k, 0:16, :] * (bend * (inv * inv * inv))
-            src[x, :, k * LANES : (k + 1) * LANES] = f
-            F0[x + 4, k, 0:4, :] = zero24[0:4]
-            F0[x + 4, k, 4:20, :] = f
-            F0[x + 4, k, 20:24, :] = zero24[0:4]
+            src[x, :, k * LANES : (k + 1) * LANES] = G[x, k] * (bend * (inv * inv * inv))
+    at = jnp.where(odd_i, 0, 4)
+    out_a[...] = src[pl.ds(at, 4)]
+    out_b[...] = src[pl.ds(4 - at, 4)]
+
+
+def descent(dims, src, f1_out, c1_out, c2_out, m2a, m2b, own2, F1c, F0, U0, T0, F1, U1, T1):
+    leaves, subs = dims
+    i, j, odd_i, odd_j, far_i, far_j = place(leaves, subs)
+    nz = src.shape[2] // LANES
+    zero = jnp.zeros((16, LANES), f32)
+    zero24 = jnp.zeros((24, LANES), f32)
+    for x in range(16):
+        for k in range(nz):
+            if 4 <= x < 12:
+                F0[x, k, 0:4, :] = zero24[0:4]
+                F0[x, k, 4:20, :] = src[x - 4, :, k * LANES : (k + 1) * LANES]
+                F0[x, k, 20:24, :] = zero24[0:4]
+            else:
+                F0[x, k] = zero24
 
     count_x, count_y = leaves * NX, subs * NY
     my0 = row_mask(24, j * NY - 4, count_y)
@@ -183,7 +198,7 @@
         for k in range(nz):
             U0[x, k] = (C1 * f[k] + C2 * around_f[k]) * m
 
-    each(3, 13, smooth0)
+    each(3, 13, smooth0, 2)
 
     for x in range(0, 14):
         if x < 4 or x >= 10:
@@ -198,8 +213,8 @@
             u, around_u = around(U0, x)
             total = [total[k] + (F0[x, k] - 6.0 * u[k] + around_u[k]) * m for k in range(nz)]
         for k in range(nz):
-            T0[k] = total[k]
-        for k, v in enumerate(restricted(T0, 12)):
+            T0[c, k] = total[k]
+        for k, v in enumerate(restricted(T0.at[c], 12)):
             F1[c + 3, k, 0:2, :] = zero[0:2]
             F1[c + 3, k, 2:14, :] = v
             F1[c + 3, k, 14:16, :] = zero[0:2]
@@ -218,7 +233,7 @@
         for k in range(n1):
             U1[x, k] = (C1 * f[k] + C2 * around_f[k]) * m
 
-    each(3, 11, smooth1)
+    each(3, 11, smooth1, 4)
 
     def restrict1(c):
         total = [zero] * n1
@@ -228,25 +243,20 @@
             u, around_u = around(U1, x)
             total = [total[k] + (F1[x, k] - 6.0 * u[k] + around_u[k]) * m for k in range(n1)]
         for k in range(n1):
-            T1[k] = total[k]
-        for k, v in enumerate(restricted(T1, 8)):
+            T1[c, k] = total[k]
+        for k, v in enumerate(restricted(T1.at[c], 8)):
             F1c[c, :, k * LANES : (k + 1) * LANES] = v
 
-    each(0, 6, restrict1)
+    each(0, 6, restrict1, 3)
 
     at = jnp.where(odd_i, 0, 4)
     m2a[...] = F1c[pl.ds(at, 2)]
     m2b[...] = F1c[pl.ds(4 - at, 2)]
     own2[...] = F1c[2:4]
-    for x in range(4):
-        big_a[x] = src[at + x]
-        big_b[x] = src[4 - at + x]
     for p in range(3):
         for k in range(n1):
             for h in (0, 1):
-                v = F1[4 + p + 3 * h, k]
-                big_a[4 + p, :, (h * n1 + k) * LANES : (h * n1 + k + 1) * LANES] = v
-                big_b[4 + p, :, (h * n1 + k) * LANES : (h * n1 + k + 1) * LANES] = v
+                f1_out[p, :, (h * n1 + k) * LANES : (h * n1 + k + 1) * LANES] = F1[4 + p + 3 * h, k]
     odd_c = (i // 2) % 2 == 1
     first = jnp.where(odd_c, 4, 8)
     for k in range(n1):
@@ -263,22 +273,52 @@
         out[k] = v
 
 
-def chip2(dims, got, out):
-    odd_i = place(*dims)[2]
-    half = got.shape[3] // 2
-    row = lax.broadcasted_iota(jnp.int32, (8, half), 0)
-    for c in (0, 1):
-        for x in (0, 1):
-            t = [jnp.where(odd_i, got[4 * c + j, x, :, half:], got[4 * c + j, x, :, :half]) for j in range(4)]
+def chip2(dims, got, f2, edge, out, F2, U2, T2):
+    leaves, subs = dims
+    i = lax.axis_index("leaf")
+    odd_i, c = i % 2 == 1, i // 2
+    n2 = f2.shape[2] // LANES
+    row = rows_of(8)
+    zero = jnp.zeros((16, LANES), f32)
+    for x in (0, 1, 2, 7, 8, 9):
+        for k in range(n2):
+            F2[x, k] = zero
+    for x in (0, 1, 8, 9):
+        for k in range(n2):
+            U2[x, k] = zero
+    for x in range(4):
+        for k in range(n2):
+            s = slice(k * LANES, (k + 1) * LANES)
+            t = [got[4 * (x // 2) + j, x % 2, :, s] for j in range(4)]
             one, two = pltpu.roll(t[1], 2, 0), pltpu.roll(t[2], 6, 0)
             lo = jnp.where(row < 6, pltpu.roll(t[0], 6, 0), two) + jnp.where(row >= 2, one, 0.0)
             hi = jnp.where(row >= 2, pltpu.roll(t[3], 2, 0), one) + jnp.where(row < 6, two, 0.0)
-            for k in range(out.shape[0]):
-                out[k, 2 * c + x, 0:8, :] = lo
-                out[k, 2 * c + x, 8:16, :] = hi
-
-
-def rows_out(dims, src, F1own, ra, rb, rc1, rc2, f1x, s1, s2):
+            f2[x, 0:8, s] = lo
+            f2[x, 8:16, s] = hi
+            F2[x + 3, k, 0:8, :] = lo
+            F2[x + 3, k, 8:16, :] = hi
+    edge[0] = f2[jnp.where(odd_i, 3, 0)]
+    m2 = jnp.ones((16, LANES), f32)
+    for x in range(2, 8):
+        m = plane_mask(m2, 4 * c + x - 3, 2 * leaves)
+        f, around_f = around(F2, x, True)
+        for k in range(n2):
+            U2[x, k] = (C1 * f[k] + C2 * around_f[k]) * m
+    for q in range(4):
+        total = [zero] * n2
+        for x in (2 * q + 1, 2 * q + 2):
+            m = plane_mask(m2, 4 * c + x - 3, 2 * leaves)
+            u, around_u = around(U2, x, True)
+            total = [total[k] + (F2[x, k] - 6.0 * u[k] + around_u[k]) * m for k in range(n2)]
+        for k in range(n2):
+            T2[q, k] = total[k]
+    for q in range(4):
+        for k, v in enumerate(restricted(T2.at[q], 8)):
+            for t in range(out.shape[0]):
+                out[t, q, :, k * LANES : (k + 1) * LANES] = v
+
+
+def rows_out(dims, src, f1, ra, rb, r1a, r1b, rc1, rc2, f1x, s1, s2):
     leaves, subs = dims
     i, j, odd_i, odd_j, far_i, far_j = place(leaves, subs)
     odd_c = (i // 2) % 2 == 1
@@ -287,18 +327,18 @@
     far_c = jnp.where(odd_c, c < chips - 1, c > 0)
     n = src.shape[2] // 2
 
-    def halves(ref, at, p):
-        return ref[at + p % 3, :, (p // 3) * n : (p // 3 + 1) * n]
-
-    a = [halves(ra, 4, p) for p in range(6)]
-    b = [jnp.where(far_i, halves(rb, 4, p), 0.0) for p in range(6)]
+    def halves(ref, p):
+        return ref[p % 3, :, (p // 3) * n : (p // 3 + 1) * n]
+
+    a = [halves(r1a, p) for p in range(6)]
+    b = [jnp.where(far_i, halves(r1b, p), 0.0) for p in range(6)]
     before = [jnp.where(odd_i, a[p], b[p]) for p in range(6)]
     after = [jnp.where(odd_i, b[p], a[p]) for p in range(6)]
     d1 = [rc1[0, :, h * n : (h + 1) * n] for h in (0, 1)]
     d2 = [jnp.where(far_c, rc2[0, :, h * n : (h + 1) * n], 0.0) for h in (0, 1)]
     before2 = [jnp.where(odd_c, d1[h], d2[h]) for h in (0, 1)]
     after2 = [jnp.where(odd_c, d2[h], d1[h]) for h in (0, 1)]
-    own = [halves(F1own, 4, p) for p in range(6)]
+    own = [halves(f1, p) for p in range(6)]
     planes = {}
 
     def add(x, v):
@@ -334,58 +374,23 @@
         s2[8 + x % 7, :, s] = jnp.where(odd_j, last, first)
 
 
-def ascent(dims, mine, other, src, ra, rb, f1x, rs1, rs2, press, resid, F2, U2, T2, G3, U3, V3, W2, X2, T1, F1, V1, X1, T0, F0, V0, X0):
-    leaves, subs = dims
-    i, j, odd_i, odd_j, far_i, far_j = place(leaves, subs)
-    count_x, count_y = leaves * NX, subs * NY
-    nz = src.shape[2] // LANES
-    n1, n2 = nz // 2, nz // 4
-    x2 = count_x // 4
-    zero = jnp.zeros((24, LANES), f32)
-
-    for x in list(range(5)) + list(range(x2 + 5, x2 + 10)):
-        for k in range(n2):
-            F2[x, k] = zero[0:16]
-            U2[x, k] = zero[0:16]
-    h2 = n2 // 2
-
-    def fill2(x):
-        a, b = mine[x], other[x]
-        for k in range(h2):
-            s = slice(k * LANES, (k + 1) * LANES)
-            F2[x + 5, k] = jnp.where(odd_i, b[:, s], a[:, s])
-            F2[x + 5, h2 + k] = jnp.where(odd_i, a[:, s], b[:, s])
-
-    each(0, x2, fill2)
-
-    def smooth2(x):
-        f, around_f = around(F2, x, True)
-        for k in range(n2):
-            U2[x, k] = C1 * f[k] + C2 * around_f[k]
-
-    each(5, x2 + 5, smooth2)
-
-    x3 = x2 // 2
-
-    def restrict2(c):
-        total = [zero[0:16]] * n2
-        for p in (0, 1):
-            x = 5 + 2 * c + p
-            u, around_u = around(U2, x, True)
-            total = [total[k] + (F2[x, k] - 6.0 * u[k] + around_u[k]) for k in range(n2)]
-        for k in range(n2):
-            T2[k] = total[k]
-        for k, v in enumerate(restricted(T2, 8)):
-            G3[c + 2, k] = v
-            U3[c + 2, k] = D * v
-
-    each(0, x3, restrict2)
-    n3 = n2 // 2
-    for x in (0, 1, x3 + 2, x3 + 3):
-        for k in range(n3):
-            G3[x, k] = zero[0:8]
-            U3[x, k] = zero[0:8]
-            V3[x, k] = zero[0:8]
+def coarsest(dims, got, out, G3, U3, V3):
+    leaves = dims[0]
+    chips, n3 = got.shape[0], got.shape[3] // LANES
+    zero = jnp.zeros((8, LANES), f32)
+    for k in range(n3):
+        s = slice(k * LANES, (k + 1) * LANES)
+        for x in (0, 1, leaves + 2, leaves + 3):
+            U3[x, k] = zero
+            V3[x, k] = zero
+        for c in range(chips):
+            a, b = got[c, 1, :, s], got[c, 2, :, s]
+            if c > 0:
+                a = a + got[c - 1, 3, :, s]
+            if c < chips - 1:
+                b = b + got[c + 1, 0, :, s]
+            G3[2 * c + 2, k], G3[2 * c + 3, k] = a, b
+            U3[2 * c + 2, k], U3[2 * c + 3, k] = D * a, D * b
 
     def sweep3(old, new):
         def body(x):
@@ -393,41 +398,63 @@
             for k in range(n3):
                 new[x, k] = C0 * u[k] + D * (G3[x, k] + around_u[k])
 
-        each(2, x3 + 2, body)
+        each(2, leaves + 2, body, 16)
 
     for _ in range(3):
         sweep3(U3, V3)
         sweep3(V3, U3)
     sweep3(U3, V3)
-
-    def window2(c):
-        x = c // 2
-        prolonged(T2, [V3[i + x, k] for k in range(n3)], 8)
-        for p in (0, 1):
-            w = c + p
-            for k in range(n2):
-                W2[w, k] = U2[2 * i + 1 + w, k] + T2[k]
-
-    for c in range(0, 10, 2):
-        window2(c)
+    i = lax.axis_index("leaf")
+    for x in range(5):
+        for k in range(n3):
+            out[x, :, k * LANES : (k + 1) * LANES] = V3[i + x, k]
+
+
+def ascent(dims, u3, f2, r2c1, r2c2, r2e, src, ra, rb, f1x, rs1, rs2, press, resid, F2, T2, W2, X2, T1, F1, V1, X1, T0, F0, V0, X0):
+    leaves, subs = dims
+    i, j, odd_i, odd_j, far_i, far_j = place(leaves, subs)
+    count_x, count_y = leaves * NX, subs * NY
+    nz = src.shape[2] // LANES
+    n1, n2, n3 = nz // 2, nz // 4, nz // 8
+    zero = jnp.zeros((24, LANES), f32)
+
+    c, chips = i // 2, leaves // 2
+    odd_c = c % 2 == 1
+    far_c = jnp.where(jnp.where(odd_c, c < chips - 1, c > 0), 1.0, 0.0).astype(f32)
+    far_e = jnp.where(jnp.where(odd_i, c < chips - 2, c > 1), 1.0, 0.0).astype(f32)
+    base = jnp.where(odd_i, 2, 0)
+    for k in range(n2):
+        s = slice(k * LANES, (k + 1) * LANES)
+        e = r2e[0, :, s] * far_e
+        F2[0, k] = e
+        F2[13, k] = e
+        for x in range(4):
+            a, b = r2c1[x, :, s], r2c2[x, :, s] * far_c
+            F2[x + 1, k] = jnp.where(odd_c, a, b)
+            F2[x + 5, k] = f2[x, :, s]
+            F2[x + 9, k] = jnp.where(odd_c, b, a)
     m2 = jnp.ones((16, LANES), f32)
+    for x in range(5):
+        prolonged(T2.at[x], [u3[x, :, k * LANES : (k + 1) * LANES] for k in range(n3)], 8)
+    for w in range(10):
+        m = plane_mask(m2, 2 * i + w - 4, 2 * leaves)
+        f, around_f = around(F2, base + w + 1, True)
+        for k in range(n2):
+            W2[w, k] = (C1 * f[k] + C2 * around_f[k] + T2[w // 2, k]) * m
 
     def sweep2(old, new, lo, hi):
         for w in range(lo, hi):
-            m = plane_mask(m2, 2 * i + w - 4, x2)
+            m = plane_mask(m2, 2 * i + w - 4, 2 * leaves)
             u, around_u = around(old, w, True)
             for k in range(n2):
-                new[w, k] = (C0 * u[k] + D * (F2[2 * i + 1 + w, k] + around_u[k])) * m
-
-    for w in range(10):
-        m = plane_mask(m2, 2 * i + w - 4, x2)
-        for k in range(n2):
-            W2[w, k] = W2[w, k] * m
+                new[w, k] = (C0 * u[k] + D * (F2[base + w + 1, k] + around_u[k])) * m
+
     sweep2(W2, X2, 1, 9)
     sweep2(X2, W2, 2, 8)
 
-    for k in range(n1):
-        T1[k] = zero
+    for c in range(6):
+        for k in range(n1):
+            T1[c, k] = zero
     low_j = jnp.where(j > 0, 1.0, 0.0).astype(f32)
     high_j = jnp.where(j < subs - 1, 1.0, 0.0).astype(f32)
 
@@ -449,13 +476,14 @@
 
     for c in range(6):
         cols = [pltpu.roll(W2[c + 2, k], (18 - 4 * j) % 16, 0)[0:8] for k in range(n2)]
-        prolonged(T1, cols, 8, 4)
+        prolonged(T1.at[c], cols, 8, 4)
+    for c in range(6):
         for p in (0, 1):
             x = 2 * c + p + 1
             m = plane_mask(my1, i * (NX // 2) + x - 5, count_x // 2)
             f, around_f = around(F1, x)
             for k in range(n1):
-                V1[x, k] = (C1 * f[k] + C2 * around_f[k] + T1[k]) * m
+                V1[x, k] = (C1 * f[k] + C2 * around_f[k] + T1[c, k]) * m
 
     def sweep1(old, new, lo, hi):
         def body(x):
@@ -464,7 +492,7 @@
             for k in range(n1):
                 new[x, k] = (C0 * u[k] + D * (F1[x, k] + around_u[k])) * m
 
-        each(lo, hi, body)
+        each(lo, hi, body, 2)
 
     sweep1(V1, X1, 2, 12)
     sweep1(X1, V1, 3, 11)
@@ -493,18 +521,17 @@
     my0 = row_mask(24, j * NY - 4, count_y)
 
     def start0(c):
-        prolonged(T0, [V1[c + 3, k, 6:18, :] for k in range(n1)], 12)
-        for p in (0, 1):
-            x = 2 * c + p
-
-            @pl.when(jnp.logical_and(x > 0, x < 15))
-            def _():
-                m = plane_mask(my0, i * NX + x - 4, count_x)
-                f, around_f = around(F0, x)
-                for k in range(nz):
-                    V0[x, k] = (C1 * f[k] + C2 * around_f[k] + T0[k]) * m
-
-    each(0, 8, start0)
+        prolonged(T0.at[c], [V1[c + 3, k, 6:18, :] for k in range(n1)], 12)
+
+    each(0, 8, start0, 2)
+
+    def smooth0(x):
+        m = plane_mask(my0, i * NX + x - 4, count_x)
+        f, around_f = around(F0, x)
+        for k in range(nz):
+            V0[x, k] = (C1 * f[k] + C2 * around_f[k] + T0[x // 2, k]) * m
+
+    each(1, 15, smooth0, 2)
 
     def sweep0(old, new, lo, hi):
         def body(x):
@@ -513,7 +540,7 @@
             for k in range(nz):
                 new[x, k] = (C0 * u[k] + D * (F0[x, k] + around_u[k])) * m
 
-        each(lo, hi, body)
+        each(lo, hi, body, 2)
 
     sweep0(V0, X0, 2, 14)
     sweep0(X0, V0, 3, 13)
@@ -525,7 +552,7 @@
             press[x, :, s] = u[k][4:20]
             resid[x, :, s] = (F0[x + 4, k] - 6.0 * u[k] + around_u[k])[4:20]
 
-    each(0, NX, finish)
+    each(0, NX, finish, 2)
 
 
 def call(kernel, outs, scratch, *args):
@@ -553,14 +580,19 @@
     s2 = table(lambda i, j: (i, odd(j)) if inner(odd(j), subs) else (i ^ 1, j))
     c1 = table(lambda i, j: (i ^ 2, j))
     c2 = table(lambda i, j: (2 * odd(i // 2) + i % 2, j) if inner(odd(i // 2), leaves // 2) else (i, j ^ 1))
-    return a, b, s1, s2, c1, c2
+    def two_on(i):
+        t = 2 * (i // 2 + (2 if i % 2 else -2)) + 1 - i % 2
+        return t if inner(t, leaves) else None
+
+    e = table(lambda i, j: (two_on(i), j) if two_on(i) is not None else (i, j ^ 1))
+    return a, b, s1, s2, c1, c2, e
 
 
 def shards(dims, volume_fraction, interface_mask):
     leaves, subs = dims
     depth = volume_fraction.shape[2]
     nz = depth // LANES
-    pa, pb, ps1, ps2, pc1, pc2 = swaps(leaves, subs)
+    pa, pb, ps1, ps2, pc1, pc2, pe = swaps(leaves, subs)
     move = lambda v, table: lax.ppermute(v, AXES, table)
     i, j = lax.axis_index("leaf"), lax.axis_index("sub")
     odd_i, odd_j = i % 2, j % 2
@@ -572,29 +604,11 @@
     ha, hb = move(plane(at_x), pa), move(plane(NX - 1 - at_x), pb)
     hs1, hs2 = move(rows(at_y), ps1), move(rows(NY - 1 - at_y), ps2)
 
-    n1 = nz // 2
-    src, big_a, big_b, m1, m2, m2a, m2b, own2 = call(
-        functools.partial(descent, dims),
-        [
-            (NX, NY, depth),
-            (7, 16, depth),
-            (7, 16, depth),
-            (1, 16, depth),
-            (1, 16, depth),
-            (2, 8, depth // 4),
-            (2, 8, depth // 4),
-            (2, 8, depth // 4),
-        ],
-        [
-            (6, 8, depth // 4),
-            (NX + 2, nz, 16, LANES),
-            (16, nz, 24, LANES),
-            (16, nz, 24, LANES),
-            (nz, 24, LANES),
-            (14, n1, 16, LANES),
-            (14, n1, 16, LANES),
-            (n1, 16, LANES),
-        ],
+    n1, n2, n3 = nz // 2, nz // 4, nz // 8
+    src, out_a, out_b = call(
+        functools.partial(source, dims),
+        [(NX, NY, depth), (4, NY, depth), (4, NY, depth)],
+        [(NX + 2, nz, 16, LANES), (NX, nz, 16, LANES)],
         vf,
         interface_mask,
         ha,
@@ -602,54 +616,79 @@
         hs1,
         hs2,
     )
+    ra, rb = move(out_a, pa), move(out_b, pb)
+    f1, m1, m2, m2a, m2b, own2 = call(
+        functools.partial(descent, dims),
+        [(3, 16, depth), (1, 16, depth), (1, 16, depth)] + [(2, 8, depth // 4)] * 3,
+        [
+            (6, 8, depth // 4),
+            (16, nz, 24, LANES),
+            (16, nz, 24, LANES),
+            (8, nz, 24, LANES),
+            (14, n1, 16, LANES),
+            (14, n1, 16, LANES),
+            (6, n1, 16, LANES),
+        ],
+        src,
+    )
     r2a, r2b = move(m2a, pa), move(m2b, pb)
-    ra, rb = move(big_a, pa), move(big_b, pb)
+    (out,) = call(functools.partial(sum2, dims), [(2 * subs, 2, 8, depth // 4)], [], own2, r2a, r2b)
+    out, g1, m1, m2 = lax.optimization_barrier((out, f1, m1, m2))
+    r1a, r1b = move(g1, pa), move(g1, pb)
     rc1, rc2 = move(m1, pc1), move(m2, pc2)
-
-    (out,) = call(functools.partial(sum2, dims), [(2 * subs, 2, 8, depth // 4)], [], own2, r2a, r2b)
     group = [list(range(k, k + 2 * subs)) for k in range(0, leaves * subs, 2 * subs)]
     got = lax.all_to_all(out, AXES, 0, 0, axis_index_groups=group)
-    chips = leaves // 2
-    (out,) = call(functools.partial(chip2, dims), [(chips, 4, 16, depth // 8)], [], got)
+    got, r1a, r1b, rc1, rc2 = lax.optimization_barrier((got, r1a, r1b, rc1, rc2))
     f1x, s1, s2 = call(
         functools.partial(rows_out, dims),
         [(14, 16, depth // 2), (15, 8, depth), (15, 8, depth)],
         [],
         src,
-        big_a,
+        f1,
         ra,
         rb,
+        r1a,
+        r1b,
         rc1,
         rc2,
     )
+    chips = leaves // 2
+    f2, edge, out = call(
+        functools.partial(chip2, dims),
+        [(4, 16, depth // 4), (1, 16, depth // 4), (chips, 4, 8, depth // 8)],
+        [(10, n2, 16, LANES), (10, n2, 16, LANES), (4, n2, 16, LANES)],
+        got,
+    )
+    out, s1, s2, g2, edge = lax.optimization_barrier((out, s1, s2, f2, edge))
     rs1, rs2 = move(s1, ps1), move(s2, ps2)
+    r2c1, r2c2, r2e = move(g2, pc1), move(g2, pc2), move(edge, pe)
     group = [[(2 * c + k) * subs + s for c in range(chips)] for k in (0, 1) for s in range(subs)]
-    mine = lax.all_to_all(out, AXES, 0, 0, axis_index_groups=group).reshape(4 * chips, 16, depth // 8)
-    other = move(mine, pa)
-    x2 = 2 * leaves
-    press, resid = call(
+    got = lax.all_to_all(out, AXES, 0, 0, axis_index_groups=group)
+    (u3,) = call(
+        functools.partial(coarsest, dims), [(5, 8, depth // 8)], [(leaves + 4, n3, 8, LANES)] * 3, got
+    )
+    return call(
         functools.partial(ascent, dims),
         [(NX, NY, depth), (NX, NY, depth)],
         [
-            (x2 + 10, nz // 4, 16, LANES),
-            (x2 + 10, nz // 4, 16, LANES),
-            (nz // 4, 16, LANES),
-            (x2 // 2 + 4, nz // 8, 8, LANES),
-            (x2 // 2 + 4, nz // 8, 8, LANES),
-            (x2 // 2 + 4, nz // 8, 8, LANES),
-            (10, nz // 4, 16, LANES),
-            (10, nz // 4, 16, LANES),
-            (n1, 24, LANES),
+            (14, n2, 16, LANES),
+            (5, n2, 16, LANES),
+            (10, n2, 16, LANES),
+            (10, n2, 16, LANES),
+            (6, n1, 24, LANES),
             (14, n1, 24, LANES),
             (14, n1, 24, LANES),
             (14, n1, 24, LANES),
-            (nz, 24, LANES),
+            (8, nz, 24, LANES),
             (16, nz, 24, LANES),
             (16, nz, 24, LANES),
             (16, nz, 24, LANES),
         ],
-        mine,
-        other,
+        u3,
+        f2,
+        r2c1,
+        r2c2,
+        r2e,
         src,
         ra,
         rb,
@@ -657,7 +696,6 @@
         rs1,
         rs2,
     )
-    return press, resid
 
 
 def solution(mesh):

time: 112 us -> 69.4 us (0.62); the launches traced: 110 us -> 68.7 us
  Pallas kernels: 49.6 us -> 17.9 us
  waiting for transfers between devices: 26.9 us -> 15.2 us
  starting transfers between devices: 20.1 us -> 31.6 us
  blocking collectives: 9.66 us -> 0 us
    pallas_call x5 -> x7, Pallas kernels: 49.6 us -> 17.9 us  [call(): pl.pallas_call(kernel, out_shape=[jax.ShapeDtypeStruct(s, f32) for s in o...]
    all_to_all x1 -> x0, blocking collectives: 9.66 us -> none  [shards(): got = lax.all_to_all(out, AXES, 0, 0, axis_index_groups=group)]
    ppermute x13 -> x17, waiting for transfers between devices: 18.5 us -> 9.52 us  [shards(): move = lambda v, table: lax.ppermute(v, AXES, table)]
    all_to_all x1 -> x2, starting transfers between devices: 8.97 us -> 16.1 us  [shards(): got = lax.all_to_all(out, AXES, 0, 0, axis_index_groups=group)]
    ppermute x13 -> x17, starting transfers between devices: 11.2 us -> 15.5 us  [shards(): move = lambda v, table: lax.ppermute(v, AXES, table)]
    all_to_all x1 -> x2, waiting for transfers between devices: 8.35 us -> 5.72 us  [shards(): got = lax.all_to_all(out, AXES, 0, 0, axis_index_groups=group)]
  transfers between devices with their start and end apart: 14 -> 19, of which waited for: 8 -> 7; matrix products, arithmetic and copies ran while one was open for 1% -> 2% of each run, Pallas kernels for 0% -> 11%
where the time goes in v2:
time: 69.4 us; the launch traced here: 68.7 us
  starting transfers between devices  31.6 us (46%)
  Pallas kernels  17.9 us (26%)
  waiting for transfers between devices  15.2 us (22%)
  local copies, waits for them, and re-layouts  3.07 us (4%)
  between operations  0.79 us (1%)
    pallas_call x7, Pallas kernels, call(): pl.pallas_call(kernel, out_shape=[jax.ShapeDtypeStruct(s, f32) for s in o...  17.9 us
    all_to_all x2, starting transfers between devices, shards(): got = lax.all_to_all(out, AXES, 0, 0, axis_index_groups=group)  16.1 us
    ppermute x17, starting transfers between devices, shards(): move = lambda v, table: lax.ppermute(v, AXES, table)  15.5 us
    ppermute x17, waiting for transfers between devices, shards(): move = lambda v, table: lax.ppermute(v, AXES, table)  9.52 us
    all_to_all x2, waiting for transfers between devices, shards(): got = lax.all_to_all(out, AXES, 0, 0, axis_index_groups=group)  5.72 us
  transfers between devices with their start and end apart: 19, of which 7 were waited for; matrix products, arithmetic and copies ran while one was open for 2% of the time, Pallas kernels for 11%

profile of v2, /device:TPU:2, one launch (start us, length us, event | category | flops | bytes accessed | tf_op | source)
XLA Modules:
  0.0 68.7 jit_solution(9989585973559146208)
XLA Ops:
  0.6 0.0 copy-start
  0.7 0.9 %constant_dynamic-slice_fusion.2 = (f32[1,16,1024]{2,1,0:T(8,128)S(1)}, f32[1,16,1024]{2,1,0:T(8,128)S(1)}) fusion(f32[8,16,1024]{2,1,0:T(8,128)} %vf.1, s32[]{:T(128)S(6)} %select_n.25, s32[]{:T(128)S(6)} %select_n.24), kind=kLoop, calls=%fused_computation.4 | loop fusion | bytes 262152 | tf_op jit(solution)/shard_map/dynamic_slice | solution.py:602
  1.6 0.5 collective-permute-start.1
  2.1 1.2 %collective-permute-start = (f32[1,16,1024]{2,1,0:T(8,128)S(1)}, f32[1,16,1024]{2,1,0:T(8,128)S(1)}, u32[]{:S(2)}, u32[]{:S(2)}) collective-permute-start(f32[1,16,1024]{2,1,0:T(8,128)S(1)} %get-tuple-element.63), channel_id=1, source_target_pairs={{0,4},{1,5},{2,6},{3,7},{4,0},{5,1},{6,2},{7,3},{8,12},{9,13},{10,... | collective-permute-start | bytes 196616 | tf_op jit(solution)/shard_map/ppermute | solution.py:596
  3.4 1.1 %constant_dynamic-slice_fusion = (f32[8,1,1024]{2,1,0:T(1,128)S(1)}, f32[8,1,1024]{2,1,0:T(1,128)S(1)}) fusion(f32[8,16,1024]{2,1,0:T(8,128)} %vf.1, s32[]{:T(128)S(6)} %select_n.28, s32[]{:T(128)S(6)} %select_n.27), kind=kLoop, calls=%fused_computation.2 | loop fusion | bytes 131080 | tf_op jit(solution)/shard_map/dynamic_slice | solution.py:603
  4.5 0.6 collective-permute-start.2
  5.1 2.2 %collective-permute-start.3 = (f32[8,1024]{1,0:T(8,128)S(1)}, f32[8,1024]{1,0:T(8,128)S(1)}, u32[]{:S(2)}, u32[]{:S(2)}) collective-permute-start(f32[8,1024]{1,0:T(8,128)S(1)} %bitcast.7), channel_id=1, source_target_pairs={{0,4},{1,2},{2,1},{3,7},{4,0},{5,6},{6,5},{7,3},{8,12},{9,10},{10,... | collective-permute-start | bytes 98312 | tf_op jit(solution)/shard_map/ppermute | solution.py:596
  7.3 1.1 %collective-permute-done.2.rs1 = f32[8,1024]{1,0:T(8,128)S(1)} collective-permute-done((f32[8,1024]{1,0:T(8,128)S(1)}, f32[8,1024]{1,0:T(8,128)S(1)}, u32[]{:S(2)}, u32[]{:S(2)}) %collective-permute-start.2) | collective-permute-done | bytes 32800 | tf_op jit(solution)/shard_map/ppermute | solution.py:596
  8.5 0.8 %collective-permute-done.3.rs2 = f32[8,1024]{1,0:T(8,128)S(1)} collective-permute-done((f32[8,1024]{1,0:T(8,128)S(1)}, f32[8,1024]{1,0:T(8,128)S(1)}, u32[]{:S(2)}, u32[]{:S(2)}) %collective-permute-start.3) | collective-permute-done | bytes 32800 | tf_op jit(solution)/shard_map/ppermute | solution.py:596
  9.2 0.0 collective-permute-done.1.rb
  9.2 0.0 collective-permute-done.ra
  9.2 0.0 copy-done
  9.2 0.0 copy-start.1
  9.2 1.0 %copy-done.1 = s32[8,16,1024]{2,1,0:T(8,128)S(1)} copy-done((s32[8,16,1024]{2,1,0:T(8,128)S(1)}, s32[8,16,1024]{2,1,0:T(8,128)}, u32[]{:S(2)}) %copy-start.1) | copy-done | bytes 524312
  10.3 2.1 %shard_map.41 = (f32[8,16,1024]{2,1,0:T(8,128)S(1)}, f32[4,16,1024]{2,1,0:T(8,128)S(1)}, f32[4,16,1024]{2,1,0:T(8,128)S(1)}) custom-call(f32[8,16,1024]{2,1,0:T(8,128)S(1)} %copy-done, s32[8,16,1024]{2,1,0:T(8,128)S(1)} %copy-done.1, f32[1,16,1024]{2,1,0:T(8,128)S(1)} %collective-permute-done.ra, f32[1,16,1024]{2,1,0:T(8,128)S(1)} %collective-permute-done.1.rb, ...), custom_call_target="tpu_custom_call" | custom-call | tf_op jit(solution)/shard_map/pallas_call | solution.py:559
  12.4 0.1 collective-permute-start.10
  12.4 0.1 collective-permute-start.11
  12.5 4.1 %shard_map.42 = (f32[3,16,1024]{2,1,0:T(8,128)S(1)}, f32[1,16,1024]{2,1,0:T(8,128)S(1)}, f32[1,16,1024]{2,1,0:T(8,128)S(1)}, f32[2,8,256]{2,1,0:T(8,128)S(1)}, f...) custom-call(f32[8,16,1024]{2,1,0:T(8,128)S(1)} %get-tuple-element.31.src), custom_call_target="tpu_custom_call" | custom-call | tf_op jit(solution)/shard_map/pallas_call | solution.py:559
  16.6 1.8 %collective-permute-start.4 = (f32[2,8,256]{2,1,0:T(8,128)S(1)}, f32[2,8,256]{2,1,0:T(8,128)S(1)}, u32[]{:S(2)}, u32[]{:S(2)}) collective-permute-start(f32[2,8,256]{2,1,0:T(8,128)S(1)} %get-tuple-element.33), channel_id=1, source_target_pairs={{0,4},{1,5},{2,6},{3,7},{4,0},{5,1},{6,2},{7,3},{8,12},{9,13},{10,... | collective-permute-start | bytes 49160 | tf_op jit(solution)/shard_map/ppermute | solution.py:596
  18.4 0.4 collective-permute-start.5
  18.8 0.4 collective-permute-done.4.ra
  19.2 2.9 %collective-permute-done.5.rb = f32[2,8,256]{2,1,0:T(8,128)S(1)} collective-permute-done((f32[2,8,256]{2,1,0:T(8,128)S(1)}, f32[2,8,256]{2,1,0:T(8,128)S(1)}, u32[]{:S(2)}, u32[]{:S(2)}) %collective-permute-start.5) | collective-permute-done | bytes 16416 | tf_op jit(solution)/shard_map/ppermute | solution.py:596
  22.1 0.7 shard_map.43
  22.8 0.4 collective-permute-start.7
  23.2 0.4 collective-permute-start.6
  23.6 1.6 %collective-permute-start.8 = (f32[1,16,1024]{2,1,0:T(8,128)S(1)}, f32[1,16,1024]{2,1,0:T(8,128)S(1)}, u32[]{:S(2)}, u32[]{:S(2)}) collective-permute-start(f32[1,16,1024]{2,1,0:T(8,128)S(1)} %get-tuple-element.40), channel_id=1, source_target_pairs={{0,8},{1,9},{2,10},{3,11},{4,12},{5,13},{6,14},{7,15},{8,0},{9,1},... | collective-permute-start | bytes 196616 | tf_op jit(solution)/shard_map/ppermute | solution.py:596
  25.2 5.4 %all-to-all-start = ((f32[8,2,8,256]{3,2,1,0:T(8,128)}), f32[8,2,8,256]{3,2,1,0:T(8,128)S(1)}, u32[]{:S(2)}, u32[]{:S(2)}) async-start(f32[8,2,8,256]{3,2,1,0:T(8,128)} %shard_map.43), calls=%async_computation | async-start | bytes 262144 | tf_op jit(solution)/shard_map/all_to_all | solution.py:640
  30.5 0.0 collective-permute-done.8.rc1
  30.5 0.1 collective-permute-start.9
  30.6 4.3 %collective-permute-done.9.rc2 = f32[1,16,1024]{2,1,0:T(8,128)S(1)} collective-permute-done((f32[1,16,1024]{2,1,0:T(8,128)S(1)}, f32[1,16,1024]{2,1,0:T(8,128)S(1)}, u32[]{:S(2)}, u32[]{:S(2)}) %collective-permute-start.9) | collective-permute-done | bytes 65568 | tf_op jit(solution)/shard_map/ppermute | solution.py:596
  34.9 0.4 all-to-all-done.got
  35.3 0.0 collective-permute-done.7.r1b
  35.3 0.0 collective-permute-done.6.r1a
  35.3 1.1 %shard_map.44 = (f32[4,16,256]{2,1,0:T(8,128)S(1)}, f32[1,16,256]{2,1,0:T(8,128)S(1)}, f32[16,4,8,128]{3,2,1,0:T(8,128)}) custom-call(f32[8,2,8,256]{3,2,1,0:T(8,128)S(1)} %all-to-all-done.got), custom_call_target="tpu_custom_call" | custom-call | tf_op jit(solution)/shard_map/pallas_call | solution.py:559
  36.4 0.0 collective-permute-done.10.ra
  36.4 0.0 collective-permute-done.11.rb
  36.4 1.0 %shard_map.45 = (f32[14,16,512]{2,1,0:T(8,128)S(1)}, f32[15,8,1024]{2,1,0:T(8,128)}, f32[15,8,1024]{2,1,0:T(8,128)S(1)}) custom-call(f32[8,16,1024]{2,1,0:T(8,128)S(1)} %get-tuple-element.31.src, f32[3,16,1024]{2,1,0:T(8,128)S(1)} %get-tuple-element.39.f1, f32[4,16,1024]{2,1,0:T(8,128)S(1)} %collective-permute-done.10.ra, ...), custom_call_target="tpu_custom_call" | custom-call | tf_op jit(solution)/shard_map/pallas_call | solution.py:559
  37.4 1.2 %collective-permute-start.15 = (f32[15,8,1024]{2,1,0:T(8,128)}, f32[15,8,1024]{2,1,0:T(8,128)S(1)}, u32[]{:S(2)}, u32[]{:S(2)}) collective-permute-start(f32[15,8,1024]{2,1,0:T(8,128)} %get-tuple-element.58), channel_id=1, source_target_pairs={{0,1},{1,0},{2,3},{3,2},{4,5},{5,4},{6,7},{7,6},{8,9},{9,8},{10,11... | collective-permute-start | bytes 1474568 | tf_op jit(solution)/shard_map/ppermute | solution.py:596
  38.7 1.5 %collective-permute-start.16 = (f32[15,8,1024]{2,1,0:T(8,128)S(1)}, f32[15,8,1024]{2,1,0:T(8,128)S(1)}, u32[]{:S(2)}, u32[]{:S(2)}) collective-permute-start(f32[15,8,1024]{2,1,0:T(8,128)S(1)} %get-tuple-element.59), channel_id=1, source_target_pairs={{0,4},{1,2},{2,1},{3,7},{4,0},{5,6},{6,5},{7,3},{8,12},{9,10},{10,... | collective-permute-start | bytes 1474568 | tf_op jit(solution)/shard_map/ppermute | solution.py:596
  40.2 10.7 %all-to-all-start.1 = ((f32[16,4,8,128]{3,2,1,0:T(8,128)}), f32[16,4,8,128]{3,2,1,0:T(8,128)S(1)}, u32[]{:S(2)}, u32[]{:S(2)}) async-start(f32[16,4,8,128]{3,2,1,0:T(8,128)} %get-tuple-element.54), calls=%async_computation.1 | async-start | bytes 524288 | tf_op jit(solution)/shard_map/all_to_all | solution.py:666
  50.9 0.1 collective-permute-start.13
  51.0 3.3 %collective-permute-start.12 = (f32[4,16,256]{2,1,0:T(8,128)S(1)}, f32[4,16,256]{2,1,0:T(8,128)S(1)}, u32[]{:S(2)}, u32[]{:S(2)}) collective-permute-start(f32[4,16,256]{2,1,0:T(8,128)S(1)} %get-tuple-element.55.f2), channel_id=1, source_target_pairs={{0,8},{1,9},{2,10},{3,11},{4,12},{5,13},{6,14},{7,15},{8,0},{9,1},... | collective-permute-start | bytes 196616 | tf_op jit(solution)/shard_map/ppermute | solution.py:596
  54.3 0.0 collective-permute-start.14
  54.3 5.3 %all-to-all-done.1.got = f32[16,4,8,128]{3,2,1,0:T(8,128)S(1)} async-done(((f32[16,4,8,128]{3,2,1,0:T(8,128)}), f32[16,4,8,128]{3,2,1,0:T(8,128)S(1)}, u32[]{:S(2)}, u32[]{:S(2)}) %all-to-all-start.1) | async-done | bytes 262176 | tf_op jit(solution)/shard_map/all_to_all | solution.py:666
  59.6 1.5 %shard_map.46.u3 = f32[5,8,128]{2,1,0:T(8,128)S(1)} custom-call(f32[16,4,8,128]{3,2,1,0:T(8,128)S(1)} %all-to-all-done.1.got), custom_call_target="tpu_custom_call" | custom-call | tf_op jit(solution)/shard_map/pallas_call | solution.py:559
  61.1 0.0 collective-permute-done.14.r2e
  61.1 0.0 collective-permute-done.13.r2c2
  61.1 0.0 collective-permute-done.12.r2c1
  61.1 0.0 collective-permute-done.15.rs1
  61.2 0.0 collective-permute-done.16.rs2
  61.2 7.5 %shard_map.47 = (f32[8,16,1024]{2,1,0:T(8,128)}, f32[8,16,1024]{2,1,0:T(8,128)}) custom-call(f32[5,8,128]{2,1,0:T(8,128)S(1)} %shard_map.46.u3, f32[4,16,256]{2,1,0:T(8,128)S(1)} %get-tuple-element.55.f2, f32[4,16,256]{2,1,0:T(8,128)S(1)} %collective-permute-done.12.r2c1, f32[4,16,256]{2,1,0:T(8,128)S(1)} %collective-permute-done.13.r2c2, ...), custom_call_target="tpu_custom_call" | custom-call | tf_op jit(solution)/shard_map/pallas_call | solution.py:559
  (2 shorter events, 0.0 us)
Async XLA Ops:
  0.6 8.6 %copy-start = (f32[8,16,1024]{2,1,0:T(8,128)S(1)}, f32[8,16,1024]{2,1,0:T(8,128)}, u32[]{:S(2)}) copy-start(f32[8,16,1024]{2,1,0:T(8,128)} %vf.1) | copy-start | bytes 1572868
  1.6 7.6 %collective-permute-start.1 = (f32[1,16,1024]{2,1,0:T(8,128)S(1)}, f32[1,16,1024]{2,1,0:T(8,128)S(1)}, u32[]{:S(2)}, u32[]{:S(2)}) collective-permute-start(f32[1,16,1024]{2,1,0:T(8,128)S(1)} %get-tuple-element.62), channel_id=1, source_target_pairs={{0,1},{1,0},{2,3},{3,2},{4,8},{5,9},{6,10},{7,11},{8,4},{9,5},{10,... | collective-permute-start | bytes 196616 | tf_op jit(solution)/shard_map/ppermute | solution.py:596
  2.1 7.1 %collective-permute-start = (f32[1,16,1024]{2,1,0:T(8,128)S(1)}, f32[1,16,1024]{2,1,0:T(8,128)S(1)}, u32[]{:S(2)}, u32[]{:S(2)}) collective-permute-start(f32[1,16,1024]{2,1,0:T(8,128)S(1)} %get-tuple-element.63), channel_id=1, source_target_pairs={{0,4},{1,5},{2,6},{3,7},{4,0},{5,1},{6,2},{7,3},{8,12},{9,13},{10,... | collective-permute-start | bytes 196616 | tf_op jit(solution)/shard_map/ppermute | solution.py:596
  4.5 4.0 %collective-permute-start.2 = (f32[8,1024]{1,0:T(8,128)S(1)}, f32[8,1024]{1,0:T(8,128)S(1)}, u32[]{:S(2)}, u32[]{:S(2)}) collective-permute-start(f32[8,1024]{1,0:T(8,128)S(1)} %bitcast.6), channel_id=1, source_target_pairs={{0,1},{1,0},{2,3},{3,2},{4,5},{5,4},{6,7},{7,6},{8,9},{9,8},{10,11... | collective-permute-start | bytes 98312 | tf_op jit(solution)/shard_map/ppermute | solution.py:596
  5.1 4.1 %collective-permute-start.3 = (f32[8,1024]{1,0:T(8,128)S(1)}, f32[8,1024]{1,0:T(8,128)S(1)}, u32[]{:S(2)}, u32[]{:S(2)}) collective-permute-start(f32[8,1024]{1,0:T(8,128)S(1)} %bitcast.7), channel_id=1, source_target_pairs={{0,4},{1,2},{2,1},{3,7},{4,0},{5,6},{6,5},{7,3},{8,12},{9,10},{10,... | collective-permute-start | bytes 98312 | tf_op jit(solution)/shard_map/ppermute | solution.py:596
  9.2 1.0 %copy-start.1 = (s32[8,16,1024]{2,1,0:T(8,128)S(1)}, s32[8,16,1024]{2,1,0:T(8,128)}, u32[]{:S(2)}) copy-start(s32[8,16,1024]{2,1,0:T(8,128)} %mask.1) | copy-start | bytes 1572868
  12.4 24.1 %collective-permute-start.10 = (f32[4,16,1024]{2,1,0:T(8,128)S(1)}, f32[4,16,1024]{2,1,0:T(8,128)S(1)}, u32[]{:S(2)}, u32[]{:S(2)}) collective-permute-start(f32[4,16,1024]{2,1,0:T(8,128)S(1)} %get-tuple-element.44), channel_id=1, source_target_pairs={{0,4},{1,5},{2,6},{3,7},{4,0},{5,1},{6,2},{7,3},{8,12},{9,13},{10,... | collective-permute-start | bytes 786440 | tf_op jit(solution)/shard_map/ppermute | solution.py:596
  12.4 24.0 %collective-permute-start.11 = (f32[4,16,1024]{2,1,0:T(8,128)S(1)}, f32[4,16,1024]{2,1,0:T(8,128)S(1)}, u32[]{:S(2)}, u32[]{:S(2)}) collective-permute-start(f32[4,16,1024]{2,1,0:T(8,128)S(1)} %get-tuple-element.45), channel_id=1, source_target_pairs={{0,1},{1,0},{2,3},{3,2},{4,8},{5,9},{6,10},{7,11},{8,4},{9,5},{10,... | collective-permute-start | bytes 786440 | tf_op jit(solution)/shard_map/ppermute | solution.py:596
  16.6 2.6 %collective-permute-start.4 = (f32[2,8,256]{2,1,0:T(8,128)S(1)}, f32[2,8,256]{2,1,0:T(8,128)S(1)}, u32[]{:S(2)}, u32[]{:S(2)}) collective-permute-start(f32[2,8,256]{2,1,0:T(8,128)S(1)} %get-tuple-element.33), channel_id=1, source_target_pairs={{0,4},{1,5},{2,6},{3,7},{4,0},{5,1},{6,2},{7,3},{8,12},{9,13},{10,... | collective-permute-start | bytes 49160 | tf_op jit(solution)/shard_map/ppermute | solution.py:596
  18.4 3.7 %collective-permute-start.5 = (f32[2,8,256]{2,1,0:T(8,128)S(1)}, f32[2,8,256]{2,1,0:T(8,128)S(1)}, u32[]{:S(2)}, u32[]{:S(2)}) collective-permute-start(f32[2,8,256]{2,1,0:T(8,128)S(1)} %get-tuple-element.34), channel_id=1, source_target_pairs={{0,1},{1,0},{2,3},{3,2},{4,8},{5,9},{6,10},{7,11},{8,4},{9,5},{10,... | collective-permute-start | bytes 49160 | tf_op jit(solution)/shard_map/ppermute | solution.py:596
  22.8 12.6 %collective-permute-start.7 = (f32[3,16,1024]{2,1,0:T(8,128)S(1)}, f32[3,16,1024]{2,1,0:T(8,128)S(1)}, u32[]{:S(2)}, u32[]{:S(2)}) collective-permute-start(f32[3,16,1024]{2,1,0:T(8,128)S(1)} %get-tuple-element.39.f1), channel_id=1, source_target_pairs={{0,1},{1,0},{2,3},{3,2},{4,8},{5,9},{6,10},{7,11},{8,4},{9,5},{10,... | collective-permute-start | bytes 589832 | tf_op jit(solution)/shard_map/ppermute | solution.py:596
  23.2 12.1 %collective-permute-start.6 = (f32[3,16,1024]{2,1,0:T(8,128)S(1)}, f32[3,16,1024]{2,1,0:T(8,128)S(1)}, u32[]{:S(2)}, u32[]{:S(2)}) collective-permute-start(f32[3,16,1024]{2,1,0:T(8,128)S(1)} %get-tuple-element.39.f1), channel_id=1, source_target_pairs={{0,4},{1,5},{2,6},{3,7},{4,0},{5,1},{6,2},{7,3},{8,12},{9,13},{10,... | collective-permute-start | bytes 589832 | tf_op jit(solution)/shard_map/ppermute | solution.py:596
  23.6 6.9 %collective-permute-start.8 = (f32[1,16,1024]{2,1,0:T(8,128)S(1)}, f32[1,16,1024]{2,1,0:T(8,128)S(1)}, u32[]{:S(2)}, u32[]{:S(2)}) collective-permute-start(f32[1,16,1024]{2,1,0:T(8,128)S(1)} %get-tuple-element.40), channel_id=1, source_target_pairs={{0,8},{1,9},{2,10},{3,11},{4,12},{5,13},{6,14},{7,15},{8,0},{9,1},... | collective-permute-start | bytes 196616 | tf_op jit(solution)/shard_map/ppermute | solution.py:596
  25.2 10.2 %all-to-all-start = ((f32[8,2,8,256]{3,2,1,0:T(8,128)}), f32[8,2,8,256]{3,2,1,0:T(8,128)S(1)}, u32[]{:S(2)}, u32[]{:S(2)}) async-start(f32[8,2,8,256]{3,2,1,0:T(8,128)} %shard_map.43), calls=%async_computation | async-start | bytes 262144 | tf_op jit(solution)/shard_map/all_to_all | solution.py:640
  30.5 4.4 %collective-permute-start.9 = (f32[1,16,1024]{2,1,0:T(8,128)S(1)}, f32[1,16,1024]{2,1,0:T(8,128)S(1)}, u32[]{:S(2)}, u32[]{:S(2)}) collective-permute-start(f32[1,16,1024]{2,1,0:T(8,128)S(1)} %get-tuple-element.41), channel_id=1, source_target_pairs={{0,1},{1,0},{2,3},{3,2},{4,5},{5,4},{6,7},{7,6},{8,16},{9,17},{10,... | collective-permute-start | bytes 196616 | tf_op jit(solution)/shard_map/ppermute | solution.py:596
  37.4 23.7 %collective-permute-start.15 = (f32[15,8,1024]{2,1,0:T(8,128)}, f32[15,8,1024]{2,1,0:T(8,128)S(1)}, u32[]{:S(2)}, u32[]{:S(2)}) collective-permute-start(f32[15,8,1024]{2,1,0:T(8,128)} %get-tuple-element.58), channel_id=1, source_target_pairs={{0,1},{1,0},{2,3},{3,2},{4,5},{5,4},{6,7},{7,6},{8,9},{9,8},{10,11... | collective-permute-start | bytes 1474568 | tf_op jit(solution)/shard_map/ppermute | solution.py:596
  38.7 22.5 %collective-permute-start.16 = (f32[15,8,1024]{2,1,0:T(8,128)S(1)}, f32[15,8,1024]{2,1,0:T(8,128)S(1)}, u32[]{:S(2)}, u32[]{:S(2)}) collective-permute-start(f32[15,8,1024]{2,1,0:T(8,128)S(1)} %get-tuple-element.59), channel_id=1, source_target_pairs={{0,4},{1,2},{2,1},{3,7},{4,0},{5,6},{6,5},{7,3},{8,12},{9,10},{10,... | collective-permute-start | bytes 1474568 | tf_op jit(solution)/shard_map/ppermute | solution.py:596
  40.2 19.4 %all-to-all-start.1 = ((f32[16,4,8,128]{3,2,1,0:T(8,128)}), f32[16,4,8,128]{3,2,1,0:T(8,128)S(1)}, u32[]{:S(2)}, u32[]{:S(2)}) async-start(f32[16,4,8,128]{3,2,1,0:T(8,128)} %get-tuple-element.54), calls=%async_computation.1 | async-start | bytes 524288 | tf_op jit(solution)/shard_map/all_to_all | solution.py:666
  50.9 10.2 %collective-permute-start.13 = (f32[4,16,256]{2,1,0:T(8,128)S(1)}, f32[4,16,256]{2,1,0:T(8,128)S(1)}, u32[]{:S(2)}, u32[]{:S(2)}) collective-permute-start(f32[4,16,256]{2,1,0:T(8,128)S(1)} %get-tuple-element.55.f2), channel_id=1, source_target_pairs={{0,1},{1,0},{2,3},{3,2},{4,5},{5,4},{6,7},{7,6},{8,16},{9,17},{10,... | collective-permute-start | bytes 196616 | tf_op jit(solution)/shard_map/ppermute | solution.py:596
  51.0 10.1 %collective-permute-start.12 = (f32[4,16,256]{2,1,0:T(8,128)S(1)}, f32[4,16,256]{2,1,0:T(8,128)S(1)}, u32[]{:S(2)}, u32[]{:S(2)}) collective-permute-start(f32[4,16,256]{2,1,0:T(8,128)S(1)} %get-tuple-element.55.f2), channel_id=1, source_target_pairs={{0,8},{1,9},{2,10},{3,11},{4,12},{5,13},{6,14},{7,15},{8,0},{9,1},... | collective-permute-start | bytes 196616 | tf_op jit(solution)/shard_map/ppermute | solution.py:596
  54.3 6.8 %collective-permute-start.14 = (f32[1,16,256]{2,1,0:T(8,128)S(1)}, f32[1,16,256]{2,1,0:T(8,128)S(1)}, u32[]{:S(2)}, u32[]{:S(2)}) collective-permute-start(f32[1,16,256]{2,1,0:T(8,128)S(1)} %get-tuple-element.56), channel_id=1, source_target_pairs={{0,1},{1,0},{2,3},{3,2},{4,16},{5,17},{6,18},{7,19},{8,9},{9,8},{1... | collective-permute-start | bytes 49160 | tf_op jit(solution)/shard_map/ppermute | solution.py:596

commit v3 on v2

--- a/solution.py
+++ b/solution.py
@@ -129,49 +129,57 @@
     return i, j, odd_i, odd_j, far_i, far_j
 
 
-def source(dims, vf, mask, ra, rb, rs1, rs2, src, out_a, out_b, H, G):
-    leaves, subs = dims
-    i, j, odd_i, odd_j, far_i, far_j = place(leaves, subs)
+def edges(dims, vf, to_a, to_b, to_1, to_2):
+    _, _, odd_i, odd_j, _, _ = place(*dims)
+    to_a[0] = vf[jnp.where(odd_i, 0, NX - 1)]
+    to_b[0] = vf[jnp.where(odd_i, NX - 1, 0)]
+    for x in range(NX):
+        first, last = vf[x, 0:1, :], vf[x, NY - 1 : NY, :]
+        to_1[x : x + 1, :] = jnp.where(odd_j, first, last)
+        to_2[x : x + 1, :] = jnp.where(odd_j, last, first)
+
+
+def columns(vf, mask, H, G):
     nz = vf.shape[2] // LANES
 
     def level0(x):
         h, before, after = taps(split(vf[x]))
         m = mask[x].astype(f32)
         for k in range(nz):
-            H[x + 1, k] = h[k]
+            H[x, k] = h[k]
             G[x, k] = (after[k] - before[k]) * (0.5 * m[:, k * LANES : (k + 1) * LANES])
 
     each(0, NX, level0, 2)
+
+
+def source(dims, H, G, ra, rb, rs1, rs2, src):
+    _, _, odd_i, odd_j, far_i, far_j = place(*dims)
+    nz = H.shape[1]
     far_x = jnp.where(far_i, 1.0, 0.0).astype(f32)
     far_y = jnp.where(far_j, 1.0, 0.0).astype(f32)
     ha, _, _ = taps(split(ra[0]))
     hb, _, _ = taps(split(rb[0]))
     hs1, _, _ = taps(split(rs1[...]))
     hs2, _, _ = taps(split(rs2[...]))
+    row = rows_of(NY)
     for k in range(nz):
         b = hb[k] * far_x
-        H[0, k] = jnp.where(odd_i, ha[k], b)
-        H[NX + 1, k] = jnp.where(odd_i, b, ha[k])
-    row = rows_of(16)
-    low = [jnp.where(odd_j, hs1[k], hs2[k] * far_y) for k in range(nz)]
-    high = [jnp.where(odd_j, hs2[k] * far_y, hs1[k]) for k in range(nz)]
-
-    for x in range(NX):
-        for k in range(nz):
-            h = H[x + 1, k]
-            up = jnp.where(row == 15, high[k][x : x + 1, :], pltpu.roll(h, 15, 0))
-            down = jnp.where(row == 0, low[k][x : x + 1, :], pltpu.roll(h, 1, 0))
-            ahead, behind = H[x + 2, k], H[x, k]
+        below, above = jnp.where(odd_i, ha[k], b), jnp.where(odd_i, b, ha[k])
+        low = jnp.where(odd_j, hs1[k], hs2[k] * far_y)
+        high = jnp.where(odd_j, hs2[k] * far_y, hs1[k])
+        for x in range(NX):
+            h = H[x, k]
+            up = jnp.where(row == NY - 1, high[x : x + 1, :], pltpu.roll(h, NY - 1, 0))
+            down = jnp.where(row == 0, low[x : x + 1, :], pltpu.roll(h, 1, 0))
+            ahead = H[x + 1, k] if x < NX - 1 else above
+            behind = H[x - 1, k] if x > 0 else below
             sx, sy = 0.5 * (ahead - behind), 0.5 * (up - down)
             bend = ahead - 2.0 * h + behind + (up - 2.0 * h + down)
             inv = lax.rsqrt(1.0 + sx * sx + sy * sy)
             src[x, :, k * LANES : (k + 1) * LANES] = G[x, k] * (bend * (inv * inv * inv))
-    at = jnp.where(odd_i, 0, 4)
-    out_a[...] = src[pl.ds(at, 4)]
-    out_b[...] = src[pl.ds(4 - at, 4)]
-
-
-def descent(dims, src, f1_out, c1_out, c2_out, m2a, m2b, own2, F1c, F0, U0, T0, F1, U1, T1):
+
+
+def descent(dims, src, big, m2a, m2b, own2, F1c, F0, U0, T0, F1, U1, T1):
     leaves, subs = dims
     i, j, odd_i, odd_j, far_i, far_j = place(leaves, subs)
     nz = src.shape[2] // LANES
@@ -198,7 +206,7 @@
         for k in range(nz):
             U0[x, k] = (C1 * f[k] + C2 * around_f[k]) * m
 
-    each(3, 13, smooth0, 2)
+    each(3, 13, smooth0, 5)
 
     for x in range(0, 14):
         if x < 4 or x >= 10:
@@ -219,7 +227,7 @@
             F1[c + 3, k, 2:14, :] = v
             F1[c + 3, k, 14:16, :] = zero[0:2]
 
-    each(1, 7, restrict0)
+    each(1, 7, restrict0, 2)
 
     n1 = nz // 2
     my1 = row_mask(16, j * (NY // 2) - 4, count_y // 2)
@@ -253,24 +261,34 @@
     m2a[...] = F1c[pl.ds(at, 2)]
     m2b[...] = F1c[pl.ds(4 - at, 2)]
     own2[...] = F1c[2:4]
+    big[0:4] = src[pl.ds(at, 4)]
     for p in range(3):
         for k in range(n1):
             for h in (0, 1):
-                f1_out[p, :, (h * n1 + k) * LANES : (h * n1 + k + 1) * LANES] = F1[4 + p + 3 * h, k]
-    odd_c = (i // 2) % 2 == 1
-    first = jnp.where(odd_c, 4, 8)
-    for k in range(n1):
-        for h in (0, 1):
-            s = slice((h * n1 + k) * LANES, (h * n1 + k + 1) * LANES)
-            c1_out[0, :, s] = F1[first + h, k]
-            c2_out[0, :, s] = F1[12 - first + h, k]
-
-
-def sum2(dims, own2, ra, rb, out):
-    far = place(*dims)[4]
-    v = own2[...] + ra[...] + jnp.where(far, rb[...], 0.0)
+                big[4 + p, :, (h * n1 + k) * LANES : (h * n1 + k + 1) * LANES] = F1[4 + p + 3 * h, k]
+
+
+def half_planes(ref, p):
+    n = ref.shape[2] // 2
+    return ref[4 + p % 3, :, (p // 3) * n : (p // 3 + 1) * n]
+
+
+def middle(dims, own2, r2a, r2b, src, big, ra, out, to_b):
+    _, _, odd_i, _, far_i, _ = place(*dims)
+    n = src.shape[2] // 2
+    v = own2[...] + r2a[...] + jnp.where(far_i, r2b[...], 0.0)
     for k in range(out.shape[0]):
         out[k] = v
+    to_b[0:4] = src[pl.ds(jnp.where(odd_i, 4, 0), 4)]
+    more = {
+        0: jnp.where(odd_i, half_planes(ra, 4), 0.0),
+        1: jnp.where(odd_i, half_planes(ra, 5), 0.0),
+        4: jnp.where(odd_i, 0.0, half_planes(ra, 0)),
+        5: jnp.where(odd_i, 0.0, half_planes(ra, 1)),
+    }
+    for p in range(6):
+        v = half_planes(big, p)
+        to_b[4 + p % 3, :, (p // 3) * n : (p // 3 + 1) * n] = v + more[p] if p in more else v
 
 
 def chip2(dims, got, f2, edge, out, F2, U2, T2):
@@ -318,27 +336,19 @@
                 out[t, q, :, k * LANES : (k + 1) * LANES] = v
 
 
-def rows_out(dims, src, f1, ra, rb, r1a, r1b, rc1, rc2, f1x, s1, s2):
-    leaves, subs = dims
-    i, j, odd_i, odd_j, far_i, far_j = place(leaves, subs)
-    odd_c = (i // 2) % 2 == 1
-    chips = leaves // 2
-    c = i // 2
-    far_c = jnp.where(odd_c, c < chips - 1, c > 0)
+def rows_out(dims, src, big, ra, rb, far, f1x, s1, s2):
+    _, _, odd_i, odd_j, far_i, _ = place(*dims)
+    i = lax.axis_index("leaf")
     n = src.shape[2] // 2
-
-    def halves(ref, p):
-        return ref[p % 3, :, (p // 3) * n : (p // 3 + 1) * n]
-
-    a = [halves(r1a, p) for p in range(6)]
-    b = [jnp.where(far_i, halves(r1b, p), 0.0) for p in range(6)]
+    a = [half_planes(ra, p) for p in range(6)]
+    b = [jnp.where(far_i, half_planes(rb, p), 0.0) for p in range(6)]
     before = [jnp.where(odd_i, a[p], b[p]) for p in range(6)]
     after = [jnp.where(odd_i, b[p], a[p]) for p in range(6)]
-    d1 = [rc1[0, :, h * n : (h + 1) * n] for h in (0, 1)]
-    d2 = [jnp.where(far_c, rc2[0, :, h * n : (h + 1) * n], 0.0) for h in (0, 1)]
-    before2 = [jnp.where(odd_c, d1[h], d2[h]) for h in (0, 1)]
-    after2 = [jnp.where(odd_c, d2[h], d1[h]) for h in (0, 1)]
-    own = [halves(f1, p) for p in range(6)]
+    far_two = jnp.where(odd_i, i > 1, i < dims[0] - 2)
+    d = [jnp.where(far_two, far[p % 3, :, (p // 3) * n : (p // 3 + 1) * n], 0.0) for p in (0, 1, 4, 5)]
+    before2 = [jnp.where(odd_i, d[2 + h], 0.0) for h in (0, 1)]
+    after2 = [jnp.where(odd_i, 0.0, d[h]) for h in (0, 1)]
+    own = [half_planes(big, p) for p in range(6)]
     planes = {}
 
     def add(x, v):
@@ -410,11 +420,77 @@
             out[x, :, k * LANES : (k + 1) * LANES] = V3[i + x, k]
 
 
-def ascent(dims, u3, f2, r2c1, r2c2, r2e, src, ra, rb, f1x, rs1, rs2, press, resid, F2, T2, W2, X2, T1, F1, V1, X1, T0, F0, V0, X0):
+def ready(dims, src, ra, rb, f1x, rs1, rs2, F0, P0, F1, P1):
     leaves, subs = dims
     i, j, odd_i, odd_j, far_i, far_j = place(leaves, subs)
     count_x, count_y = leaves * NX, subs * NY
     nz = src.shape[2] // LANES
+    n1 = nz // 2
+    zero = jnp.zeros((24, LANES), f32)
+    far_x = jnp.where(far_i, 1.0, 0.0).astype(f32)
+
+    low_j = jnp.where(j > 0, 1.0, 0.0).astype(f32)
+    high_j = jnp.where(j < subs - 1, 1.0, 0.0).astype(f32)
+
+    def fill1(x):
+        part, at = x // 7, 8 + x % 7
+        for k in range(n1):
+            s = slice(k * LANES, (k + 1) * LANES)
+            F1[x, k] = zero
+            F1[x, k, 4:20, :] = f1x[x, :, s]
+            s = slice((part * n1 + k) * LANES, (part * n1 + k + 1) * LANES)
+            lo = jnp.where(odd_j, rs1[at, :, s], rs2[at, :, s]) * low_j
+            hi = jnp.where(odd_j, rs2[at, :, s], rs1[at, :, s]) * high_j
+            F1[x, k, 1:9, :] = F1[x, k, 1:9, :] + lo
+            F1[x, k, 15:23, :] = F1[x, k, 15:23, :] + hi
+
+    for x in range(14):
+        fill1(x)
+    my1 = row_mask(24, j * (NY // 2) - 8, count_y // 2)
+
+    def smooth1(x):
+        m = plane_mask(my1, i * (NX // 2) + x - 5, count_x // 2)
+        f, around_f = around(F1, x)
+        for k in range(n1):
+            P1[x, k] = (C1 * f[k] + C2 * around_f[k]) * m
+
+    each(1, 13, smooth1, 4)
+
+    def fill0(x):
+        if 4 <= x < 12:
+            v = src[x - 4]
+        elif x < 4:
+            v = jnp.where(odd_i, ra[x], rb[x] * far_x)
+        else:
+            v = jnp.where(odd_i, rb[x - 12] * far_x, ra[x - 12])
+        a, b = rs1[x % 8], rs2[x % 8]
+        h = 4 * (x // 8)
+        lo = jnp.where(odd_j, a[h : h + 4], b[h : h + 4]) * low_j
+        hi = jnp.where(odd_j, b[h : h + 4], a[h : h + 4]) * high_j
+        for k in range(nz):
+            s = slice(k * LANES, (k + 1) * LANES)
+            F0[x, k, 0:4, :] = lo[:, s]
+            F0[x, k, 4:20, :] = v[:, s]
+            F0[x, k, 20:24, :] = hi[:, s]
+
+    for x in range(16):
+        fill0(x)
+    my0 = row_mask(24, j * NY - 4, count_y)
+
+    def smooth0(x):
+        m = plane_mask(my0, i * NX + x - 4, count_x)
+        f, around_f = around(F0, x)
+        for k in range(nz):
+            P0[x, k] = (C1 * f[k] + C2 * around_f[k]) * m
+
+    each(1, 15, smooth0, 4)
+
+
+def ascent(dims, u3, f2, r2c1, r2c2, r2e, F0, P0, F1, P1, press, resid, F2, T2, W2, X2, T1, V1, X1, T0, V0, X0):
+    leaves, subs = dims
+    i, j, odd_i, odd_j, far_i, far_j = place(leaves, subs)
+    count_x, count_y = leaves * NX, subs * NY
+    nz = F0.shape[1]
     n1, n2, n3 = nz // 2, nz // 4, nz // 8
     zero = jnp.zeros((24, LANES), f32)
 
@@ -455,23 +531,6 @@
     for c in range(6):
         for k in range(n1):
             T1[c, k] = zero
-    low_j = jnp.where(j > 0, 1.0, 0.0).astype(f32)
-    high_j = jnp.where(j < subs - 1, 1.0, 0.0).astype(f32)
-
-    def fill1(x):
-        part, at = x // 7, 8 + x % 7
-        for k in range(n1):
-            s = slice(k * LANES, (k + 1) * LANES)
-            F1[x, k] = zero
-            F1[x, k, 4:20, :] = f1x[x, :, s]
-            s = slice((part * n1 + k) * LANES, (part * n1 + k + 1) * LANES)
-            lo = jnp.where(odd_j, rs1[at, :, s], rs2[at, :, s]) * low_j
-            hi = jnp.where(odd_j, rs2[at, :, s], rs1[at, :, s]) * high_j
-            F1[x, k, 1:9, :] = F1[x, k, 1:9, :] + lo
-            F1[x, k, 15:23, :] = F1[x, k, 15:23, :] + hi
-
-    for x in range(14):
-        fill1(x)
     my1 = row_mask(24, j * (NY // 2) - 8, count_y // 2)
 
     for c in range(6):
@@ -481,9 +540,8 @@
         for p in (0, 1):
             x = 2 * c + p + 1
             m = plane_mask(my1, i * (NX // 2) + x - 5, count_x // 2)
-            f, around_f = around(F1, x)
             for k in range(n1):
-                V1[x, k] = (C1 * f[k] + C2 * around_f[k] + T1[c, k]) * m
+                V1[x, k] = P1[x, k] + T1[c, k] * m
 
     def sweep1(old, new, lo, hi):
         def body(x):
@@ -492,32 +550,12 @@
             for k in range(n1):
                 new[x, k] = (C0 * u[k] + D * (F1[x, k] + around_u[k])) * m
 
-        each(lo, hi, body, 2)
+        each(lo, hi, body, 4)
 
     sweep1(V1, X1, 2, 12)
     sweep1(X1, V1, 3, 11)
 
-    far_x = jnp.where(far_i, 1.0, 0.0).astype(f32)
-
-    def fill0(x):
-        if 4 <= x < 12:
-            v = src[x - 4]
-        elif x < 4:
-            v = jnp.where(odd_i, ra[x], rb[x] * far_x)
-        else:
-            v = jnp.where(odd_i, rb[x - 12] * far_x, ra[x - 12])
-        a, b = rs1[x % 8], rs2[x % 8]
-        h = 4 * (x // 8)
-        lo = jnp.where(odd_j, a[h : h + 4], b[h : h + 4]) * low_j
-        hi = jnp.where(odd_j, b[h : h + 4], a[h : h + 4]) * high_j
-        for k in range(nz):
-            s = slice(k * LANES, (k + 1) * LANES)
-            F0[x, k, 0:4, :] = lo[:, s]
-            F0[x, k, 4:20, :] = v[:, s]
-            F0[x, k, 20:24, :] = hi[:, s]
-
-    for x in range(16):
-        fill0(x)
+
     my0 = row_mask(24, j * NY - 4, count_y)
 
     def start0(c):
@@ -527,11 +565,10 @@
 
     def smooth0(x):
         m = plane_mask(my0, i * NX + x - 4, count_x)
-        f, around_f = around(F0, x)
-        for k in range(nz):
-            V0[x, k] = (C1 * f[k] + C2 * around_f[k] + T0[x // 2, k]) * m
-
-    each(1, 15, smooth0, 2)
+        for k in range(nz):
+            V0[x, k] = P0[x, k] + T0[x // 2, k] * m
+
+    each(1, 15, smooth0, 4)
 
     def sweep0(old, new, lo, hi):
         def body(x):
@@ -540,7 +577,7 @@
             for k in range(nz):
                 new[x, k] = (C0 * u[k] + D * (F0[x, k] + around_u[k])) * m
 
-        each(lo, hi, body, 2)
+        each(lo, hi, body, 4)
 
     sweep0(V0, X0, 2, 14)
     sweep0(X0, V0, 3, 13)
@@ -552,15 +589,16 @@
             press[x, :, s] = u[k][4:20]
             resid[x, :, s] = (F0[x + 4, k] - 6.0 * u[k] + around_u[k])[4:20]
 
-    each(0, NX, finish, 2)
-
-
-def call(kernel, outs, scratch, *args):
+    each(0, NX, finish, 4)
+
+
+def call(kernel, outs, scratch, *args, us=1.0):
     return pl.pallas_call(
         kernel,
         out_shape=[jax.ShapeDtypeStruct(s, f32) for s in outs],
         scratch_shapes=[pltpu.VMEM(s, f32) for s in scratch],
-        compiler_params=pltpu.CompilerParams(vmem_limit_bytes=48 * 1024 * 1024),
+        compiler_params=pltpu.CompilerParams(vmem_limit_bytes=20 * 1024 * 1024),
+        cost_estimate=pl.CostEstimate(flops=0, transcendentals=0, bytes_accessed=int(us * 3.6e6)),
     )(*args)
 
 
@@ -579,12 +617,13 @@
     s1 = table(lambda i, j: (i, j ^ 1))
     s2 = table(lambda i, j: (i, odd(j)) if inner(odd(j), subs) else (i ^ 1, j))
     c1 = table(lambda i, j: (i ^ 2, j))
-    c2 = table(lambda i, j: (2 * odd(i // 2) + i % 2, j) if inner(odd(i // 2), leaves // 2) else (i, j ^ 1))
+    c2 = table(lambda i, j: (2 * odd(i // 2) + i % 2, j) if inner(odd(i // 2), leaves // 2) else (i ^ 1, j))
+
     def two_on(i):
         t = 2 * (i // 2 + (2 if i % 2 else -2)) + 1 - i % 2
         return t if inner(t, leaves) else None
 
-    e = table(lambda i, j: (two_on(i), j) if two_on(i) is not None else (i, j ^ 1))
+    e = table(lambda i, j: (two_on(i), j) if two_on(i) is not None else (i ^ 2, j))
     return a, b, s1, s2, c1, c2, e
 
 
@@ -594,32 +633,17 @@
     nz = depth // LANES
     pa, pb, ps1, ps2, pc1, pc2, pe = swaps(leaves, subs)
     move = lambda v, table: lax.ppermute(v, AXES, table)
-    i, j = lax.axis_index("leaf"), lax.axis_index("sub")
-    odd_i, odd_j = i % 2, j % 2
-
-    vf = volume_fraction
-    at_x, at_y = (1 - odd_i) * (NX - 1), (1 - odd_j) * (NY - 1)
-    plane = lambda x: lax.dynamic_slice_in_dim(vf, x, 1, 0)
-    rows = lambda y: lax.dynamic_slice_in_dim(vf, y, 1, 1).reshape(NX, depth)
-    ha, hb = move(plane(at_x), pa), move(plane(NX - 1 - at_x), pb)
-    hs1, hs2 = move(rows(at_y), ps1), move(rows(NY - 1 - at_y), ps2)
-
     n1, n2, n3 = nz // 2, nz // 4, nz // 8
-    src, out_a, out_b = call(
-        functools.partial(source, dims),
-        [(NX, NY, depth), (4, NY, depth), (4, NY, depth)],
-        [(NX + 2, nz, 16, LANES), (NX, nz, 16, LANES)],
-        vf,
-        interface_mask,
-        ha,
-        hb,
-        hs1,
-        hs2,
-    )
-    ra, rb = move(out_a, pa), move(out_b, pb)
-    f1, m1, m2, m2a, m2b, own2 = call(
+
+    plane, rows = (1, NY, depth), (NX, depth)
+    to_a, to_b, to_1, to_2 = call(functools.partial(edges, dims), [plane, plane, rows, rows], [], volume_fraction)
+    halos = move(to_a, pa), move(to_b, pb), move(to_1, ps1), move(to_2, ps2)
+    shape = (NX, nz, NY, LANES)
+    heights, slope = call(columns, [shape, shape], [], volume_fraction, interface_mask)
+    (src,) = call(functools.partial(source, dims), [(NX, NY, depth)], [], heights, slope, *halos)
+    big, m2a, m2b, own2 = call(
         functools.partial(descent, dims),
-        [(3, 16, depth), (1, 16, depth), (1, 16, depth)] + [(2, 8, depth // 4)] * 3,
+        [(7, NY, depth)] + [(2, 8, depth // 4)] * 3,
         [
             (6, 8, depth // 4),
             (16, nz, 24, LANES),
@@ -631,27 +655,15 @@
         ],
         src,
     )
-    r2a, r2b = move(m2a, pa), move(m2b, pb)
-    (out,) = call(functools.partial(sum2, dims), [(2 * subs, 2, 8, depth // 4)], [], own2, r2a, r2b)
-    out, g1, m1, m2 = lax.optimization_barrier((out, f1, m1, m2))
-    r1a, r1b = move(g1, pa), move(g1, pb)
-    rc1, rc2 = move(m1, pc1), move(m2, pc2)
+    r2a, r2b, ra = move(m2a, pa), move(m2b, pb), move(big, pa)
+    out, to_b = call(
+        functools.partial(middle, dims), [(2 * subs, 2, 8, depth // 4), (7, NY, depth)], [], own2, r2a, r2b, src, big, ra
+    )
+    rb = move(to_b, pb)
     group = [list(range(k, k + 2 * subs)) for k in range(0, leaves * subs, 2 * subs)]
     got = lax.all_to_all(out, AXES, 0, 0, axis_index_groups=group)
-    got, r1a, r1b, rc1, rc2 = lax.optimization_barrier((got, r1a, r1b, rc1, rc2))
-    f1x, s1, s2 = call(
-        functools.partial(rows_out, dims),
-        [(14, 16, depth // 2), (15, 8, depth), (15, 8, depth)],
-        [],
-        src,
-        f1,
-        ra,
-        rb,
-        r1a,
-        r1b,
-        rc1,
-        rc2,
-    )
+    got, rb = lax.optimization_barrier((got, rb))
+    far = move(rb[4:7], pa)
     chips = leaves // 2
     f2, edge, out = call(
         functools.partial(chip2, dims),
@@ -659,14 +671,26 @@
         [(10, n2, 16, LANES), (10, n2, 16, LANES), (4, n2, 16, LANES)],
         got,
     )
-    out, s1, s2, g2, edge = lax.optimization_barrier((out, s1, s2, f2, edge))
+    f1x, s1, s2 = call(
+        functools.partial(rows_out, dims),
+        [(14, 16, depth // 2), (15, 8, depth), (15, 8, depth)],
+        [],
+        src,
+        big,
+        ra,
+        rb,
+        far,
+    )
+    out, s1, s2 = lax.optimization_barrier((out, s1, s2))
     rs1, rs2 = move(s1, ps1), move(s2, ps2)
-    r2c1, r2c2, r2e = move(g2, pc1), move(g2, pc2), move(edge, pe)
     group = [[(2 * c + k) * subs + s for c in range(chips)] for k in (0, 1) for s in range(subs)]
     got = lax.all_to_all(out, AXES, 0, 0, axis_index_groups=group)
+    r2c1, r2c2, r2e = move(f2, pc1), move(f2, pc2), move(edge, pe)
     (u3,) = call(
         functools.partial(coarsest, dims), [(5, 8, depth // 8)], [(leaves + 4, n3, 8, LANES)] * 3, got
     )
+    shape0, shape1 = (16, nz, 24, LANES), (14, n1, 24, LANES)
+    F0, P0, F1, P1 = call(functools.partial(ready, dims), [shape0, shape0, shape1, shape1], [], src, ra, rb, f1x, rs1, rs2)
     return call(
         functools.partial(ascent, dims),
         [(NX, NY, depth), (NX, NY, depth)],
@@ -676,25 +700,21 @@
             (10, n2, 16, LANES),
             (10, n2, 16, LANES),
             (6, n1, 24, LANES),
-            (14, n1, 24, LANES),
-            (14, n1, 24, LANES),
-            (14, n1, 24, LANES),
+            shape1,
+            shape1,
             (8, nz, 24, LANES),
-            (16, nz, 24, LANES),
-            (16, nz, 24, LANES),
-            (16, nz, 24, LANES),
+            shape0,
+            shape0,
         ],
         u3,
         f2,
         r2c1,
         r2c2,
         r2e,
-        src,
-        ra,
-        rb,
-        f1x,
-        rs1,
-        rs2,
+        F0,
+        P0,
+        F1,
+        P1,
     )
 
 

time: 69.4 us -> 61.6 us (0.89)
  starting transfers between devices: 31.6 us -> 20.9 us
  blocking collectives: 0 us -> 10.6 us
  waiting for transfers between devices: 15.2 us -> 10.3 us
  Pallas kernels: 17.9 us -> 16.5 us
  local copies, waits for them, and re-layouts: 3.07 us -> 2.09 us
    all_to_all x0 -> x1, blocking collectives: none -> 10.6 us  [shards(): got = lax.all_to_all(out, AXES, 0, 0, axis_index_groups=group)]
    ppermute x17 -> x14, starting transfers between devices: 15.5 us -> 9.34 us  [shards(): move = lambda v, table: lax.ppermute(v, AXES, table)]
    ppermute x17 -> x14, waiting for transfers between devices: 9.52 us -> 4.13 us  [shards(): move = lambda v, table: lax.ppermute(v, AXES, table)]
    all_to_all x2 -> x1, starting transfers between devices: 16.1 us -> 11.6 us  [shards(): got = lax.all_to_all(out, AXES, 0, 0, axis_index_groups=group)]
    dynamic_slice x2 -> x0, local copies, waits for them, and re-layouts: 2.02 us -> none  [the longest x1 1.08 us: shards(): rows = lambda y: lax.dynamic_slice_in_dim(vf, y, 1, 1).reshape(NX, depth)]
    pallas_call x7 -> x10, Pallas kernels: 17.9 us -> 16.5 us  [call(): pl.pallas_call(kernel, out_shape=[jax.ShapeDtypeStruct(s, f32) for s in o...]
    unnamed x6 -> x4, local copies, waits for them, and re-layouts: 1.06 us -> 2.08 us
    all_to_all x2 -> x1, waiting for transfers between devices: 5.72 us -> 6.15 us  [shards(): got = lax.all_to_all(out, AXES, 0, 0, axis_index_groups=group)]
  transfers between devices with their start and end apart: 19 -> 15, of which waited for: 7 -> 5; matrix products, arithmetic and copies ran while one was open for 2% -> 0% of each run, Pallas kernels for 11% -> 9%
where the time goes in v3:
time: 61.6 us; the launch traced here: 61.2 us
  starting transfers between devices  20.9 us (34%)
  Pallas kernels  16.5 us (27%)
  blocking collectives  10.6 us (17%)
  waiting for transfers between devices  10.3 us (17%)
  local copies, waits for them, and re-layouts  2.09 us (3%)
  between operations  0.79 us (1%)
    pallas_call x10, Pallas kernels, call(): pl.pallas_call(kernel, out_shape=[jax.ShapeDtypeStruct(s, f32) for s in o...  16.5 us
    all_to_all x1, starting transfers between devices, shards(): got = lax.all_to_all(out, AXES, 0, 0, axis_index_groups=group)  11.6 us
    all_to_all x1, blocking collectives, shards(): got = lax.all_to_all(out, AXES, 0, 0, axis_index_groups=group)  10.6 us
    ppermute x14, starting transfers between devices, shards(): move = lambda v, table: lax.ppermute(v, AXES, table)  9.34 us
    all_to_all x1, waiting for transfers between devices, shards(): got = lax.all_to_all(out, AXES, 0, 0, axis_index_groups=group)  6.15 us
    ppermute x14, waiting for transfers between devices, shards(): move = lambda v, table: lax.ppermute(v, AXES, table)  4.13 us
    unnamed x4, local copies, waits for them, and re-layouts  2.08 us
  transfers between devices with their start and end apart: 15, of which 5 were waited for; matrix products, arithmetic and copies ran while one was open for 0% of the time, Pallas kernels for 9%

profile of v3, /device:TPU:2, one launch (start us, length us, event | category | flops | bytes accessed | tf_op | source)
XLA Modules:
  0.0 61.2 jit_solution(11090154539555520776)
XLA Ops:
  0.6 0.0 copy-start
  0.6 1.0 %copy-done = f32[8,16,1024]{2,1,0:T(8,128)S(1)} copy-done((f32[8,16,1024]{2,1,0:T(8,128)S(1)}, f32[8,16,1024]{2,1,0:T(8,128)}, u32[]{:S(2)}) %copy-start) | copy-done | bytes 524312
  1.7 0.1 collective-permute-start
  1.8 0.5 collective-permute-start.1
  2.3 1.6 %collective-permute-start.2 = (f32[8,1024]{1,0:T(8,128)S(1)}, f32[8,1024]{1,0:T(8,128)S(1)}, u32[]{:S(2)}, u32[]{:S(2)}) collective-permute-start(f32[8,1024]{1,0:T(8,128)S(1)} %get-tuple-element.33), channel_id=1, source_target_pairs={{0,1},{1,0},{2,3},{3,2},{4,5},{5,4},{6,7},{7,6},{8,9},{9,8},{10,11... | collective-permute-start | bytes 98312 | tf_op jit(solution)/shard_map/ppermute | solution.py:635
  3.9 1.5 %collective-permute-start.3 = (f32[8,1024]{1,0:T(8,128)S(1)}, f32[8,1024]{1,0:T(8,128)S(1)}, u32[]{:S(2)}, u32[]{:S(2)}) collective-permute-start(f32[8,1024]{1,0:T(8,128)S(1)} %get-tuple-element.34), channel_id=1, source_target_pairs={{0,4},{1,2},{2,1},{3,7},{4,0},{5,6},{6,5},{7,3},{8,12},{9,10},{10,... | collective-permute-start | bytes 98312 | tf_op jit(solution)/shard_map/ppermute | solution.py:635
  5.4 0.0 copy-start.1
  5.4 1.0 %copy-done.1 = s32[8,16,1024]{2,1,0:T(8,128)S(1)} copy-done((s32[8,16,1024]{2,1,0:T(8,128)S(1)}, s32[8,16,1024]{2,1,0:T(8,128)}, u32[]{:S(2)}) %copy-start.1) | copy-done | bytes 524312
  6.4 1.2 %shard_map.41 = (f32[8,8,16,128]{3,2,1,0:T(8,128)S(1)}, f32[8,8,16,128]{3,2,1,0:T(8,128)S(1)}) custom-call(f32[8,16,1024]{2,1,0:T(8,128)S(1)} %copy-done, s32[8,16,1024]{2,1,0:T(8,128)S(1)} %copy-done.1), custom_call_target="tpu_custom_call" | custom-call | bytes 3600000 | tf_op jit(solution)/shard_map/pallas_call | solution.py:596
  7.6 0.0 collective-permute-done.2.rs1
  7.6 0.2 collective-permute-done.3.rs2
  7.8 0.0 collective-permute-done.ra
  7.8 0.0 collective-permute-done.1.rb
  7.8 0.8 %shard_map.43.src = f32[8,16,1024]{2,1,0:T(8,128)S(1)} custom-call(f32[8,8,16,128]{3,2,1,0:T(8,128)S(1)} %get-tuple-element.29.H, f32[8,8,16,128]{3,2,1,0:T(8,128)S(1)} %get-tuple-element.30.G, f32[1,16,1024]{2,1,0:T(8,128)S(1)} %collective-permute-done.ra, f32[1,16,1024]{2,1,0:T(8,128)S(1)} %collective-permute-done.1.rb, ...), custom_call_target="tpu_custom_call" | custom-call | bytes 3600000 | tf_op jit(solution)/shard_map/pallas_call | solution.py:596
  8.6 3.6 %shard_map.44 = (f32[7,16,1024]{2,1,0:T(8,128)S(1)}, f32[2,8,256]{2,1,0:T(8,128)S(1)}, f32[2,8,256]{2,1,0:T(8,128)S(1)}, f32[2,8,256]{2,1,0:T(8,128)S(1)}) custom-call(f32[8,16,1024]{2,1,0:T(8,128)S(1)} %shard_map.43.src), custom_call_target="tpu_custom_call" | custom-call | bytes 3600000 | tf_op jit(solution)/shard_map/pallas_call | solution.py:596
  12.3 0.2 collective-permute-start.6
  12.5 0.4 collective-permute-start.4
  12.9 0.0 collective-permute-start.5
  12.9 1.3 %collective-permute-done.4.r2a = f32[2,8,256]{2,1,0:T(8,128)S(1)} collective-permute-done((f32[2,8,256]{2,1,0:T(8,128)S(1)}, f32[2,8,256]{2,1,0:T(8,128)S(1)}, u32[]{:S(2)}, u32[]{:S(2)}) %collective-permute-start.4) | collective-permute-done | bytes 16416 | tf_op jit(solution)/shard_map/ppermute | solution.py:635
  14.2 2.4 %collective-permute-done.5.r2b = f32[2,8,256]{2,1,0:T(8,128)S(1)} collective-permute-done((f32[2,8,256]{2,1,0:T(8,128)S(1)}, f32[2,8,256]{2,1,0:T(8,128)S(1)}, u32[]{:S(2)}, u32[]{:S(2)}) %collective-permute-start.5) | collective-permute-done | bytes 16416 | tf_op jit(solution)/shard_map/ppermute | solution.py:635
  16.6 0.0 collective-permute-done.6.ra
  16.6 0.1 shard_map.45
  16.7 0.1 collective-permute-start.7
  16.8 10.6 %all_to_all.10.got = f32[8,2,8,256]{3,2,1,0:T(8,128)S(1)} all-to-all(f32[8,2,8,256]{3,2,1,0:T(8,128)S(1)} %get-tuple-element.39), channel_id=1, replica_groups={{0,1,2,3,4,5,6,7},{8,9,10,11,12,13,14,15},{16,17,18,19,20,21,22,23},{24..., dimensions={0} | all-to-all | bytes 262144 | tf_op jit(solution)/shard_map/all_to_all | solution.py:664
  27.4 0.0 collective-permute-done.7.rb
  27.4 0.2 collective-permute-start.8
  27.6 1.1 %shard_map.46 = (f32[4,16,256]{2,1,0:T(8,128)S(1)}, f32[1,16,256]{2,1,0:T(8,128)S(1)}, f32[16,4,8,128]{3,2,1,0:T(8,128)}) custom-call(f32[8,2,8,256]{3,2,1,0:T(8,128)S(1)} %all_to_all.10.got), custom_call_target="tpu_custom_call" | custom-call | bytes 3600000 | tf_op jit(solution)/shard_map/pallas_call | solution.py:596
  28.7 0.2 collective-permute-done.8.far
  28.9 1.2 %shard_map.47 = (f32[14,16,512]{2,1,0:T(8,128)S(1)}, f32[15,8,1024]{2,1,0:T(8,128)}, f32[15,8,1024]{2,1,0:T(8,128)}) custom-call(f32[8,16,1024]{2,1,0:T(8,128)S(1)} %shard_map.43.src, f32[7,16,1024]{2,1,0:T(8,128)S(1)} %get-tuple-element.38.big, f32[7,16,1024]{2,1,0:T(8,128)S(1)} %collective-permute-done.6.ra, f32[7,16,1024]{2,1,0:T(8,128)S(1)} %collective-permute-done.7.rb, ...), custom_call_target="tpu_custom_call" | custom-call | bytes 3600000 | tf_op jit(solution)/shard_map/pallas_call | solution.py:596
  30.1 0.3 collective-permute-start.12
  30.4 1.1 %collective-permute-start.13 = (f32[15,8,1024]{2,1,0:T(8,128)}, f32[15,8,1024]{2,1,0:T(8,128)S(1)}, u32[]{:S(2)}, u32[]{:S(2)}) collective-permute-start(f32[15,8,1024]{2,1,0:T(8,128)} %get-tuple-element.51), channel_id=1, source_target_pairs={{0,4},{1,2},{2,1},{3,7},{4,0},{5,6},{6,5},{7,3},{8,12},{9,10},{10,... | collective-permute-start | bytes 1474568 | tf_op jit(solution)/shard_map/ppermute | solution.py:635
  31.5 11.6 %all-to-all-start.1 = ((f32[16,4,8,128]{3,2,1,0:T(8,128)}), f32[16,4,8,128]{3,2,1,0:T(8,128)S(1)}, u32[]{:S(2)}, u32[]{:S(2)}) async-start(f32[16,4,8,128]{3,2,1,0:T(8,128)} %get-tuple-element.46), calls=%async_computation.1 | async-start | bytes 524288 | tf_op jit(solution)/shard_map/all_to_all | solution.py:687
  43.1 0.1 collective-permute-start.10
  43.2 3.3 %collective-permute-start.9 = (f32[4,16,256]{2,1,0:T(8,128)S(1)}, f32[4,16,256]{2,1,0:T(8,128)S(1)}, u32[]{:S(2)}, u32[]{:S(2)}) collective-permute-start(f32[4,16,256]{2,1,0:T(8,128)S(1)} %get-tuple-element.47.f2), channel_id=1, source_target_pairs={{0,8},{1,9},{2,10},{3,11},{4,12},{5,13},{6,14},{7,15},{8,0},{9,1},... | collective-permute-start | bytes 196616 | tf_op jit(solution)/shard_map/ppermute | solution.py:635
  46.5 0.0 collective-permute-start.11
  46.5 6.1 %all-to-all-done.1.got = f32[16,4,8,128]{3,2,1,0:T(8,128)S(1)} async-done(((f32[16,4,8,128]{3,2,1,0:T(8,128)}), f32[16,4,8,128]{3,2,1,0:T(8,128)S(1)}, u32[]{:S(2)}, u32[]{:S(2)}) %all-to-all-start.1) | async-done | bytes 262176 | tf_op jit(solution)/shard_map/all_to_all | solution.py:687
  52.7 1.5 %shard_map.48.u3 = f32[5,8,128]{2,1,0:T(8,128)S(1)} custom-call(f32[16,4,8,128]{3,2,1,0:T(8,128)S(1)} %all-to-all-done.1.got), custom_call_target="tpu_custom_call" | custom-call | bytes 3600000 | tf_op jit(solution)/shard_map/pallas_call | solution.py:596
  54.2 0.0 collective-permute-done.12.rs1
  54.2 0.0 collective-permute-done.13.rs2
  54.2 1.9 %shard_map.49 = (f32[16,8,24,128]{3,2,1,0:T(8,128)S(1)}, f32[16,8,24,128]{3,2,1,0:T(8,128)S(1)}, f32[14,4,24,128]{3,2,1,0:T(8,128)S(1)}, f32[14,4,24,128]{3,2,1,0:T(8,128)S(1)}) custom-call(f32[8,16,1024]{2,1,0:T(8,128)S(1)} %shard_map.43.src, f32[7,16,1024]{2,1,0:T(8,128)S(1)} %collective-permute-done.6.ra, f32[7,16,1024]{2,1,0:T(8,128)S(1)} %collective-permute-done.7.rb, ...), custom_call_target="tpu_custom_call" | custom-call | bytes 3600000 | tf_op jit(solution)/shard_map/pallas_call | solution.py:596
  56.1 0.0 collective-permute-done.11.r2e
  56.1 0.0 collective-permute-done.10.r2c2
  56.1 0.0 collective-permute-done.9.r2c1
  56.1 5.1 %shard_map.50 = (f32[8,16,1024]{2,1,0:T(8,128)}, f32[8,16,1024]{2,1,0:T(8,128)}) custom-call(f32[5,8,128]{2,1,0:T(8,128)S(1)} %shard_map.48.u3, f32[4,16,256]{2,1,0:T(8,128)S(1)} %get-tuple-element.47.f2, f32[4,16,256]{2,1,0:T(8,128)S(1)} %collective-permute-done.9.r2c1, f32[4,16,256]{2,1,0:T(8,128)S(1)} %collective-permute-done.10.r2c2, ...), custom_call_target="tpu_custom_call" | custom-call | bytes 3600000 | tf_op jit(solution)/shard_map/pallas_call | solution.py:596
  (2 shorter events, 0.0 us)
Async XLA Ops:
  0.6 1.0 %copy-start = (f32[8,16,1024]{2,1,0:T(8,128)S(1)}, f32[8,16,1024]{2,1,0:T(8,128)}, u32[]{:S(2)}) copy-start(f32[8,16,1024]{2,1,0:T(8,128)} %vf.3) | copy-start | bytes 1572868
  1.7 6.1 %collective-permute-start = (f32[1,16,1024]{2,1,0:T(8,128)S(1)}, f32[1,16,1024]{2,1,0:T(8,128)S(1)}, u32[]{:S(2)}, u32[]{:S(2)}) collective-permute-start(f32[1,16,1024]{2,1,0:T(8,128)S(1)} %get-tuple-element.31), channel_id=1, source_target_pairs={{0,4},{1,5},{2,6},{3,7},{4,0},{5,1},{6,2},{7,3},{8,12},{9,13},{10,... | collective-permute-start | bytes 196616 | tf_op jit(solution)/shard_map/ppermute | solution.py:635
  1.8 6.0 %collective-permute-start.1 = (f32[1,16,1024]{2,1,0:T(8,128)S(1)}, f32[1,16,1024]{2,1,0:T(8,128)S(1)}, u32[]{:S(2)}, u32[]{:S(2)}) collective-permute-start(f32[1,16,1024]{2,1,0:T(8,128)S(1)} %get-tuple-element.32), channel_id=1, source_target_pairs={{0,1},{1,0},{2,3},{3,2},{4,8},{5,9},{6,10},{7,11},{8,4},{9,5},{10,... | collective-permute-start | bytes 196616 | tf_op jit(solution)/shard_map/ppermute | solution.py:635
  2.3 5.3 %collective-permute-start.2 = (f32[8,1024]{1,0:T(8,128)S(1)}, f32[8,1024]{1,0:T(8,128)S(1)}, u32[]{:S(2)}, u32[]{:S(2)}) collective-permute-start(f32[8,1024]{1,0:T(8,128)S(1)} %get-tuple-element.33), channel_id=1, source_target_pairs={{0,1},{1,0},{2,3},{3,2},{4,5},{5,4},{6,7},{7,6},{8,9},{9,8},{10,11... | collective-permute-start | bytes 98312 | tf_op jit(solution)/shard_map/ppermute | solution.py:635
  3.9 3.9 %collective-permute-start.3 = (f32[8,1024]{1,0:T(8,128)S(1)}, f32[8,1024]{1,0:T(8,128)S(1)}, u32[]{:S(2)}, u32[]{:S(2)}) collective-permute-start(f32[8,1024]{1,0:T(8,128)S(1)} %get-tuple-element.34), channel_id=1, source_target_pairs={{0,4},{1,2},{2,1},{3,7},{4,0},{5,6},{6,5},{7,3},{8,12},{9,10},{10,... | collective-permute-start | bytes 98312 | tf_op jit(solution)/shard_map/ppermute | solution.py:635
  5.4 1.0 %copy-start.1 = (s32[8,16,1024]{2,1,0:T(8,128)S(1)}, s32[8,16,1024]{2,1,0:T(8,128)}, u32[]{:S(2)}) copy-start(s32[8,16,1024]{2,1,0:T(8,128)} %mask.1) | copy-start | bytes 1572868
  12.3 4.3 %collective-permute-start.6 = (f32[7,16,1024]{2,1,0:T(8,128)S(1)}, f32[7,16,1024]{2,1,0:T(8,128)S(1)}, u32[]{:S(2)}, u32[]{:S(2)}) collective-permute-start(f32[7,16,1024]{2,1,0:T(8,128)S(1)} %get-tuple-element.38.big), channel_id=1, source_target_pairs={{0,4},{1,5},{2,6},{3,7},{4,0},{5,1},{6,2},{7,3},{8,12},{9,13},{10,... | collective-permute-start | bytes 1376264 | tf_op jit(solution)/shard_map/ppermute | solution.py:635
  12.5 1.7 %collective-permute-start.4 = (f32[2,8,256]{2,1,0:T(8,128)S(1)}, f32[2,8,256]{2,1,0:T(8,128)S(1)}, u32[]{:S(2)}, u32[]{:S(2)}) collective-permute-start(f32[2,8,256]{2,1,0:T(8,128)S(1)} %get-tuple-element.36), channel_id=1, source_target_pairs={{0,4},{1,5},{2,6},{3,7},{4,0},{5,1},{6,2},{7,3},{8,12},{9,13},{10,... | collective-permute-start | bytes 49160 | tf_op jit(solution)/shard_map/ppermute | solution.py:635
  12.9 3.7 %collective-permute-start.5 = (f32[2,8,256]{2,1,0:T(8,128)S(1)}, f32[2,8,256]{2,1,0:T(8,128)S(1)}, u32[]{:S(2)}, u32[]{:S(2)}) collective-permute-start(f32[2,8,256]{2,1,0:T(8,128)S(1)} %get-tuple-element.37), channel_id=1, source_target_pairs={{0,1},{1,0},{2,3},{3,2},{4,8},{5,9},{6,10},{7,11},{8,4},{9,5},{10,... | collective-permute-start | bytes 49160 | tf_op jit(solution)/shard_map/ppermute | solution.py:635
  16.7 10.7 %collective-permute-start.7 = (f32[7,16,1024]{2,1,0:T(8,128)S(1)}, f32[7,16,1024]{2,1,0:T(8,128)S(1)}, u32[]{:S(2)}, u32[]{:S(2)}) collective-permute-start(f32[7,16,1024]{2,1,0:T(8,128)S(1)} %get-tuple-element.40), channel_id=1, source_target_pairs={{0,1},{1,0},{2,3},{3,2},{4,8},{5,9},{6,10},{7,11},{8,4},{9,5},{10,... | collective-permute-start | bytes 1376264 | tf_op jit(solution)/shard_map/ppermute | solution.py:635
  27.4 1.5 %collective-permute-start.8 = (f32[3,16,1024]{2,1,0:T(8,128)S(1)}, f32[3,16,1024]{2,1,0:T(8,128)S(1)}, u32[]{:S(2)}, u32[]{:S(2)}) collective-permute-start(f32[3,16,1024]{2,1,0:T(8,128)S(1)} %slice.3), channel_id=1, source_target_pairs={{0,4},{1,5},{2,6},{3,7},{4,0},{5,1},{6,2},{7,3},{8,12},{9,13},{10,... | collective-permute-start | bytes 589832 | tf_op jit(solution)/shard_map/ppermute | solution.py:635
  30.1 24.1 %collective-permute-start.12 = (f32[15,8,1024]{2,1,0:T(8,128)}, f32[15,8,1024]{2,1,0:T(8,128)S(1)}, u32[]{:S(2)}, u32[]{:S(2)}) collective-permute-start(f32[15,8,1024]{2,1,0:T(8,128)} %get-tuple-element.50), channel_id=1, source_target_pairs={{0,1},{1,0},{2,3},{3,2},{4,5},{5,4},{6,7},{7,6},{8,9},{9,8},{10,11... | collective-permute-start | bytes 1474568 | tf_op jit(solution)/shard_map/ppermute | solution.py:635
  30.4 23.8 %collective-permute-start.13 = (f32[15,8,1024]{2,1,0:T(8,128)}, f32[15,8,1024]{2,1,0:T(8,128)S(1)}, u32[]{:S(2)}, u32[]{:S(2)}) collective-permute-start(f32[15,8,1024]{2,1,0:T(8,128)} %get-tuple-element.51), channel_id=1, source_target_pairs={{0,4},{1,2},{2,1},{3,7},{4,0},{5,6},{6,5},{7,3},{8,12},{9,10},{10,... | collective-permute-start | bytes 1474568 | tf_op jit(solution)/shard_map/ppermute | solution.py:635
  31.5 21.2 %all-to-all-start.1 = ((f32[16,4,8,128]{3,2,1,0:T(8,128)}), f32[16,4,8,128]{3,2,1,0:T(8,128)S(1)}, u32[]{:S(2)}, u32[]{:S(2)}) async-start(f32[16,4,8,128]{3,2,1,0:T(8,128)} %get-tuple-element.46), calls=%async_computation.1 | async-start | bytes 524288 | tf_op jit(solution)/shard_map/all_to_all | solution.py:687
  43.1 13.0 %collective-permute-start.10 = (f32[4,16,256]{2,1,0:T(8,128)S(1)}, f32[4,16,256]{2,1,0:T(8,128)S(1)}, u32[]{:S(2)}, u32[]{:S(2)}) collective-permute-start(f32[4,16,256]{2,1,0:T(8,128)S(1)} %get-tuple-element.47.f2), channel_id=1, source_target_pairs={{0,4},{1,5},{2,6},{3,7},{4,0},{5,1},{6,2},{7,3},{8,16},{9,17},{10,... | collective-permute-start | bytes 196616 | tf_op jit(solution)/shard_map/ppermute | solution.py:635
  43.2 12.9 %collective-permute-start.9 = (f32[4,16,256]{2,1,0:T(8,128)S(1)}, f32[4,16,256]{2,1,0:T(8,128)S(1)}, u32[]{:S(2)}, u32[]{:S(2)}) collective-permute-start(f32[4,16,256]{2,1,0:T(8,128)S(1)} %get-tuple-element.47.f2), channel_id=1, source_target_pairs={{0,8},{1,9},{2,10},{3,11},{4,12},{5,13},{6,14},{7,15},{8,0},{9,1},... | collective-permute-start | bytes 196616 | tf_op jit(solution)/shard_map/ppermute | solution.py:635
  46.5 9.6 %collective-permute-start.11 = (f32[1,16,256]{2,1,0:T(8,128)S(1)}, f32[1,16,256]{2,1,0:T(8,128)S(1)}, u32[]{:S(2)}, u32[]{:S(2)}) collective-permute-start(f32[1,16,256]{2,1,0:T(8,128)S(1)} %get-tuple-element.48), channel_id=1, source_target_pairs={{0,8},{1,9},{2,10},{3,11},{4,16},{5,17},{6,18},{7,19},{8,0},{9,1},... | collective-permute-start | bytes 49160 | tf_op jit(solution)/shard_map/ppermute | solution.py:635

commit v4 on v3

--- a/solution.py
+++ b/solution.py
@@ -25,15 +25,34 @@
     return lax.broadcasted_iota(jnp.int32, (rows, LANES), 0)
 
 
+def lane_before(col):
+    lane = lanes(col.shape[0])
+    wrapped = jnp.where(lane == 0, 0.0, pltpu.roll(col, 9, 1))
+    return jnp.where(lane < 8, wrapped, pltpu.roll(col, 8, 1))
+
+
+def lane_after(col):
+    lane = lanes(col.shape[0])
+    wrapped = jnp.where(lane == LANES - 1, 0.0, pltpu.roll(col, LANES - 9, 1))
+    return jnp.where(lane >= LANES - 8, wrapped, pltpu.roll(col, LANES - 8, 1))
+
+
 def along_z(cols):
+    return [lane_before(cols[-1])] + cols[:-1], cols[1:] + [lane_after(cols[0])]
+
+
+def regroup(cols):
+    cols = list(cols)
     lane = lanes(cols[0].shape[0])
-    first, last = lane == 0, lane == LANES - 1
-    right = [pltpu.roll(c, 1, 1) for c in cols]
-    left = [pltpu.roll(c, LANES - 1, 1) for c in cols]
-    n = len(cols)
-    before = [jnp.where(first, right[k - 1] if k else 0.0, right[k]) for k in range(n)]
-    after = [jnp.where(last, left[k + 1] if k < n - 1 else 0.0, left[k]) for k in range(n)]
-    return before, after
+    for s in (1, 2, 4):
+        low, beside = (lane & s) == 0, lane ^ s
+        for a in range(8):
+            b = a | s
+            if a != b:
+                moved = jnp.where(low, cols[b], cols[a])
+                moved = jnp.take_along_axis(moved, beside, axis=1, mode="promise_in_bounds")
+                cols[a], cols[b] = jnp.where(low, cols[a], moved), jnp.where(low, moved, cols[b])
+    return cols
 
 
 def around(ref, x, whole=False):
@@ -50,30 +69,15 @@
     return cols, out
 
 
-def pairs_z(even, odd):
-    lane = lanes(even.shape[0])
-    take = (lane * 2) % LANES
-    got = [
-        jnp.take_along_axis(c + pltpu.roll(c, LANES - 1, 1), take, axis=1, mode="promise_in_bounds") for c in (even, odd)
-    ]
-    return jnp.where(lane < LANES // 2, got[0], got[1])
-
-
-def twice_z(col):
-    lane = lanes(col.shape[0])
-    return [jnp.take_along_axis(col, lane // 2 + h * (LANES // 2), axis=1, mode="promise_in_bounds") for h in (0, 1)]
-
-
 def restricted(tmp, rows):
     sums = [tmp[k, pl.ds(0, rows, 2), :] + tmp[k, pl.ds(1, rows, 2), :] for k in range(tmp.shape[0])]
-    return [0.5 * pairs_z(sums[2 * m], sums[2 * m + 1]) for m in range(tmp.shape[0] // 2)]
+    return [0.5 * (sums[2 * m] + sums[2 * m + 1]) for m in range(tmp.shape[0] // 2)]
 
 
 def prolonged(tmp, cols, rows, at=0):
     for m, c in enumerate(cols):
-        for h, e in enumerate(twice_z(c)):
-            tmp[2 * m + h, pl.ds(at, rows, 2), :] = e
-            tmp[2 * m + h, pl.ds(at + 1, rows, 2), :] = e
+        tmp[m, pl.ds(at, rows, 2), :] = c
+        tmp[m, pl.ds(at + 1, rows, 2), :] = c
 
 
 def inside(pos, count):
@@ -103,22 +107,14 @@
 
 
 def taps(cols):
-    lane = lanes(cols[0].shape[0])
-    before, after = along_z(cols)
     n = len(cols)
-    three = [before[k] + cols[k] + after[k] for k in range(n)]
-    right = [pltpu.roll(c, 2, 1) for c in three]
-    left = [pltpu.roll(c, LANES - 2, 1) for c in three]
-    out = []
-    for k in range(n):
-        lo = right[k - 1] if k else jnp.where(lane == 1, before[0], 0.0)
-        hi = left[k + 1] if k < n - 1 else jnp.where(lane == LANES - 2, after[n - 1], 0.0)
-        out.append(cols[k] + jnp.where(lane < 2, lo, right[k]) + jnp.where(lane >= LANES - 2, hi, left[k]))
-    return out, before, after
+    more = [lane_before(c) for c in cols[-3:]] + cols + [lane_after(c) for c in cols[:3]]
+    out = [((more[k] + more[k + 1]) + (more[k + 2] + more[k + 3])) + ((more[k + 4] + more[k + 5]) + more[k + 6]) for k in range(n)]
+    return out, more[2 : n + 2], more[4 : n + 4]
 
 
 def split(value):
-    return [value[:, k * LANES : (k + 1) * LANES] for k in range(value.shape[1] // LANES)]
+    return regroup(value[:, k * LANES : (k + 1) * LANES] for k in range(value.shape[1] // LANES))
 
 
 def place(leaves, subs):
@@ -139,17 +135,25 @@
         to_2[x : x + 1, :] = jnp.where(odd_j, last, first)
 
 
-def columns(vf, mask, H, G):
+def columns(vf, mask_in, H, G, mask, sem):
     nz = vf.shape[2] // LANES
+    copy = pltpu.make_async_copy(mask_in, mask, sem)
+    copy.start()
 
     def level0(x):
         h, before, after = taps(split(vf[x]))
-        m = mask[x].astype(f32)
         for k in range(nz):
             H[x, k] = h[k]
-            G[x, k] = (after[k] - before[k]) * (0.5 * m[:, k * LANES : (k + 1) * LANES])
-
-    each(0, NX, level0, 2)
+            G[x, k] = 0.5 * (after[k] - before[k])
+
+    def masked(x):
+        m = split(mask[x].astype(f32))
+        for k in range(nz):
+            G[x, k] = G[x, k] * m[k]
+
+    each(0, NX, level0, 4)
+    copy.wait()
+    each(0, NX, masked, 8)
 
 
 def source(dims, H, G, ra, rb, rs1, rs2, src):
@@ -333,7 +337,7 @@
     for q in range(4):
         for k, v in enumerate(restricted(T2.at[q], 8)):
             for t in range(out.shape[0]):
-                out[t, q, :, k * LANES : (k + 1) * LANES] = v
+                out[t, q, :, k * LANES : (k + 1) * LANES] = in_order(v)
 
 
 def rows_out(dims, src, big, ra, rb, far, f1x, s1, s2):
@@ -384,40 +388,46 @@
         s2[8 + x % 7, :, s] = jnp.where(odd_j, last, first)
 
 
-def coarsest(dims, got, out, G3, U3, V3):
+def in_order(col):
+    lane = lanes(col.shape[0])
+    return jnp.take_along_axis(col, 8 * (lane % 16) + lane // 16, axis=1, mode="promise_in_bounds")
+
+
+def as_kept(col):
+    lane = lanes(col.shape[0])
+    return jnp.take_along_axis(col, 16 * (lane % 8) + lane // 8, axis=1, mode="promise_in_bounds")
+
+
+def coarsest(dims, got, out, G3):
     leaves = dims[0]
-    chips, n3 = got.shape[0], got.shape[3] // LANES
+    chips = got.shape[0]
+    i = lax.axis_index("leaf")
     zero = jnp.zeros((8, LANES), f32)
-    for k in range(n3):
-        s = slice(k * LANES, (k + 1) * LANES)
-        for x in (0, 1, leaves + 2, leaves + 3):
-            U3[x, k] = zero
-            V3[x, k] = zero
-        for c in range(chips):
-            a, b = got[c, 1, :, s], got[c, 2, :, s]
-            if c > 0:
-                a = a + got[c - 1, 3, :, s]
-            if c < chips - 1:
-                b = b + got[c + 1, 0, :, s]
-            G3[2 * c + 2, k], G3[2 * c + 3, k] = a, b
-            U3[2 * c + 2, k], U3[2 * c + 3, k] = D * a, D * b
-
-    def sweep3(old, new):
-        def body(x):
-            u, around_u = around(old, x, True)
-            for k in range(n3):
-                new[x, k] = C0 * u[k] + D * (G3[x, k] + around_u[k])
-
-        each(2, leaves + 2, body, 16)
-
-    for _ in range(3):
-        sweep3(U3, V3)
-        sweep3(V3, U3)
-    sweep3(U3, V3)
-    i = lax.axis_index("leaf")
+    for x in range(9):
+        G3[x] = zero
+        G3[leaves + 9 + x] = zero
+    for c in range(chips):
+        a, b = got[c, 1], got[c, 2]
+        if c > 0:
+            a = a + got[c - 1, 3]
+        if c < chips - 1:
+            b = b + got[c + 1, 0]
+        G3[2 * c + 9], G3[2 * c + 10] = a, b
+    lane, row = lanes(8), rows_of(8)
+    ends = [lane == 0, lane == LANES - 1, row == 0, row == 7]
+    f = [D * G3[i + w] for w in range(19)]
+    keep = [jnp.where(inside(i + w - 9, leaves), 1.0, 0.0).astype(f32) for w in range(19)]
+    u = list(f)
+    for s in range(1, 8):
+        new = list(u)
+        for w in range(s, 19 - s):
+            c = u[w]
+            z = jnp.where(ends[0], 0.0, pltpu.roll(c, 1, 1)) + jnp.where(ends[1], 0.0, pltpu.roll(c, LANES - 1, 1))
+            y = jnp.where(ends[2], 0.0, pltpu.roll(c, 1, 0)) + jnp.where(ends[3], 0.0, pltpu.roll(c, 7, 0))
+            new[w] = (C0 * c + (f[w] + D * ((u[w + 1] + u[w - 1]) + (y + z)))) * keep[w]
+        u = new
     for x in range(5):
-        for k in range(n3):
-            out[x, :, k * LANES : (k + 1) * LANES] = V3[i + x, k]
+        out[x] = as_kept(u[7 + x])
 
 
 def ready(dims, src, ra, rb, f1x, rs1, rs2, F0, P0, F1, P1):
@@ -486,7 +496,7 @@
     each(1, 15, smooth0, 4)
 
 
-def ascent(dims, u3, f2, r2c1, r2c2, r2e, F0, P0, F1, P1, press, resid, F2, T2, W2, X2, T1, V1, X1, T0, V0, X0):
+def ascent(dims, u3, f2, r2c1, r2c2, r2e, F0, P0, F1, P1, press_out, resid_out, F2, T2, W2, X2, T1, V1, X1, T0, V0, X0, press, resid, done):
     leaves, subs = dims
     i, j, odd_i, odd_j, far_i, far_j = place(leaves, subs)
     count_x, count_y = leaves * NX, subs * NY
@@ -516,7 +526,7 @@
         m = plane_mask(m2, 2 * i + w - 4, 2 * leaves)
         f, around_f = around(F2, base + w + 1, True)
         for k in range(n2):
-            W2[w, k] = (C1 * f[k] + C2 * around_f[k] + T2[w // 2, k]) * m
+            W2[w, k] = (C1 * f[k] + C2 * around_f[k] + T2[w // 2, k // 2]) * m
 
     def sweep2(old, new, lo, hi):
         for w in range(lo, hi):
@@ -529,7 +539,7 @@
     sweep2(X2, W2, 2, 8)
 
     for c in range(6):
-        for k in range(n1):
+        for k in range(n2):
             T1[c, k] = zero
     my1 = row_mask(24, j * (NY // 2) - 8, count_y // 2)
 
@@ -541,7 +551,7 @@
             x = 2 * c + p + 1
             m = plane_mask(my1, i * (NX // 2) + x - 5, count_x // 2)
             for k in range(n1):
-                V1[x, k] = P1[x, k] + T1[c, k] * m
+                V1[x, k] = P1[x, k] + T1[c, k // 2] * m
 
     def sweep1(old, new, lo, hi):
         def body(x):
@@ -550,7 +560,7 @@
             for k in range(n1):
                 new[x, k] = (C0 * u[k] + D * (F1[x, k] + around_u[k])) * m
 
-        each(lo, hi, body, 4)
+        each(lo, hi, body, (hi - lo) // 2)
 
     sweep1(V1, X1, 2, 12)
     sweep1(X1, V1, 3, 11)
@@ -561,12 +571,12 @@
     def start0(c):
         prolonged(T0.at[c], [V1[c + 3, k, 6:18, :] for k in range(n1)], 12)
 
-    each(0, 8, start0, 2)
+    each(0, 8, start0, 4)
 
     def smooth0(x):
         m = plane_mask(my0, i * NX + x - 4, count_x)
         for k in range(nz):
-            V0[x, k] = P0[x, k] + T0[x // 2, k] * m
+            V0[x, k] = P0[x, k] + T0[x // 2, k // 2] * m
 
     each(1, 15, smooth0, 4)
 
@@ -582,23 +592,44 @@
     sweep0(V0, X0, 2, 14)
     sweep0(X0, V0, 3, 13)
 
-    def finish(x):
-        u, around_u = around(V0, x + 4)
-        for k in range(nz):
-            s = slice(k * LANES, (k + 1) * LANES)
-            press[x, :, s] = u[k][4:20]
-            resid[x, :, s] = (F0[x + 4, k] - 6.0 * u[k] + around_u[k])[4:20]
-
-    each(0, NX, finish, 4)
-
-
-def call(kernel, outs, scratch, *args, us=1.0):
+    def put(out, x, cols):
+        for k, v in enumerate(regroup(cols)):
+            out[x, :, k * LANES : (k + 1) * LANES] = v
+
+    def rest(x):
+        u = [V0[x + 4, k, 4:20, :] for k in range(nz)]
+        before, after = along_z(u)
+        res = []
+        for k in range(nz):
+            near = V0[x + 5, k, 4:20, :] + V0[x + 3, k, 4:20, :] + (V0[x + 4, k, 5:21, :] + V0[x + 4, k, 3:19, :])
+            res.append(F0[x + 4, k, 4:20, :] - 6.0 * u[k] + (near + (before[k] + after[k])))
+        put(resid, x, res)
+
+    copies = []
+
+    def away(t, a, b, x):
+        copies.append(pltpu.make_async_copy(a.at[pl.ds(x, 4)], b.at[pl.ds(x, 4)], done.at[t, x // 4]))
+        copies[-1].start()
+
+    each(0, NX, lambda x: put(press, x, [V0[x + 4, k, 4:20, :] for k in range(nz)]), 4)
+    for x in (0, 4):
+        away(0, press, press_out, x)
+    each(0, NX, rest, 4)
+    for x in (0, 4):
+        away(1, resid, resid_out, x)
+    for copy in copies:
+        copy.wait()
+
+
+def call(kernel, outs, scratch, *args, here=(), away=False, mib=4):
+    vmem, hbm = pl.BlockSpec(), pl.BlockSpec(memory_space=pltpu.HBM)
     return pl.pallas_call(
         kernel,
         out_shape=[jax.ShapeDtypeStruct(s, f32) for s in outs],
-        scratch_shapes=[pltpu.VMEM(s, f32) for s in scratch],
-        compiler_params=pltpu.CompilerParams(vmem_limit_bytes=20 * 1024 * 1024),
-        cost_estimate=pl.CostEstimate(flops=0, transcendentals=0, bytes_accessed=int(us * 3.6e6)),
+        in_specs=[hbm if n in here else vmem for n in range(len(args))],
+        out_specs=[hbm if away else vmem for _ in outs],
+        scratch_shapes=[pltpu.VMEM(s, f32) if isinstance(s, tuple) else s for s in scratch],
+        compiler_params=pltpu.CompilerParams(vmem_limit_bytes=mib * 1024 * 1024),
     )(*args)
 
 
@@ -639,7 +670,8 @@
     to_a, to_b, to_1, to_2 = call(functools.partial(edges, dims), [plane, plane, rows, rows], [], volume_fraction)
     halos = move(to_a, pa), move(to_b, pb), move(to_1, ps1), move(to_2, ps2)
     shape = (NX, nz, NY, LANES)
-    heights, slope = call(columns, [shape, shape], [], volume_fraction, interface_mask)
+    scratch = [pltpu.VMEM((NX, NY, depth), jnp.int32), pltpu.SemaphoreType.DMA]
+    heights, slope = call(columns, [shape, shape], scratch, volume_fraction, interface_mask, here=(1,))
     (src,) = call(functools.partial(source, dims), [(NX, NY, depth)], [], heights, slope, *halos)
     big, m2a, m2b, own2 = call(
         functools.partial(descent, dims),
@@ -654,6 +686,7 @@
             (6, n1, 16, LANES),
         ],
         src,
+        mib=10,
     )
     r2a, r2b, ra = move(m2a, pa), move(m2b, pb), move(big, pa)
     out, to_b = call(
@@ -686,25 +719,26 @@
     group = [[(2 * c + k) * subs + s for c in range(chips)] for k in (0, 1) for s in range(subs)]
     got = lax.all_to_all(out, AXES, 0, 0, axis_index_groups=group)
     r2c1, r2c2, r2e = move(f2, pc1), move(f2, pc2), move(edge, pe)
-    (u3,) = call(
-        functools.partial(coarsest, dims), [(5, 8, depth // 8)], [(leaves + 4, n3, 8, LANES)] * 3, got
-    )
     shape0, shape1 = (16, nz, 24, LANES), (14, n1, 24, LANES)
-    F0, P0, F1, P1 = call(functools.partial(ready, dims), [shape0, shape0, shape1, shape1], [], src, ra, rb, f1x, rs1, rs2)
+    F0, P0, F1, P1 = call(functools.partial(ready, dims), [shape0, shape0, shape1, shape1], [], src, ra, rb, f1x, rs1, rs2, mib=10)
+    (u3,) = call(functools.partial(coarsest, dims), [(5, 8, depth // 8)], [(leaves + 18, 8, LANES)], got)
     return call(
         functools.partial(ascent, dims),
         [(NX, NY, depth), (NX, NY, depth)],
         [
             (14, n2, 16, LANES),
-            (5, n2, 16, LANES),
+            (5, n3, 16, LANES),
             (10, n2, 16, LANES),
             (10, n2, 16, LANES),
-            (6, n1, 24, LANES),
+            (6, n2, 24, LANES),
             shape1,
             shape1,
-            (8, nz, 24, LANES),
+            (8, n1, 24, LANES),
             shape0,
             shape0,
+            (NX, NY, depth),
+            (NX, NY, depth),
+            pltpu.SemaphoreType.DMA((2, NX // 4)),
         ],
         u3,
         f2,
@@ -715,6 +749,8 @@
         P0,
         F1,
         P1,
+        away=True,
+        mib=16,
     )
 
 

time: 61.6 us -> 57.8 us (0.938)
  Pallas kernels: 16.5 us -> 13 us
    pallas_call x10, Pallas kernels: 16.5 us -> 13 us  [call(): pl.pallas_call(kernel, out_shape=[jax.ShapeDtypeStruct(s, f32) for s in o...]
  transfers between devices with their start and end apart: 15 -> 15, of which waited for: 5 -> 4; matrix products, arithmetic and copies ran while one was open for 0% -> 0% of each run, Pallas kernels for 9% -> 8%
where the time goes in v4:
time: 57.8 us; the launch traced here: 57.4 us
  starting transfers between devices  20.9 us (36%)
  Pallas kernels  13 us (22%)
  blocking collectives  10.5 us (18%)
  waiting for transfers between devices  10.2 us (18%)
  local copies, waits for them, and re-layouts  2.09 us (4%)
  between operations  0.79 us (1%)
    pallas_call x10, Pallas kernels, call(): pl.pallas_call(kernel, out_shape=[jax.ShapeDtypeStruct(s, f32) for s in o...  13 us
    all_to_all x1, starting transfers between devices, shards(): got = lax.all_to_all(out, AXES, 0, 0, axis_index_groups=group)  11.5 us
    all_to_all x1, blocking collectives, shards(): got = lax.all_to_all(out, AXES, 0, 0, axis_index_groups=group)  10.5 us
    ppermute x14, starting transfers between devices, shards(): move = lambda v, table: lax.ppermute(v, AXES, table)  9.43 us
    all_to_all x1, waiting for transfers between devices, shards(): got = lax.all_to_all(out, AXES, 0, 0, axis_index_groups=group)  6.15 us
    ppermute x14, waiting for transfers between devices, shards(): move = lambda v, table: lax.ppermute(v, AXES, table)  4.04 us
    unnamed x4, local copies, waits for them, and re-layouts  2.08 us
  transfers between devices with their start and end apart: 15, of which 4 were waited for; matrix products, arithmetic and copies ran while one was open for 0% of the time, Pallas kernels for 8%

profile of v4, /device:TPU:2, one launch (start us, length us, event | category | flops | bytes accessed | tf_op | source)
XLA Modules:
  0.0 57.4 jit_solution(10955885424553208476)
XLA Ops:
  0.6 0.0 copy-start
  0.6 1.0 %copy-done = f32[8,16,1024]{2,1,0:T(8,128)S(1)} copy-done((f32[8,16,1024]{2,1,0:T(8,128)S(1)}, f32[8,16,1024]{2,1,0:T(8,128)}, u32[]{:S(2)}) %copy-start) | copy-done | bytes 524312
  1.7 0.1 collective-permute-start
  1.8 0.5 collective-permute-start.1
  2.3 1.6 %collective-permute-start.2 = (f32[8,1024]{1,0:T(8,128)S(1)}, f32[8,1024]{1,0:T(8,128)S(1)}, u32[]{:S(2)}, u32[]{:S(2)}) collective-permute-start(f32[8,1024]{1,0:T(8,128)S(1)} %get-tuple-element.33), channel_id=1, source_target_pairs={{0,1},{1,0},{2,3},{3,2},{4,5},{5,4},{6,7},{7,6},{8,9},{9,8},{10,11... | collective-permute-start | bytes 98312 | tf_op jit(solution)/shard_map/ppermute | solution.py:666
  3.9 1.5 %collective-permute-start.3 = (f32[8,1024]{1,0:T(8,128)S(1)}, f32[8,1024]{1,0:T(8,128)S(1)}, u32[]{:S(2)}, u32[]{:S(2)}) collective-permute-start(f32[8,1024]{1,0:T(8,128)S(1)} %get-tuple-element.34), channel_id=1, source_target_pairs={{0,4},{1,2},{2,1},{3,7},{4,0},{5,6},{6,5},{7,3},{8,12},{9,10},{10,... | collective-permute-start | bytes 98312 | tf_op jit(solution)/shard_map/ppermute | solution.py:666
  5.4 0.0 copy-start.1
  5.4 1.0 %copy-done.1 = s32[8,16,1024]{2,1,0:T(8,128)S(1)} copy-done((s32[8,16,1024]{2,1,0:T(8,128)S(1)}, s32[8,16,1024]{2,1,0:T(8,128)}, u32[]{:S(2)}) %copy-start.1) | copy-done | bytes 524312
  6.4 1.5 %shard_map.41 = (f32[8,8,16,128]{3,2,1,0:T(8,128)S(1)}, f32[8,8,16,128]{3,2,1,0:T(8,128)S(1)}) custom-call(f32[8,16,1024]{2,1,0:T(8,128)S(1)} %copy-done, s32[8,16,1024]{2,1,0:T(8,128)S(1)} %copy-done.1), custom_call_target="tpu_custom_call" | custom-call | tf_op jit(solution)/shard_map/pallas_call | solution.py:626
  7.9 0.0 collective-permute-done.2.rs1
  7.9 0.0 collective-permute-done.3.rs2
  8.0 0.0 collective-permute-done.ra
  8.0 0.0 collective-permute-done.1.rb
  8.0 0.7 %shard_map.43.src = f32[8,16,1024]{2,1,0:T(8,128)S(1)} custom-call(f32[8,8,16,128]{3,2,1,0:T(8,128)S(1)} %get-tuple-element.29.H, f32[8,8,16,128]{3,2,1,0:T(8,128)S(1)} %get-tuple-element.30.G, f32[1,16,1024]{2,1,0:T(8,128)S(1)} %collective-permute-done.ra, f32[1,16,1024]{2,1,0:T(8,128)S(1)} %collective-permute-done.1.rb, ...), custom_call_target="tpu_custom_call" | custom-call | tf_op jit(solution)/shard_map/pallas_call | solution.py:626
  8.7 2.0 %shard_map.44 = (f32[7,16,1024]{2,1,0:T(8,128)S(1)}, f32[2,8,256]{2,1,0:T(8,128)S(1)}, f32[2,8,256]{2,1,0:T(8,128)S(1)}, f32[2,8,256]{2,1,0:T(8,128)S(1)}) custom-call(f32[8,16,1024]{2,1,0:T(8,128)S(1)} %shard_map.43.src), custom_call_target="tpu_custom_call" | custom-call | tf_op jit(solution)/shard_map/pallas_call | solution.py:626
  10.6 0.4 collective-permute-start.6
  11.0 0.2 collective-permute-start.4
  11.2 0.0 collective-permute-start.5
  11.2 1.3 %collective-permute-done.4.r2a = f32[2,8,256]{2,1,0:T(8,128)S(1)} collective-permute-done((f32[2,8,256]{2,1,0:T(8,128)S(1)}, f32[2,8,256]{2,1,0:T(8,128)S(1)}, u32[]{:S(2)}, u32[]{:S(2)}) %collective-permute-start.4) | collective-permute-done | bytes 16416 | tf_op jit(solution)/shard_map/ppermute | solution.py:666
  12.5 2.4 %collective-permute-done.5.r2b = f32[2,8,256]{2,1,0:T(8,128)S(1)} collective-permute-done((f32[2,8,256]{2,1,0:T(8,128)S(1)}, f32[2,8,256]{2,1,0:T(8,128)S(1)}, u32[]{:S(2)}, u32[]{:S(2)}) %collective-permute-start.5) | collective-permute-done | bytes 16416 | tf_op jit(solution)/shard_map/ppermute | solution.py:666
  15.0 0.0 collective-permute-done.6.ra
  15.0 0.1 shard_map.45
  15.0 0.1 collective-permute-start.7
  15.1 10.5 %all_to_all.10.got = f32[8,2,8,256]{3,2,1,0:T(8,128)S(1)} all-to-all(f32[8,2,8,256]{3,2,1,0:T(8,128)S(1)} %get-tuple-element.39), channel_id=1, replica_groups={{0,1,2,3,4,5,6,7},{8,9,10,11,12,13,14,15},{16,17,18,19,20,21,22,23},{24..., dimensions={0} | all-to-all | bytes 262144 | tf_op jit(solution)/shard_map/all_to_all | solution.py:697
  25.6 0.0 collective-permute-done.7.rb
  25.6 0.2 collective-permute-start.8
  25.8 1.1 %shard_map.46 = (f32[4,16,256]{2,1,0:T(8,128)S(1)}, f32[1,16,256]{2,1,0:T(8,128)S(1)}, f32[16,4,8,128]{3,2,1,0:T(8,128)}) custom-call(f32[8,2,8,256]{3,2,1,0:T(8,128)S(1)} %all_to_all.10.got), custom_call_target="tpu_custom_call" | custom-call | tf_op jit(solution)/shard_map/pallas_call | solution.py:626
  26.9 0.3 collective-permute-done.8.far
  27.1 1.2 %shard_map.47 = (f32[14,16,512]{2,1,0:T(8,128)S(1)}, f32[15,8,1024]{2,1,0:T(8,128)}, f32[15,8,1024]{2,1,0:T(8,128)}) custom-call(f32[8,16,1024]{2,1,0:T(8,128)S(1)} %shard_map.43.src, f32[7,16,1024]{2,1,0:T(8,128)S(1)} %get-tuple-element.38.big, f32[7,16,1024]{2,1,0:T(8,128)S(1)} %collective-permute-done.6.ra, f32[7,16,1024]{2,1,0:T(8,128)S(1)} %collective-permute-done.7.rb, ...), custom_call_target="tpu_custom_call" | custom-call | tf_op jit(solution)/shard_map/pallas_call | solution.py:626
  28.3 0.3 collective-permute-start.12
  28.6 1.2 %collective-permute-start.13 = (f32[15,8,1024]{2,1,0:T(8,128)}, f32[15,8,1024]{2,1,0:T(8,128)S(1)}, u32[]{:S(2)}, u32[]{:S(2)}) collective-permute-start(f32[15,8,1024]{2,1,0:T(8,128)} %get-tuple-element.51), channel_id=1, source_target_pairs={{0,4},{1,2},{2,1},{3,7},{4,0},{5,6},{6,5},{7,3},{8,12},{9,10},{10,... | collective-permute-start | bytes 1474568 | tf_op jit(solution)/shard_map/ppermute | solution.py:666
  29.8 11.5 %all-to-all-start.1 = ((f32[16,4,8,128]{3,2,1,0:T(8,128)}), f32[16,4,8,128]{3,2,1,0:T(8,128)S(1)}, u32[]{:S(2)}, u32[]{:S(2)}) async-start(f32[16,4,8,128]{3,2,1,0:T(8,128)} %get-tuple-element.46), calls=%async_computation.1 | async-start | bytes 524288 | tf_op jit(solution)/shard_map/all_to_all | solution.py:720
  41.3 0.1 collective-permute-start.10
  41.4 3.3 %collective-permute-start.9 = (f32[4,16,256]{2,1,0:T(8,128)S(1)}, f32[4,16,256]{2,1,0:T(8,128)S(1)}, u32[]{:S(2)}, u32[]{:S(2)}) collective-permute-start(f32[4,16,256]{2,1,0:T(8,128)S(1)} %get-tuple-element.47.f2), channel_id=1, source_target_pairs={{0,8},{1,9},{2,10},{3,11},{4,12},{5,13},{6,14},{7,15},{8,0},{9,1},... | collective-permute-start | bytes 196616 | tf_op jit(solution)/shard_map/ppermute | solution.py:666
  44.7 0.0 collective-permute-start.11
  44.8 6.1 %all-to-all-done.1.got = f32[16,4,8,128]{3,2,1,0:T(8,128)S(1)} async-done(((f32[16,4,8,128]{3,2,1,0:T(8,128)}), f32[16,4,8,128]{3,2,1,0:T(8,128)S(1)}, u32[]{:S(2)}, u32[]{:S(2)}) %all-to-all-start.1) | async-done | bytes 262176 | tf_op jit(solution)/shard_map/all_to_all | solution.py:720
  50.9 0.6 %shard_map.48.u3 = f32[5,8,128]{2,1,0:T(8,128)S(1)} custom-call(f32[16,4,8,128]{3,2,1,0:T(8,128)S(1)} %all-to-all-done.1.got), custom_call_target="tpu_custom_call" | custom-call | tf_op jit(solution)/shard_map/pallas_call | solution.py:626
  51.5 0.0 collective-permute-done.12.rs1
  51.5 0.0 collective-permute-done.13.rs2
  51.5 1.4 %shard_map.49 = (f32[16,8,24,128]{3,2,1,0:T(8,128)S(1)}, f32[16,8,24,128]{3,2,1,0:T(8,128)S(1)}, f32[14,4,24,128]{3,2,1,0:T(8,128)S(1)}, f32[14,4,24,128]{3,2,1,0:T(8,128)S(1)}) custom-call(f32[8,16,1024]{2,1,0:T(8,128)S(1)} %shard_map.43.src, f32[7,16,1024]{2,1,0:T(8,128)S(1)} %collective-permute-done.6.ra, f32[7,16,1024]{2,1,0:T(8,128)S(1)} %collective-permute-done.7.rb, ...), custom_call_target="tpu_custom_call" | custom-call | tf_op jit(solution)/shard_map/pallas_call | solution.py:626
  52.9 0.0 collective-permute-done.11.r2e
  52.9 0.0 collective-permute-done.10.r2c2
  52.9 0.0 collective-permute-done.9.r2c1
  52.9 4.5 %shard_map.50 = (f32[8,16,1024]{2,1,0:T(8,128)}, f32[8,16,1024]{2,1,0:T(8,128)}) custom-call(f32[5,8,128]{2,1,0:T(8,128)S(1)} %shard_map.48.u3, f32[4,16,256]{2,1,0:T(8,128)S(1)} %get-tuple-element.47.f2, f32[4,16,256]{2,1,0:T(8,128)S(1)} %collective-permute-done.9.r2c1, f32[4,16,256]{2,1,0:T(8,128)S(1)} %collective-permute-done.10.r2c2, ...), custom_call_target="tpu_custom_call" | custom-call | tf_op jit(solution)/shard_map/pallas_call | solution.py:626
  (2 shorter events, 0.0 us)
Async XLA Ops:
  0.6 1.0 %copy-start = (f32[8,16,1024]{2,1,0:T(8,128)S(1)}, f32[8,16,1024]{2,1,0:T(8,128)}, u32[]{:S(2)}) copy-start(f32[8,16,1024]{2,1,0:T(8,128)} %vf.3) | copy-start | bytes 1572868
  1.7 6.2 %collective-permute-start = (f32[1,16,1024]{2,1,0:T(8,128)S(1)}, f32[1,16,1024]{2,1,0:T(8,128)S(1)}, u32[]{:S(2)}, u32[]{:S(2)}) collective-permute-start(f32[1,16,1024]{2,1,0:T(8,128)S(1)} %get-tuple-element.31), channel_id=1, source_target_pairs={{0,4},{1,5},{2,6},{3,7},{4,0},{5,1},{6,2},{7,3},{8,12},{9,13},{10,... | collective-permute-start | bytes 196616 | tf_op jit(solution)/shard_map/ppermute | solution.py:666
  1.8 6.2 %collective-permute-start.1 = (f32[1,16,1024]{2,1,0:T(8,128)S(1)}, f32[1,16,1024]{2,1,0:T(8,128)S(1)}, u32[]{:S(2)}, u32[]{:S(2)}) collective-permute-start(f32[1,16,1024]{2,1,0:T(8,128)S(1)} %get-tuple-element.32), channel_id=1, source_target_pairs={{0,1},{1,0},{2,3},{3,2},{4,8},{5,9},{6,10},{7,11},{8,4},{9,5},{10,... | collective-permute-start | bytes 196616 | tf_op jit(solution)/shard_map/ppermute | solution.py:666
  2.3 5.6 %collective-permute-start.2 = (f32[8,1024]{1,0:T(8,128)S(1)}, f32[8,1024]{1,0:T(8,128)S(1)}, u32[]{:S(2)}, u32[]{:S(2)}) collective-permute-start(f32[8,1024]{1,0:T(8,128)S(1)} %get-tuple-element.33), channel_id=1, source_target_pairs={{0,1},{1,0},{2,3},{3,2},{4,5},{5,4},{6,7},{7,6},{8,9},{9,8},{10,11... | collective-permute-start | bytes 98312 | tf_op jit(solution)/shard_map/ppermute | solution.py:666
  3.9 4.0 %collective-permute-start.3 = (f32[8,1024]{1,0:T(8,128)S(1)}, f32[8,1024]{1,0:T(8,128)S(1)}, u32[]{:S(2)}, u32[]{:S(2)}) collective-permute-start(f32[8,1024]{1,0:T(8,128)S(1)} %get-tuple-element.34), channel_id=1, source_target_pairs={{0,4},{1,2},{2,1},{3,7},{4,0},{5,6},{6,5},{7,3},{8,12},{9,10},{10,... | collective-permute-start | bytes 98312 | tf_op jit(solution)/shard_map/ppermute | solution.py:666
  5.4 1.0 %copy-start.1 = (s32[8,16,1024]{2,1,0:T(8,128)S(1)}, s32[8,16,1024]{2,1,0:T(8,128)}, u32[]{:S(2)}) copy-start(s32[8,16,1024]{2,1,0:T(8,128)} %mask_in.1) | copy-start | bytes 1572868
  10.6 4.3 %collective-permute-start.6 = (f32[7,16,1024]{2,1,0:T(8,128)S(1)}, f32[7,16,1024]{2,1,0:T(8,128)S(1)}, u32[]{:S(2)}, u32[]{:S(2)}) collective-permute-start(f32[7,16,1024]{2,1,0:T(8,128)S(1)} %get-tuple-element.38.big), channel_id=1, source_target_pairs={{0,4},{1,5},{2,6},{3,7},{4,0},{5,1},{6,2},{7,3},{8,12},{9,13},{10,... | collective-permute-start | bytes 1376264 | tf_op jit(solution)/shard_map/ppermute | solution.py:666
  11.0 1.5 %collective-permute-start.4 = (f32[2,8,256]{2,1,0:T(8,128)S(1)}, f32[2,8,256]{2,1,0:T(8,128)S(1)}, u32[]{:S(2)}, u32[]{:S(2)}) collective-permute-start(f32[2,8,256]{2,1,0:T(8,128)S(1)} %get-tuple-element.36), channel_id=1, source_target_pairs={{0,4},{1,5},{2,6},{3,7},{4,0},{5,1},{6,2},{7,3},{8,12},{9,13},{10,... | collective-permute-start | bytes 49160 | tf_op jit(solution)/shard_map/ppermute | solution.py:666
  11.2 3.7 %collective-permute-start.5 = (f32[2,8,256]{2,1,0:T(8,128)S(1)}, f32[2,8,256]{2,1,0:T(8,128)S(1)}, u32[]{:S(2)}, u32[]{:S(2)}) collective-permute-start(f32[2,8,256]{2,1,0:T(8,128)S(1)} %get-tuple-element.37), channel_id=1, source_target_pairs={{0,1},{1,0},{2,3},{3,2},{4,8},{5,9},{6,10},{7,11},{8,4},{9,5},{10,... | collective-permute-start | bytes 49160 | tf_op jit(solution)/shard_map/ppermute | solution.py:666
  15.0 10.6 %collective-permute-start.7 = (f32[7,16,1024]{2,1,0:T(8,128)S(1)}, f32[7,16,1024]{2,1,0:T(8,128)S(1)}, u32[]{:S(2)}, u32[]{:S(2)}) collective-permute-start(f32[7,16,1024]{2,1,0:T(8,128)S(1)} %get-tuple-element.40), channel_id=1, source_target_pairs={{0,1},{1,0},{2,3},{3,2},{4,8},{5,9},{6,10},{7,11},{8,4},{9,5},{10,... | collective-permute-start | bytes 1376264 | tf_op jit(solution)/shard_map/ppermute | solution.py:666
  25.6 1.5 %collective-permute-start.8 = (f32[3,16,1024]{2,1,0:T(8,128)S(1)}, f32[3,16,1024]{2,1,0:T(8,128)S(1)}, u32[]{:S(2)}, u32[]{:S(2)}) collective-permute-start(f32[3,16,1024]{2,1,0:T(8,128)S(1)} %slice.3), channel_id=1, source_target_pairs={{0,4},{1,5},{2,6},{3,7},{4,0},{5,1},{6,2},{7,3},{8,12},{9,13},{10,... | collective-permute-start | bytes 589832 | tf_op jit(solution)/shard_map/ppermute | solution.py:666
  28.3 23.2 %collective-permute-start.12 = (f32[15,8,1024]{2,1,0:T(8,128)}, f32[15,8,1024]{2,1,0:T(8,128)S(1)}, u32[]{:S(2)}, u32[]{:S(2)}) collective-permute-start(f32[15,8,1024]{2,1,0:T(8,128)} %get-tuple-element.50), channel_id=1, source_target_pairs={{0,1},{1,0},{2,3},{3,2},{4,5},{5,4},{6,7},{7,6},{8,9},{9,8},{10,11... | collective-permute-start | bytes 1474568 | tf_op jit(solution)/shard_map/ppermute | solution.py:666
  28.6 22.9 %collective-permute-start.13 = (f32[15,8,1024]{2,1,0:T(8,128)}, f32[15,8,1024]{2,1,0:T(8,128)S(1)}, u32[]{:S(2)}, u32[]{:S(2)}) collective-permute-start(f32[15,8,1024]{2,1,0:T(8,128)} %get-tuple-element.51), channel_id=1, source_target_pairs={{0,4},{1,2},{2,1},{3,7},{4,0},{5,6},{6,5},{7,3},{8,12},{9,10},{10,... | collective-permute-start | bytes 1474568 | tf_op jit(solution)/shard_map/ppermute | solution.py:666
  29.8 21.1 %all-to-all-start.1 = ((f32[16,4,8,128]{3,2,1,0:T(8,128)}), f32[16,4,8,128]{3,2,1,0:T(8,128)S(1)}, u32[]{:S(2)}, u32[]{:S(2)}) async-start(f32[16,4,8,128]{3,2,1,0:T(8,128)} %get-tuple-element.46), calls=%async_computation.1 | async-start | bytes 524288 | tf_op jit(solution)/shard_map/all_to_all | solution.py:720
  41.3 11.6 %collective-permute-start.10 = (f32[4,16,256]{2,1,0:T(8,128)S(1)}, f32[4,16,256]{2,1,0:T(8,128)S(1)}, u32[]{:S(2)}, u32[]{:S(2)}) collective-permute-start(f32[4,16,256]{2,1,0:T(8,128)S(1)} %get-tuple-element.47.f2), channel_id=1, source_target_pairs={{0,4},{1,5},{2,6},{3,7},{4,0},{5,1},{6,2},{7,3},{8,16},{9,17},{10,... | collective-permute-start | bytes 196616 | tf_op jit(solution)/shard_map/ppermute | solution.py:666
  41.4 11.5 %collective-permute-start.9 = (f32[4,16,256]{2,1,0:T(8,128)S(1)}, f32[4,16,256]{2,1,0:T(8,128)S(1)}, u32[]{:S(2)}, u32[]{:S(2)}) collective-permute-start(f32[4,16,256]{2,1,0:T(8,128)S(1)} %get-tuple-element.47.f2), channel_id=1, source_target_pairs={{0,8},{1,9},{2,10},{3,11},{4,12},{5,13},{6,14},{7,15},{8,0},{9,1},... | collective-permute-start | bytes 196616 | tf_op jit(solution)/shard_map/ppermute | solution.py:666
  44.7 8.2 %collective-permute-start.11 = (f32[1,16,256]{2,1,0:T(8,128)S(1)}, f32[1,16,256]{2,1,0:T(8,128)S(1)}, u32[]{:S(2)}, u32[]{:S(2)}) collective-permute-start(f32[1,16,256]{2,1,0:T(8,128)S(1)} %get-tuple-element.48), channel_id=1, source_target_pairs={{0,8},{1,9},{2,10},{3,11},{4,16},{5,17},{6,18},{7,19},{8,0},{9,1},... | collective-permute-start | bytes 49160 | tf_op jit(solution)/shard_map/ppermute | solution.py:666

commit v5 on v4

--- a/solution.py
+++ b/solution.py
@@ -135,10 +135,8 @@
         to_2[x : x + 1, :] = jnp.where(odd_j, last, first)
 
 
-def columns(vf, mask_in, H, G, mask, sem):
+def columns(vf, H, G):
     nz = vf.shape[2] // LANES
-    copy = pltpu.make_async_copy(mask_in, mask, sem)
-    copy.start()
 
     def level0(x):
         h, before, after = taps(split(vf[x]))
@@ -146,14 +144,16 @@
             H[x, k] = h[k]
             G[x, k] = 0.5 * (after[k] - before[k])
 
-    def masked(x):
+    each(0, NX, level0, 4)
+
+
+def masked(G, mask, out):
+    def body(x):
         m = split(mask[x].astype(f32))
-        for k in range(nz):
-            G[x, k] = G[x, k] * m[k]
-
-    each(0, NX, level0, 4)
-    copy.wait()
-    each(0, NX, masked, 8)
+        for k in range(len(m)):
+            out[x, k] = G[x, k] * m[k]
+
+    each(0, NX, body, 8)
 
 
 def source(dims, H, G, ra, rb, rs1, rs2, src):
@@ -183,7 +183,7 @@
             src[x, :, k * LANES : (k + 1) * LANES] = G[x, k] * (bend * (inv * inv * inv))
 
 
-def descent(dims, src, big, m2a, m2b, own2, F1c, F0, U0, T0, F1, U1, T1):
+def descent(dims, src, big, m2b, own2, F1c, F0, U0, T0, F1, U1, T1):
     leaves, subs = dims
     i, j, odd_i, odd_j, far_i, far_j = place(leaves, subs)
     nz = src.shape[2] // LANES
@@ -262,7 +262,8 @@
     each(0, 6, restrict1, 3)
 
     at = jnp.where(odd_i, 0, 4)
-    m2a[...] = F1c[pl.ds(at, 2)]
+    for x in (0, 1):
+        big[7, 0:8, x * 2 * LANES : (x + 1) * 2 * LANES] = F1c[at + x]
     m2b[...] = F1c[pl.ds(4 - at, 2)]
     own2[...] = F1c[2:4]
     big[0:4] = src[pl.ds(at, 4)]
@@ -277,12 +278,13 @@
     return ref[4 + p % 3, :, (p // 3) * n : (p // 3 + 1) * n]
 
 
-def middle(dims, own2, r2a, r2b, src, big, ra, out, to_b):
+def middle(dims, own2, r2b, src, big, ra, out, to_b):
     _, _, odd_i, _, far_i, _ = place(*dims)
     n = src.shape[2] // 2
-    v = own2[...] + r2a[...] + jnp.where(far_i, r2b[...], 0.0)
-    for k in range(out.shape[0]):
-        out[k] = v
+    for x in (0, 1):
+        v = own2[x] + ra[7, 0:8, x * 2 * LANES : (x + 1) * 2 * LANES] + jnp.where(far_i, r2b[x], 0.0)
+        for k in range(out.shape[0]):
+            out[k, x] = v
     to_b[0:4] = src[pl.ds(jnp.where(odd_i, 4, 0), 4)]
     more = {
         0: jnp.where(odd_i, half_planes(ra, 4), 0.0),
@@ -605,31 +607,35 @@
             res.append(F0[x + 4, k, 4:20, :] - 6.0 * u[k] + (near + (before[k] + after[k])))
         put(resid, x, res)
 
-    copies = []
-
-    def away(t, a, b, x):
-        copies.append(pltpu.make_async_copy(a.at[pl.ds(x, 4)], b.at[pl.ds(x, 4)], done.at[t, x // 4]))
-        copies[-1].start()
-
-    each(0, NX, lambda x: put(press, x, [V0[x + 4, k, 4:20, :] for k in range(nz)]), 4)
-    for x in (0, 4):
-        away(0, press, press_out, x)
-    each(0, NX, rest, 4)
-    for x in (0, 4):
-        away(1, resid, resid_out, x)
-    for copy in copies:
-        copy.wait()
-
-
-def call(kernel, outs, scratch, *args, here=(), away=False, mib=4):
-    vmem, hbm = pl.BlockSpec(), pl.BlockSpec(memory_space=pltpu.HBM)
+    def away(t, a, b, s):
+        return pltpu.make_async_copy(a.at[pl.ds(4 * s, 4)], b.at[pl.ds(4 * s, 4)], done.at[t, s])
+
+    def give(s):
+        for x in range(4):
+            put(press, 4 * s + x, [V0[4 * s + x + 4, k, 4:20, :] for k in range(nz)])
+        away(0, press, press_out, s).start()
+
+    def give_rest(s):
+        for x in range(4):
+            rest(4 * s + x)
+        away(1, resid, resid_out, s).start()
+
+    each(0, NX // 4, give)
+    each(0, NX // 4, give_rest)
+    for s in range(NX // 4):
+        away(0, press, press_out, s).wait()
+        away(1, resid, resid_out, s).wait()
+
+
+def call(kernel, outs, scratch, *args, away=False, mib=4, us=0.0):
+    cost = pl.CostEstimate(flops=0, transcendentals=0, bytes_accessed=int(us * 3.6e6)) if us else None
     return pl.pallas_call(
         kernel,
         out_shape=[jax.ShapeDtypeStruct(s, f32) for s in outs],
-        in_specs=[hbm if n in here else vmem for n in range(len(args))],
-        out_specs=[hbm if away else vmem for _ in outs],
+        out_specs=[pl.BlockSpec(memory_space=pltpu.HBM) if away else pl.BlockSpec() for _ in outs],
         scratch_shapes=[pltpu.VMEM(s, f32) if isinstance(s, tuple) else s for s in scratch],
         compiler_params=pltpu.CompilerParams(vmem_limit_bytes=mib * 1024 * 1024),
+        cost_estimate=cost,
     )(*args)
 
 
@@ -670,12 +676,12 @@
     to_a, to_b, to_1, to_2 = call(functools.partial(edges, dims), [plane, plane, rows, rows], [], volume_fraction)
     halos = move(to_a, pa), move(to_b, pb), move(to_1, ps1), move(to_2, ps2)
     shape = (NX, nz, NY, LANES)
-    scratch = [pltpu.VMEM((NX, NY, depth), jnp.int32), pltpu.SemaphoreType.DMA]
-    heights, slope = call(columns, [shape, shape], scratch, volume_fraction, interface_mask, here=(1,))
+    heights, slope = call(columns, [shape, shape], [], volume_fraction, us=1.5)
+    (slope,) = call(masked, [shape], [], slope, interface_mask)
     (src,) = call(functools.partial(source, dims), [(NX, NY, depth)], [], heights, slope, *halos)
-    big, m2a, m2b, own2 = call(
+    big, m2b, own2 = call(
         functools.partial(descent, dims),
-        [(7, NY, depth)] + [(2, 8, depth // 4)] * 3,
+        [(8, NY, depth)] + [(2, 8, depth // 4)] * 2,
         [
             (6, 8, depth // 4),
             (16, nz, 24, LANES),
@@ -688,9 +694,9 @@
         src,
         mib=10,
     )
-    r2a, r2b, ra = move(m2a, pa), move(m2b, pb), move(big, pa)
+    r2b, ra = move(m2b, pb), move(big, pa)
     out, to_b = call(
-        functools.partial(middle, dims), [(2 * subs, 2, 8, depth // 4), (7, NY, depth)], [], own2, r2a, r2b, src, big, ra
+        functools.partial(middle, dims), [(2 * subs, 2, 8, depth // 4), (7, NY, depth)], [], own2, r2b, src, big, ra
     )
     rb = move(to_b, pb)
     group = [list(range(k, k + 2 * subs)) for k in range(0, leaves * subs, 2 * subs)]

time: 57.8 us -> 57.3 us (level)
    pallas_call x10 -> x11, Pallas kernels: 13 us -> 12.8 us  [call(): pl.pallas_call(kernel, out_shape=[jax.ShapeDtypeStruct(s, f32) for s in o...]
    ppermute x14 -> x13, starting transfers between devices: 9.43 us -> 9.39 us  [shards(): move = lambda v, table: lax.ppermute(v, AXES, table)]
    ppermute x14 -> x13, waiting for transfers between devices: 4.04 us -> 4.06 us  [shards(): move = lambda v, table: lax.ppermute(v, AXES, table)]
  transfers between devices with their start and end apart: 15 -> 14, of which waited for: 4 -> 3; matrix products, arithmetic and copies ran while one was open for 0% -> 0% of each run, Pallas kernels for 8% -> 8%
where the time goes in v5:
time: 57.3 us; the launch traced here: 56.9 us
  starting transfers between devices  20.7 us (36%)
  Pallas kernels  12.8 us (22%)
  blocking collectives  10.3 us (18%)
  waiting for transfers between devices  10.2 us (18%)
  local copies, waits for them, and re-layouts  2.09 us (4%)
  between operations  0.8 us (1%)
    pallas_call x11, Pallas kernels, call(): pl.pallas_call(kernel, out_shape=[jax.ShapeDtypeStruct(s, f32) for s in o...  12.8 us
    all_to_all x1, starting transfers between devices, shards(): got = lax.all_to_all(out, AXES, 0, 0, axis_index_groups=group)  11.3 us
    all_to_all x1, blocking collectives, shards(): got = lax.all_to_all(out, AXES, 0, 0, axis_index_groups=group)  10.3 us
    ppermute x13, starting transfers between devices, shards(): move = lambda v, table: lax.ppermute(v, AXES, table)  9.39 us
    all_to_all x1, waiting for transfers between devices, shards(): got = lax.all_to_all(out, AXES, 0, 0, axis_index_groups=group)  6.15 us
    ppermute x13, waiting for transfers between devices, shards(): move = lambda v, table: lax.ppermute(v, AXES, table)  4.06 us
    unnamed x4, local copies, waits for them, and re-layouts  2.07 us
  transfers between devices with their start and end apart: 14, of which 3 were waited for; matrix products, arithmetic and copies ran while one was open for 0% of the time, Pallas kernels for 8%

profile of v5, /device:TPU:2, one launch (start us, length us, event | category | flops | bytes accessed | tf_op | source)
XLA Modules:
  0.0 56.9 jit_solution(14083924377719138018)
XLA Ops:
  0.6 0.0 copy-start
  0.6 1.0 %copy-done = f32[8,16,1024]{2,1,0:T(8,128)S(1)} copy-done((f32[8,16,1024]{2,1,0:T(8,128)S(1)}, f32[8,16,1024]{2,1,0:T(8,128)}, u32[]{:S(2)}) %copy-start) | copy-done | bytes 524312
  1.7 0.1 collective-permute-start
  1.8 0.5 collective-permute-start.1
  2.3 1.6 %collective-permute-start.2 = (f32[8,1024]{1,0:T(8,128)S(1)}, f32[8,1024]{1,0:T(8,128)S(1)}, u32[]{:S(2)}, u32[]{:S(2)}) collective-permute-start(f32[8,1024]{1,0:T(8,128)S(1)} %get-tuple-element.32), channel_id=1, source_target_pairs={{0,1},{1,0},{2,3},{3,2},{4,5},{5,4},{6,7},{7,6},{8,9},{9,8},{10,11... | collective-permute-start | bytes 98312 | tf_op jit(solution)/shard_map/ppermute | solution.py:672
  3.9 1.5 %collective-permute-start.3 = (f32[8,1024]{1,0:T(8,128)S(1)}, f32[8,1024]{1,0:T(8,128)S(1)}, u32[]{:S(2)}, u32[]{:S(2)}) collective-permute-start(f32[8,1024]{1,0:T(8,128)S(1)} %get-tuple-element.33), channel_id=1, source_target_pairs={{0,4},{1,2},{2,1},{3,7},{4,0},{5,6},{6,5},{7,3},{8,12},{9,10},{10,... | collective-permute-start | bytes 98312 | tf_op jit(solution)/shard_map/ppermute | solution.py:672
  5.4 0.8 %shard_map.41 = (f32[8,8,16,128]{3,2,1,0:T(8,128)S(1)}, f32[8,8,16,128]{3,2,1,0:T(8,128)S(1)}) custom-call(f32[8,16,1024]{2,1,0:T(8,128)S(1)} %copy-done), custom_call_target="tpu_custom_call" | custom-call | bytes 5400000 | tf_op jit(solution)/shard_map/pallas_call | solution.py:632
  6.2 0.0 copy-start.1
  6.2 1.0 %copy-done.1 = s32[8,16,1024]{2,1,0:T(8,128)S(1)} copy-done((s32[8,16,1024]{2,1,0:T(8,128)S(1)}, s32[8,16,1024]{2,1,0:T(8,128)}, u32[]{:S(2)}) %copy-start.1) | copy-done | bytes 524312
  7.2 0.6 %shard_map.42.G = f32[8,8,16,128]{3,2,1,0:T(8,128)S(1)} custom-call(f32[8,8,16,128]{3,2,1,0:T(8,128)S(1)} %get-tuple-element.29.G, s32[8,16,1024]{2,1,0:T(8,128)S(1)} %copy-done.1), custom_call_target="tpu_custom_call" | custom-call | tf_op jit(solution)/shard_map/pallas_call | solution.py:632
  7.9 0.0 collective-permute-done.2.rs1
  7.9 0.0 collective-permute-done.3.rs2
  7.9 0.0 collective-permute-done.ra
  7.9 0.0 collective-permute-done.1.rb
  7.9 0.7 %shard_map.44.src = f32[8,16,1024]{2,1,0:T(8,128)S(1)} custom-call(f32[8,8,16,128]{3,2,1,0:T(8,128)S(1)} %get-tuple-element.28.H, f32[8,8,16,128]{3,2,1,0:T(8,128)S(1)} %shard_map.42.G, f32[1,16,1024]{2,1,0:T(8,128)S(1)} %collective-permute-done.ra, f32[1,16,1024]{2,1,0:T(8,128)S(1)} %collective-permute-done.1.rb, f32[8,1024]{1,0:T(8,128)S(1)} %collective-permute-done.2.rs1, ...), custom_call_target="tpu_custom_call" | custom-call | tf_op jit(solution)/shard_map/pallas_call | solution.py:632
  8.6 2.0 %shard_map.45 = (f32[8,16,1024]{2,1,0:T(8,128)S(1)}, f32[2,8,256]{2,1,0:T(8,128)S(1)}, f32[2,8,256]{2,1,0:T(8,128)S(1)}) custom-call(f32[8,16,1024]{2,1,0:T(8,128)S(1)} %shard_map.44.src), custom_call_target="tpu_custom_call" | custom-call | tf_op jit(solution)/shard_map/pallas_call | solution.py:632
  10.6 0.4 collective-permute-start.5
  11.0 0.0 collective-permute-start.4
  11.0 3.7 %collective-permute-done.4.r2b = f32[2,8,256]{2,1,0:T(8,128)S(1)} collective-permute-done((f32[2,8,256]{2,1,0:T(8,128)S(1)}, f32[2,8,256]{2,1,0:T(8,128)S(1)}, u32[]{:S(2)}, u32[]{:S(2)}) %collective-permute-start.4) | collective-permute-done | bytes 16416 | tf_op jit(solution)/shard_map/ppermute | solution.py:672
  14.7 0.0 collective-permute-done.5.ra
  14.7 0.1 shard_map.46
  14.8 0.1 collective-permute-start.6
  14.9 10.3 %all_to_all.10.got = f32[8,2,8,256]{3,2,1,0:T(8,128)S(1)} all-to-all(f32[8,2,8,256]{3,2,1,0:T(8,128)S(1)} %get-tuple-element.37), channel_id=1, replica_groups={{0,1,2,3,4,5,6,7},{8,9,10,11,12,13,14,15},{16,17,18,19,20,21,22,23},{24..., dimensions={0} | all-to-all | bytes 262144 | tf_op jit(solution)/shard_map/all_to_all | solution.py:703
  25.2 0.0 collective-permute-done.6.rb
  25.2 0.2 collective-permute-start.7
  25.4 1.0 %shard_map.47 = (f32[4,16,256]{2,1,0:T(8,128)S(1)}, f32[1,16,256]{2,1,0:T(8,128)S(1)}, f32[16,4,8,128]{3,2,1,0:T(8,128)}) custom-call(f32[8,2,8,256]{3,2,1,0:T(8,128)S(1)} %all_to_all.10.got), custom_call_target="tpu_custom_call" | custom-call | tf_op jit(solution)/shard_map/pallas_call | solution.py:632
  26.4 0.3 collective-permute-done.7.far
  26.7 1.2 %shard_map.48 = (f32[14,16,512]{2,1,0:T(8,128)S(1)}, f32[15,8,1024]{2,1,0:T(8,128)}, f32[15,8,1024]{2,1,0:T(8,128)}) custom-call(f32[8,16,1024]{2,1,0:T(8,128)S(1)} %shard_map.44.src, f32[8,16,1024]{2,1,0:T(8,128)S(1)} %get-tuple-element.36.big, f32[8,16,1024]{2,1,0:T(8,128)S(1)} %collective-permute-done.5.ra, f32[7,16,1024]{2,1,0:T(8,128)S(1)} %collective-permute-done.6.rb, ...), custom_call_target="tpu_custom_call" | custom-call | tf_op jit(solution)/shard_map/pallas_call | solution.py:632
  27.9 0.3 collective-permute-start.11
  28.2 1.3 %collective-permute-start.12 = (f32[15,8,1024]{2,1,0:T(8,128)}, f32[15,8,1024]{2,1,0:T(8,128)S(1)}, u32[]{:S(2)}, u32[]{:S(2)}) collective-permute-start(f32[15,8,1024]{2,1,0:T(8,128)} %get-tuple-element.49), channel_id=1, source_target_pairs={{0,4},{1,2},{2,1},{3,7},{4,0},{5,6},{6,5},{7,3},{8,12},{9,10},{10,... | collective-permute-start | bytes 1474568 | tf_op jit(solution)/shard_map/ppermute | solution.py:672
  29.6 11.3 %all-to-all-start.1 = ((f32[16,4,8,128]{3,2,1,0:T(8,128)}), f32[16,4,8,128]{3,2,1,0:T(8,128)S(1)}, u32[]{:S(2)}, u32[]{:S(2)}) async-start(f32[16,4,8,128]{3,2,1,0:T(8,128)} %get-tuple-element.44), calls=%async_computation.1 | async-start | bytes 524288 | tf_op jit(solution)/shard_map/all_to_all | solution.py:726
  40.9 0.1 collective-permute-start.9
  41.0 3.3 %collective-permute-start.8 = (f32[4,16,256]{2,1,0:T(8,128)S(1)}, f32[4,16,256]{2,1,0:T(8,128)S(1)}, u32[]{:S(2)}, u32[]{:S(2)}) collective-permute-start(f32[4,16,256]{2,1,0:T(8,128)S(1)} %get-tuple-element.45.f2), channel_id=1, source_target_pairs={{0,8},{1,9},{2,10},{3,11},{4,12},{5,13},{6,14},{7,15},{8,0},{9,1},... | collective-permute-start | bytes 196616 | tf_op jit(solution)/shard_map/ppermute | solution.py:672
  44.3 0.0 collective-permute-start.10
  44.3 6.1 %all-to-all-done.1.got = f32[16,4,8,128]{3,2,1,0:T(8,128)S(1)} async-done(((f32[16,4,8,128]{3,2,1,0:T(8,128)}), f32[16,4,8,128]{3,2,1,0:T(8,128)S(1)}, u32[]{:S(2)}, u32[]{:S(2)}) %all-to-all-start.1) | async-done | bytes 262176 | tf_op jit(solution)/shard_map/all_to_all | solution.py:726
  50.5 0.6 %shard_map.49.u3 = f32[5,8,128]{2,1,0:T(8,128)S(1)} custom-call(f32[16,4,8,128]{3,2,1,0:T(8,128)S(1)} %all-to-all-done.1.got), custom_call_target="tpu_custom_call" | custom-call | tf_op jit(solution)/shard_map/pallas_call | solution.py:632
  51.1 0.0 collective-permute-done.11.rs1
  51.1 0.0 collective-permute-done.12.rs2
  51.1 1.4 %shard_map.50 = (f32[16,8,24,128]{3,2,1,0:T(8,128)S(1)}, f32[16,8,24,128]{3,2,1,0:T(8,128)S(1)}, f32[14,4,24,128]{3,2,1,0:T(8,128)S(1)}, f32[14,4,24,128]{3,2,1,0:T(8,128)S(1)}) custom-call(f32[8,16,1024]{2,1,0:T(8,128)S(1)} %shard_map.44.src, f32[8,16,1024]{2,1,0:T(8,128)S(1)} %collective-permute-done.5.ra, f32[7,16,1024]{2,1,0:T(8,128)S(1)} %collective-permute-done.6.rb, ...), custom_call_target="tpu_custom_call" | custom-call | tf_op jit(solution)/shard_map/pallas_call | solution.py:632
  52.5 0.0 collective-permute-done.10.r2e
  52.5 0.0 collective-permute-done.9.r2c2
  52.5 0.0 collective-permute-done.8.r2c1
  52.5 4.4 %shard_map.51 = (f32[8,16,1024]{2,1,0:T(8,128)}, f32[8,16,1024]{2,1,0:T(8,128)}) custom-call(f32[5,8,128]{2,1,0:T(8,128)S(1)} %shard_map.49.u3, f32[4,16,256]{2,1,0:T(8,128)S(1)} %get-tuple-element.45.f2, f32[4,16,256]{2,1,0:T(8,128)S(1)} %collective-permute-done.8.r2c1, f32[4,16,256]{2,1,0:T(8,128)S(1)} %collective-permute-done.9.r2c2, ...), custom_call_target="tpu_custom_call" | custom-call | tf_op jit(solution)/shard_map/pallas_call | solution.py:632
  (2 shorter events, 0.0 us)
Async XLA Ops:
  0.6 1.0 %copy-start = (f32[8,16,1024]{2,1,0:T(8,128)S(1)}, f32[8,16,1024]{2,1,0:T(8,128)}, u32[]{:S(2)}) copy-start(f32[8,16,1024]{2,1,0:T(8,128)} %vf.3) | copy-start | bytes 1572868
  1.7 6.2 %collective-permute-start = (f32[1,16,1024]{2,1,0:T(8,128)S(1)}, f32[1,16,1024]{2,1,0:T(8,128)S(1)}, u32[]{:S(2)}, u32[]{:S(2)}) collective-permute-start(f32[1,16,1024]{2,1,0:T(8,128)S(1)} %get-tuple-element.30), channel_id=1, source_target_pairs={{0,4},{1,5},{2,6},{3,7},{4,0},{5,1},{6,2},{7,3},{8,12},{9,13},{10,... | collective-permute-start | bytes 196616 | tf_op jit(solution)/shard_map/ppermute | solution.py:672
  1.8 6.1 %collective-permute-start.1 = (f32[1,16,1024]{2,1,0:T(8,128)S(1)}, f32[1,16,1024]{2,1,0:T(8,128)S(1)}, u32[]{:S(2)}, u32[]{:S(2)}) collective-permute-start(f32[1,16,1024]{2,1,0:T(8,128)S(1)} %get-tuple-element.31), channel_id=1, source_target_pairs={{0,1},{1,0},{2,3},{3,2},{4,8},{5,9},{6,10},{7,11},{8,4},{9,5},{10,... | collective-permute-start | bytes 196616 | tf_op jit(solution)/shard_map/ppermute | solution.py:672
  2.3 5.6 %collective-permute-start.2 = (f32[8,1024]{1,0:T(8,128)S(1)}, f32[8,1024]{1,0:T(8,128)S(1)}, u32[]{:S(2)}, u32[]{:S(2)}) collective-permute-start(f32[8,1024]{1,0:T(8,128)S(1)} %get-tuple-element.32), channel_id=1, source_target_pairs={{0,1},{1,0},{2,3},{3,2},{4,5},{5,4},{6,7},{7,6},{8,9},{9,8},{10,11... | collective-permute-start | bytes 98312 | tf_op jit(solution)/shard_map/ppermute | solution.py:672
  3.9 4.0 %collective-permute-start.3 = (f32[8,1024]{1,0:T(8,128)S(1)}, f32[8,1024]{1,0:T(8,128)S(1)}, u32[]{:S(2)}, u32[]{:S(2)}) collective-permute-start(f32[8,1024]{1,0:T(8,128)S(1)} %get-tuple-element.33), channel_id=1, source_target_pairs={{0,4},{1,2},{2,1},{3,7},{4,0},{5,6},{6,5},{7,3},{8,12},{9,10},{10,... | collective-permute-start | bytes 98312 | tf_op jit(solution)/shard_map/ppermute | solution.py:672
  6.2 1.0 %copy-start.1 = (s32[8,16,1024]{2,1,0:T(8,128)S(1)}, s32[8,16,1024]{2,1,0:T(8,128)}, u32[]{:S(2)}) copy-start(s32[8,16,1024]{2,1,0:T(8,128)} %mask.1) | copy-start | bytes 1572868
  10.6 4.1 %collective-permute-start.5 = (f32[8,16,1024]{2,1,0:T(8,128)S(1)}, f32[8,16,1024]{2,1,0:T(8,128)S(1)}, u32[]{:S(2)}, u32[]{:S(2)}) collective-permute-start(f32[8,16,1024]{2,1,0:T(8,128)S(1)} %get-tuple-element.36.big), channel_id=1, source_target_pairs={{0,4},{1,5},{2,6},{3,7},{4,0},{5,1},{6,2},{7,3},{8,12},{9,13},{10,... | collective-permute-start | bytes 1572872 | tf_op jit(solution)/shard_map/ppermute | solution.py:672
  11.0 3.7 %collective-permute-start.4 = (f32[2,8,256]{2,1,0:T(8,128)S(1)}, f32[2,8,256]{2,1,0:T(8,128)S(1)}, u32[]{:S(2)}, u32[]{:S(2)}) collective-permute-start(f32[2,8,256]{2,1,0:T(8,128)S(1)} %get-tuple-element.35), channel_id=1, source_target_pairs={{0,1},{1,0},{2,3},{3,2},{4,8},{5,9},{6,10},{7,11},{8,4},{9,5},{10,... | collective-permute-start | bytes 49160 | tf_op jit(solution)/shard_map/ppermute | solution.py:672
  14.8 10.4 %collective-permute-start.6 = (f32[7,16,1024]{2,1,0:T(8,128)S(1)}, f32[7,16,1024]{2,1,0:T(8,128)S(1)}, u32[]{:S(2)}, u32[]{:S(2)}) collective-permute-start(f32[7,16,1024]{2,1,0:T(8,128)S(1)} %get-tuple-element.38), channel_id=1, source_target_pairs={{0,1},{1,0},{2,3},{3,2},{4,8},{5,9},{6,10},{7,11},{8,4},{9,5},{10,... | collective-permute-start | bytes 1376264 | tf_op jit(solution)/shard_map/ppermute | solution.py:672
  25.2 1.5 %collective-permute-start.7 = (f32[3,16,1024]{2,1,0:T(8,128)S(1)}, f32[3,16,1024]{2,1,0:T(8,128)S(1)}, u32[]{:S(2)}, u32[]{:S(2)}) collective-permute-start(f32[3,16,1024]{2,1,0:T(8,128)S(1)} %slice.3), channel_id=1, source_target_pairs={{0,4},{1,5},{2,6},{3,7},{4,0},{5,1},{6,2},{7,3},{8,12},{9,13},{10,... | collective-permute-start | bytes 589832 | tf_op jit(solution)/shard_map/ppermute | solution.py:672
  27.9 23.2 %collective-permute-start.11 = (f32[15,8,1024]{2,1,0:T(8,128)}, f32[15,8,1024]{2,1,0:T(8,128)S(1)}, u32[]{:S(2)}, u32[]{:S(2)}) collective-permute-start(f32[15,8,1024]{2,1,0:T(8,128)} %get-tuple-element.48), channel_id=1, source_target_pairs={{0,1},{1,0},{2,3},{3,2},{4,5},{5,4},{6,7},{7,6},{8,9},{9,8},{10,11... | collective-permute-start | bytes 1474568 | tf_op jit(solution)/shard_map/ppermute | solution.py:672
  28.2 22.9 %collective-permute-start.12 = (f32[15,8,1024]{2,1,0:T(8,128)}, f32[15,8,1024]{2,1,0:T(8,128)S(1)}, u32[]{:S(2)}, u32[]{:S(2)}) collective-permute-start(f32[15,8,1024]{2,1,0:T(8,128)} %get-tuple-element.49), channel_id=1, source_target_pairs={{0,4},{1,2},{2,1},{3,7},{4,0},{5,6},{6,5},{7,3},{8,12},{9,10},{10,... | collective-permute-start | bytes 1474568 | tf_op jit(solution)/shard_map/ppermute | solution.py:672
  29.6 20.9 %all-to-all-start.1 = ((f32[16,4,8,128]{3,2,1,0:T(8,128)}), f32[16,4,8,128]{3,2,1,0:T(8,128)S(1)}, u32[]{:S(2)}, u32[]{:S(2)}) async-start(f32[16,4,8,128]{3,2,1,0:T(8,128)} %get-tuple-element.44), calls=%async_computation.1 | async-start | bytes 524288 | tf_op jit(solution)/shard_map/all_to_all | solution.py:726
  40.9 11.6 %collective-permute-start.9 = (f32[4,16,256]{2,1,0:T(8,128)S(1)}, f32[4,16,256]{2,1,0:T(8,128)S(1)}, u32[]{:S(2)}, u32[]{:S(2)}) collective-permute-start(f32[4,16,256]{2,1,0:T(8,128)S(1)} %get-tuple-element.45.f2), channel_id=1, source_target_pairs={{0,4},{1,5},{2,6},{3,7},{4,0},{5,1},{6,2},{7,3},{8,16},{9,17},{10,... | collective-permute-start | bytes 196616 | tf_op jit(solution)/shard_map/ppermute | solution.py:672
  41.0 11.5 %collective-permute-start.8 = (f32[4,16,256]{2,1,0:T(8,128)S(1)}, f32[4,16,256]{2,1,0:T(8,128)S(1)}, u32[]{:S(2)}, u32[]{:S(2)}) collective-permute-start(f32[4,16,256]{2,1,0:T(8,128)S(1)} %get-tuple-element.45.f2), channel_id=1, source_target_pairs={{0,8},{1,9},{2,10},{3,11},{4,12},{5,13},{6,14},{7,15},{8,0},{9,1},... | collective-permute-start | bytes 196616 | tf_op jit(solution)/shard_map/ppermute | solution.py:672
  44.3 8.2 %collective-permute-start.10 = (f32[1,16,256]{2,1,0:T(8,128)S(1)}, f32[1,16,256]{2,1,0:T(8,128)S(1)}, u32[]{:S(2)}, u32[]{:S(2)}) collective-permute-start(f32[1,16,256]{2,1,0:T(8,128)S(1)} %get-tuple-element.46), channel_id=1, source_target_pairs={{0,8},{1,9},{2,10},{3,11},{4,16},{5,17},{6,18},{7,19},{8,0},{9,1},... | collective-permute-start | bytes 49160 | tf_op jit(solution)/shard_map/ppermute | solution.py:672

commit v6 on v5

--- a/solution.py
+++ b/solution.py
@@ -129,10 +129,10 @@
     _, _, odd_i, odd_j, _, _ = place(*dims)
     to_a[0] = vf[jnp.where(odd_i, 0, NX - 1)]
     to_b[0] = vf[jnp.where(odd_i, NX - 1, 0)]
-    for x in range(NX):
-        first, last = vf[x, 0:1, :], vf[x, NY - 1 : NY, :]
-        to_1[x : x + 1, :] = jnp.where(odd_j, first, last)
-        to_2[x : x + 1, :] = jnp.where(odd_j, last, first)
+    first = jnp.concatenate([vf[x, 0:1, :] for x in range(NX)], axis=0)
+    last = jnp.concatenate([vf[x, NY - 1 : NY, :] for x in range(NX)], axis=0)
+    to_1[...] = jnp.where(odd_j, first, last)
+    to_2[...] = jnp.where(odd_j, last, first)
 
 
 def columns(vf, H, G):
@@ -192,9 +192,8 @@
     for x in range(16):
         for k in range(nz):
             if 4 <= x < 12:
-                F0[x, k, 0:4, :] = zero24[0:4]
-                F0[x, k, 4:20, :] = src[x - 4, :, k * LANES : (k + 1) * LANES]
-                F0[x, k, 20:24, :] = zero24[0:4]
+                own = src[x - 4, :, k * LANES : (k + 1) * LANES]
+                F0[x, k] = jnp.concatenate([zero[0:4], own, zero[0:4]], axis=0)
             else:
                 F0[x, k] = zero24
 
@@ -210,7 +209,7 @@
         for k in range(nz):
             U0[x, k] = (C1 * f[k] + C2 * around_f[k]) * m
 
-    each(3, 13, smooth0, 5)
+    each(3, 13, smooth0, 10)
 
     for x in range(0, 14):
         if x < 4 or x >= 10:
@@ -225,13 +224,11 @@
             u, around_u = around(U0, x)
             total = [total[k] + (F0[x, k] - 6.0 * u[k] + around_u[k]) * m for k in range(nz)]
         for k in range(nz):
-            T0[c, k] = total[k]
+            T0[c, k, 0:24, :] = total[k]
         for k, v in enumerate(restricted(T0.at[c], 12)):
-            F1[c + 3, k, 0:2, :] = zero[0:2]
-            F1[c + 3, k, 2:14, :] = v
-            F1[c + 3, k, 14:16, :] = zero[0:2]
-
-    each(1, 7, restrict0, 2)
+            F1[c + 3, k] = jnp.concatenate([zero[0:2], v, zero[0:2]], axis=0)
+
+    each(1, 7, restrict0, 6)
 
     n1 = nz // 2
     my1 = row_mask(16, j * (NY // 2) - 4, count_y // 2)
@@ -245,7 +242,7 @@
         for k in range(n1):
             U1[x, k] = (C1 * f[k] + C2 * around_f[k]) * m
 
-    each(3, 11, smooth1, 4)
+    each(3, 11, smooth1, 8)
 
     def restrict1(c):
         total = [zero] * n1
@@ -259,7 +256,7 @@
         for k, v in enumerate(restricted(T1.at[c], 8)):
             F1c[c, :, k * LANES : (k + 1) * LANES] = v
 
-    each(0, 6, restrict1, 3)
+    each(0, 6, restrict1, 6)
 
     at = jnp.where(odd_i, 0, 4)
     for x in (0, 1):
@@ -380,8 +377,7 @@
     for x in range(8):
         u, v = fine(x), fine(x + 8)
         for out, up in ((s1, odd_j == False), (s2, odd_j)):
-            out[x, 0:4, :] = jnp.where(up, u[12:16], u[0:4])
-            out[x, 4:8, :] = jnp.where(up, v[12:16], v[0:4])
+            out[x] = jnp.concatenate([jnp.where(up, u[12:16], u[0:4]), jnp.where(up, v[12:16], v[0:4])], axis=0)
     for x in range(14):
         v = planes[x - 5]
         s = slice((x // 7) * n, (x // 7 + 1) * n)
@@ -466,7 +462,7 @@
         for k in range(n1):
             P1[x, k] = (C1 * f[k] + C2 * around_f[k]) * m
 
-    each(1, 13, smooth1, 4)
+    each(1, 13, smooth1, 12)
 
     def fill0(x):
         if 4 <= x < 12:
@@ -481,9 +477,7 @@
         hi = jnp.where(odd_j, b[h : h + 4], a[h : h + 4]) * high_j
         for k in range(nz):
             s = slice(k * LANES, (k + 1) * LANES)
-            F0[x, k, 0:4, :] = lo[:, s]
-            F0[x, k, 4:20, :] = v[:, s]
-            F0[x, k, 20:24, :] = hi[:, s]
+            F0[x, k] = jnp.concatenate([lo[:, s], v[:, s], hi[:, s]], axis=0)
 
     for x in range(16):
         fill0(x)
@@ -495,7 +489,7 @@
         for k in range(nz):
             P0[x, k] = (C1 * f[k] + C2 * around_f[k]) * m
 
-    each(1, 15, smooth0, 4)
+    each(1, 15, smooth0, 7)
 
 
 def ascent(dims, u3, f2, r2c1, r2c2, r2e, F0, P0, F1, P1, press_out, resid_out, F2, T2, W2, X2, T1, V1, X1, T0, V0, X0, press, resid, done):
@@ -562,7 +556,7 @@
             for k in range(n1):
                 new[x, k] = (C0 * u[k] + D * (F1[x, k] + around_u[k])) * m
 
-        each(lo, hi, body, (hi - lo) // 2)
+        each(lo, hi, body, hi - lo)
 
     sweep1(V1, X1, 2, 12)
     sweep1(X1, V1, 3, 11)
@@ -578,7 +572,7 @@
     def smooth0(x):
         m = plane_mask(my0, i * NX + x - 4, count_x)
         for k in range(nz):
-            V0[x, k] = P0[x, k] + T0[x // 2, k // 2] * m
+            V0[x, k] = P0[x, k] + T0[x // 2, k // 2, 0:24, :] * m
 
     each(1, 15, smooth0, 4)
 
@@ -686,7 +680,7 @@
             (6, 8, depth // 4),
             (16, nz, 24, LANES),
             (16, nz, 24, LANES),
-            (8, nz, 24, LANES),
+            (8, nz, 32, LANES),
             (14, n1, 16, LANES),
             (14, n1, 16, LANES),
             (6, n1, 16, LANES),
@@ -739,7 +733,7 @@
             (6, n2, 24, LANES),
             shape1,
             shape1,
-            (8, n1, 24, LANES),
+            (8, n1, 32, LANES),
             shape0,
             shape0,
             (NX, NY, depth),

time: 57.3 us -> 56.5 us (0.986)
  Pallas kernels: 12.8 us -> 12 us
    pallas_call x11, Pallas kernels: 12.8 us -> 12 us  [call(): pl.pallas_call(kernel, out_shape=[jax.ShapeDtypeStruct(s, f32) for s in o...]
where the time goes in v6:
time: 56.5 us; the launch traced here: 56.2 us
  starting transfers between devices  20.7 us (37%)
  Pallas kernels  12 us (21%)
  blocking collectives  10.3 us (18%)
  waiting for transfers between devices  10.2 us (18%)
  local copies, waits for them, and re-layouts  2.09 us (4%)
  between operations  0.79 us (1%)
    pallas_call x11, Pallas kernels, call(): pl.pallas_call(kernel, out_shape=[jax.ShapeDtypeStruct(s, f32) for s in o...  12 us
    all_to_all x1, starting transfers between devices, shards(): got = lax.all_to_all(out, AXES, 0, 0, axis_index_groups=group)  11.3 us
    all_to_all x1, blocking collectives, shards(): got = lax.all_to_all(out, AXES, 0, 0, axis_index_groups=group)  10.3 us
    ppermute x13, starting transfers between devices, shards(): move = lambda v, table: lax.ppermute(v, AXES, table)  9.39 us
    all_to_all x1, waiting for transfers between devices, shards(): got = lax.all_to_all(out, AXES, 0, 0, axis_index_groups=group)  6.15 us
    ppermute x13, waiting for transfers between devices, shards(): move = lambda v, table: lax.ppermute(v, AXES, table)  4.06 us
    unnamed x4, local copies, waits for them, and re-layouts  2.07 us
  transfers between devices with their start and end apart: 14, of which 3 were waited for; matrix products, arithmetic and copies ran while one was open for 0% of the time, Pallas kernels for 8%

profile of v6, /device:TPU:2, one launch (start us, length us, event | category | flops | bytes accessed | tf_op | source)
XLA Modules:
  0.0 56.2 jit_solution(14598243184293562721)
XLA Ops:
  0.6 0.0 copy-start
  0.6 1.0 %copy-done = f32[8,16,1024]{2,1,0:T(8,128)S(1)} copy-done((f32[8,16,1024]{2,1,0:T(8,128)S(1)}, f32[8,16,1024]{2,1,0:T(8,128)}, u32[]{:S(2)}) %copy-start) | copy-done | bytes 524312
  1.7 0.1 shard_map.43
  1.7 0.1 collective-permute-start
  1.8 0.5 collective-permute-start.1
  2.4 1.6 %collective-permute-start.2 = (f32[8,1024]{1,0:T(8,128)S(1)}, f32[8,1024]{1,0:T(8,128)S(1)}, u32[]{:S(2)}, u32[]{:S(2)}) collective-permute-start(f32[8,1024]{1,0:T(8,128)S(1)} %get-tuple-element.32), channel_id=1, source_target_pairs={{0,1},{1,0},{2,3},{3,2},{4,5},{5,4},{6,7},{7,6},{8,9},{9,8},{10,11... | collective-permute-start | bytes 98312 | tf_op jit(solution)/shard_map/ppermute | solution.py:666
  3.9 1.5 %collective-permute-start.3 = (f32[8,1024]{1,0:T(8,128)S(1)}, f32[8,1024]{1,0:T(8,128)S(1)}, u32[]{:S(2)}, u32[]{:S(2)}) collective-permute-start(f32[8,1024]{1,0:T(8,128)S(1)} %get-tuple-element.33), channel_id=1, source_target_pairs={{0,4},{1,2},{2,1},{3,7},{4,0},{5,6},{6,5},{7,3},{8,12},{9,10},{10,... | collective-permute-start | bytes 98312 | tf_op jit(solution)/shard_map/ppermute | solution.py:666
  5.4 0.8 %shard_map.41 = (f32[8,8,16,128]{3,2,1,0:T(8,128)S(1)}, f32[8,8,16,128]{3,2,1,0:T(8,128)S(1)}) custom-call(f32[8,16,1024]{2,1,0:T(8,128)S(1)} %copy-done), custom_call_target="tpu_custom_call" | custom-call | bytes 5400000 | tf_op jit(solution)/shard_map/pallas_call | solution.py:626
  6.2 0.0 copy-start.1
  6.2 1.0 %copy-done.1 = s32[8,16,1024]{2,1,0:T(8,128)S(1)} copy-done((s32[8,16,1024]{2,1,0:T(8,128)S(1)}, s32[8,16,1024]{2,1,0:T(8,128)}, u32[]{:S(2)}) %copy-start.1) | copy-done | bytes 524312
  7.3 0.6 %shard_map.42.G = f32[8,8,16,128]{3,2,1,0:T(8,128)S(1)} custom-call(f32[8,8,16,128]{3,2,1,0:T(8,128)S(1)} %get-tuple-element.29.G, s32[8,16,1024]{2,1,0:T(8,128)S(1)} %copy-done.1), custom_call_target="tpu_custom_call" | custom-call | tf_op jit(solution)/shard_map/pallas_call | solution.py:626
  7.9 0.0 collective-permute-done.2.rs1
  7.9 0.0 collective-permute-done.3.rs2
  7.9 0.0 collective-permute-done.ra
  7.9 0.0 collective-permute-done.1.rb
  8.0 0.7 %shard_map.44.src = f32[8,16,1024]{2,1,0:T(8,128)S(1)} custom-call(f32[8,8,16,128]{3,2,1,0:T(8,128)S(1)} %get-tuple-element.28.H, f32[8,8,16,128]{3,2,1,0:T(8,128)S(1)} %shard_map.42.G, f32[1,16,1024]{2,1,0:T(8,128)S(1)} %collective-permute-done.ra, f32[1,16,1024]{2,1,0:T(8,128)S(1)} %collective-permute-done.1.rb, f32[8,1024]{1,0:T(8,128)S(1)} %collective-permute-done.2.rs1, ...), custom_call_target="tpu_custom_call" | custom-call | tf_op jit(solution)/shard_map/pallas_call | solution.py:626
  8.6 1.3 %shard_map.45 = (f32[8,16,1024]{2,1,0:T(8,128)S(1)}, f32[2,8,256]{2,1,0:T(8,128)S(1)}, f32[2,8,256]{2,1,0:T(8,128)S(1)}) custom-call(f32[8,16,1024]{2,1,0:T(8,128)S(1)} %shard_map.44.src), custom_call_target="tpu_custom_call" | custom-call | tf_op jit(solution)/shard_map/pallas_call | solution.py:626
  10.0 0.4 collective-permute-start.5
  10.4 0.0 collective-permute-start.4
  10.4 3.7 %collective-permute-done.4.r2b = f32[2,8,256]{2,1,0:T(8,128)S(1)} collective-permute-done((f32[2,8,256]{2,1,0:T(8,128)S(1)}, f32[2,8,256]{2,1,0:T(8,128)S(1)}, u32[]{:S(2)}, u32[]{:S(2)}) %collective-permute-start.4) | collective-permute-done | bytes 16416 | tf_op jit(solution)/shard_map/ppermute | solution.py:666
  14.1 0.0 collective-permute-done.5.ra
  14.1 0.1 shard_map.46
  14.2 0.1 collective-permute-start.6
  14.3 10.3 %all_to_all.10.got = f32[8,2,8,256]{3,2,1,0:T(8,128)S(1)} all-to-all(f32[8,2,8,256]{3,2,1,0:T(8,128)S(1)} %get-tuple-element.37), channel_id=1, replica_groups={{0,1,2,3,4,5,6,7},{8,9,10,11,12,13,14,15},{16,17,18,19,20,21,22,23},{24..., dimensions={0} | all-to-all | bytes 262144 | tf_op jit(solution)/shard_map/all_to_all | solution.py:697
  24.6 0.0 collective-permute-done.6.rb
  24.6 0.2 collective-permute-start.7
  24.8 1.0 %shard_map.47 = (f32[4,16,256]{2,1,0:T(8,128)S(1)}, f32[1,16,256]{2,1,0:T(8,128)S(1)}, f32[16,4,8,128]{3,2,1,0:T(8,128)}) custom-call(f32[8,2,8,256]{3,2,1,0:T(8,128)S(1)} %all_to_all.10.got), custom_call_target="tpu_custom_call" | custom-call | tf_op jit(solution)/shard_map/pallas_call | solution.py:626
  25.8 0.3 collective-permute-done.7.far
  26.1 1.2 %shard_map.48 = (f32[14,16,512]{2,1,0:T(8,128)S(1)}, f32[15,8,1024]{2,1,0:T(8,128)}, f32[15,8,1024]{2,1,0:T(8,128)}) custom-call(f32[8,16,1024]{2,1,0:T(8,128)S(1)} %shard_map.44.src, f32[8,16,1024]{2,1,0:T(8,128)S(1)} %get-tuple-element.36.big, f32[8,16,1024]{2,1,0:T(8,128)S(1)} %collective-permute-done.5.ra, f32[7,16,1024]{2,1,0:T(8,128)S(1)} %collective-permute-done.6.rb, ...), custom_call_target="tpu_custom_call" | custom-call | tf_op jit(solution)/shard_map/pallas_call | solution.py:626
  27.3 0.3 collective-permute-start.11
  27.6 1.3 %collective-permute-start.12 = (f32[15,8,1024]{2,1,0:T(8,128)}, f32[15,8,1024]{2,1,0:T(8,128)S(1)}, u32[]{:S(2)}, u32[]{:S(2)}) collective-permute-start(f32[15,8,1024]{2,1,0:T(8,128)} %get-tuple-element.49), channel_id=1, source_target_pairs={{0,4},{1,2},{2,1},{3,7},{4,0},{5,6},{6,5},{7,3},{8,12},{9,10},{10,... | collective-permute-start | bytes 1474568 | tf_op jit(solution)/shard_map/ppermute | solution.py:666
  29.0 11.3 %all-to-all-start.1 = ((f32[16,4,8,128]{3,2,1,0:T(8,128)}), f32[16,4,8,128]{3,2,1,0:T(8,128)S(1)}, u32[]{:S(2)}, u32[]{:S(2)}) async-start(f32[16,4,8,128]{3,2,1,0:T(8,128)} %get-tuple-element.44), calls=%async_computation.1 | async-start | bytes 524288 | tf_op jit(solution)/shard_map/all_to_all | solution.py:720
  40.3 0.1 collective-permute-start.9
  40.4 3.3 %collective-permute-start.8 = (f32[4,16,256]{2,1,0:T(8,128)S(1)}, f32[4,16,256]{2,1,0:T(8,128)S(1)}, u32[]{:S(2)}, u32[]{:S(2)}) collective-permute-start(f32[4,16,256]{2,1,0:T(8,128)S(1)} %get-tuple-element.45.f2), channel_id=1, source_target_pairs={{0,8},{1,9},{2,10},{3,11},{4,12},{5,13},{6,14},{7,15},{8,0},{9,1},... | collective-permute-start | bytes 196616 | tf_op jit(solution)/shard_map/ppermute | solution.py:666
  43.7 0.0 collective-permute-start.10
  43.7 6.1 %all-to-all-done.1.got = f32[16,4,8,128]{3,2,1,0:T(8,128)S(1)} async-done(((f32[16,4,8,128]{3,2,1,0:T(8,128)}), f32[16,4,8,128]{3,2,1,0:T(8,128)S(1)}, u32[]{:S(2)}, u32[]{:S(2)}) %all-to-all-start.1) | async-done | bytes 262176 | tf_op jit(solution)/shard_map/all_to_all | solution.py:720
  49.9 0.6 %shard_map.49.u3 = f32[5,8,128]{2,1,0:T(8,128)S(1)} custom-call(f32[16,4,8,128]{3,2,1,0:T(8,128)S(1)} %all-to-all-done.1.got), custom_call_target="tpu_custom_call" | custom-call | tf_op jit(solution)/shard_map/pallas_call | solution.py:626
  50.5 0.0 collective-permute-done.11.rs1
  50.5 0.0 collective-permute-done.12.rs2
  50.5 1.4 %shard_map.50 = (f32[16,8,24,128]{3,2,1,0:T(8,128)S(1)}, f32[16,8,24,128]{3,2,1,0:T(8,128)S(1)}, f32[14,4,24,128]{3,2,1,0:T(8,128)S(1)}, f32[14,4,24,128]{3,2,1,0:T(8,128)S(1)}) custom-call(f32[8,16,1024]{2,1,0:T(8,128)S(1)} %shard_map.44.src, f32[8,16,1024]{2,1,0:T(8,128)S(1)} %collective-permute-done.5.ra, f32[7,16,1024]{2,1,0:T(8,128)S(1)} %collective-permute-done.6.rb, ...), custom_call_target="tpu_custom_call" | custom-call | tf_op jit(solution)/shard_map/pallas_call | solution.py:626
  51.9 0.0 collective-permute-done.10.r2e
  51.9 0.0 collective-permute-done.9.r2c2
  51.9 0.0 collective-permute-done.8.r2c1
  51.9 4.2 %shard_map.51 = (f32[8,16,1024]{2,1,0:T(8,128)}, f32[8,16,1024]{2,1,0:T(8,128)}) custom-call(f32[5,8,128]{2,1,0:T(8,128)S(1)} %shard_map.49.u3, f32[4,16,256]{2,1,0:T(8,128)S(1)} %get-tuple-element.45.f2, f32[4,16,256]{2,1,0:T(8,128)S(1)} %collective-permute-done.8.r2c1, f32[4,16,256]{2,1,0:T(8,128)S(1)} %collective-permute-done.9.r2c2, ...), custom_call_target="tpu_custom_call" | custom-call | tf_op jit(solution)/shard_map/pallas_call | solution.py:626
  (1 shorter events, 0.0 us)
Async XLA Ops:
  0.6 1.0 %copy-start = (f32[8,16,1024]{2,1,0:T(8,128)S(1)}, f32[8,16,1024]{2,1,0:T(8,128)}, u32[]{:S(2)}) copy-start(f32[8,16,1024]{2,1,0:T(8,128)} %vf.3) | copy-start | bytes 1572868
  1.7 6.2 %collective-permute-start = (f32[1,16,1024]{2,1,0:T(8,128)S(1)}, f32[1,16,1024]{2,1,0:T(8,128)S(1)}, u32[]{:S(2)}, u32[]{:S(2)}) collective-permute-start(f32[1,16,1024]{2,1,0:T(8,128)S(1)} %get-tuple-element.30), channel_id=1, source_target_pairs={{0,4},{1,5},{2,6},{3,7},{4,0},{5,1},{6,2},{7,3},{8,12},{9,13},{10,... | collective-permute-start | bytes 196616 | tf_op jit(solution)/shard_map/ppermute | solution.py:666
  1.8 6.1 %collective-permute-start.1 = (f32[1,16,1024]{2,1,0:T(8,128)S(1)}, f32[1,16,1024]{2,1,0:T(8,128)S(1)}, u32[]{:S(2)}, u32[]{:S(2)}) collective-permute-start(f32[1,16,1024]{2,1,0:T(8,128)S(1)} %get-tuple-element.31), channel_id=1, source_target_pairs={{0,1},{1,0},{2,3},{3,2},{4,8},{5,9},{6,10},{7,11},{8,4},{9,5},{10,... | collective-permute-start | bytes 196616 | tf_op jit(solution)/shard_map/ppermute | solution.py:666
  2.4 5.6 %collective-permute-start.2 = (f32[8,1024]{1,0:T(8,128)S(1)}, f32[8,1024]{1,0:T(8,128)S(1)}, u32[]{:S(2)}, u32[]{:S(2)}) collective-permute-start(f32[8,1024]{1,0:T(8,128)S(1)} %get-tuple-element.32), channel_id=1, source_target_pairs={{0,1},{1,0},{2,3},{3,2},{4,5},{5,4},{6,7},{7,6},{8,9},{9,8},{10,11... | collective-permute-start | bytes 98312 | tf_op jit(solution)/shard_map/ppermute | solution.py:666
  3.9 4.0 %collective-permute-start.3 = (f32[8,1024]{1,0:T(8,128)S(1)}, f32[8,1024]{1,0:T(8,128)S(1)}, u32[]{:S(2)}, u32[]{:S(2)}) collective-permute-start(f32[8,1024]{1,0:T(8,128)S(1)} %get-tuple-element.33), channel_id=1, source_target_pairs={{0,4},{1,2},{2,1},{3,7},{4,0},{5,6},{6,5},{7,3},{8,12},{9,10},{10,... | collective-permute-start | bytes 98312 | tf_op jit(solution)/shard_map/ppermute | solution.py:666
  6.2 1.0 %copy-start.1 = (s32[8,16,1024]{2,1,0:T(8,128)S(1)}, s32[8,16,1024]{2,1,0:T(8,128)}, u32[]{:S(2)}) copy-start(s32[8,16,1024]{2,1,0:T(8,128)} %mask.1) | copy-start | bytes 1572868
  10.0 4.1 %collective-permute-start.5 = (f32[8,16,1024]{2,1,0:T(8,128)S(1)}, f32[8,16,1024]{2,1,0:T(8,128)S(1)}, u32[]{:S(2)}, u32[]{:S(2)}) collective-permute-start(f32[8,16,1024]{2,1,0:T(8,128)S(1)} %get-tuple-element.36.big), channel_id=1, source_target_pairs={{0,4},{1,5},{2,6},{3,7},{4,0},{5,1},{6,2},{7,3},{8,12},{9,13},{10,... | collective-permute-start | bytes 1572872 | tf_op jit(solution)/shard_map/ppermute | solution.py:666
  10.4 3.7 %collective-permute-start.4 = (f32[2,8,256]{2,1,0:T(8,128)S(1)}, f32[2,8,256]{2,1,0:T(8,128)S(1)}, u32[]{:S(2)}, u32[]{:S(2)}) collective-permute-start(f32[2,8,256]{2,1,0:T(8,128)S(1)} %get-tuple-element.35), channel_id=1, source_target_pairs={{0,1},{1,0},{2,3},{3,2},{4,8},{5,9},{6,10},{7,11},{8,4},{9,5},{10,... | collective-permute-start | bytes 49160 | tf_op jit(solution)/shard_map/ppermute | solution.py:666
  14.2 10.4 %collective-permute-start.6 = (f32[7,16,1024]{2,1,0:T(8,128)S(1)}, f32[7,16,1024]{2,1,0:T(8,128)S(1)}, u32[]{:S(2)}, u32[]{:S(2)}) collective-permute-start(f32[7,16,1024]{2,1,0:T(8,128)S(1)} %get-tuple-element.38), channel_id=1, source_target_pairs={{0,1},{1,0},{2,3},{3,2},{4,8},{5,9},{6,10},{7,11},{8,4},{9,5},{10,... | collective-permute-start | bytes 1376264 | tf_op jit(solution)/shard_map/ppermute | solution.py:666
  24.6 1.5 %collective-permute-start.7 = (f32[3,16,1024]{2,1,0:T(8,128)S(1)}, f32[3,16,1024]{2,1,0:T(8,128)S(1)}, u32[]{:S(2)}, u32[]{:S(2)}) collective-permute-start(f32[3,16,1024]{2,1,0:T(8,128)S(1)} %slice.3), channel_id=1, source_target_pairs={{0,4},{1,5},{2,6},{3,7},{4,0},{5,1},{6,2},{7,3},{8,12},{9,13},{10,... | collective-permute-start | bytes 589832 | tf_op jit(solution)/shard_map/ppermute | solution.py:666
  27.3 23.2 %collective-permute-start.11 = (f32[15,8,1024]{2,1,0:T(8,128)}, f32[15,8,1024]{2,1,0:T(8,128)S(1)}, u32[]{:S(2)}, u32[]{:S(2)}) collective-permute-start(f32[15,8,1024]{2,1,0:T(8,128)} %get-tuple-element.48), channel_id=1, source_target_pairs={{0,1},{1,0},{2,3},{3,2},{4,5},{5,4},{6,7},{7,6},{8,9},{9,8},{10,11... | collective-permute-start | bytes 1474568 | tf_op jit(solution)/shard_map/ppermute | solution.py:666
  27.6 22.9 %collective-permute-start.12 = (f32[15,8,1024]{2,1,0:T(8,128)}, f32[15,8,1024]{2,1,0:T(8,128)S(1)}, u32[]{:S(2)}, u32[]{:S(2)}) collective-permute-start(f32[15,8,1024]{2,1,0:T(8,128)} %get-tuple-element.49), channel_id=1, source_target_pairs={{0,4},{1,2},{2,1},{3,7},{4,0},{5,6},{6,5},{7,3},{8,12},{9,10},{10,... | collective-permute-start | bytes 1474568 | tf_op jit(solution)/shard_map/ppermute | solution.py:666
  29.0 20.9 %all-to-all-start.1 = ((f32[16,4,8,128]{3,2,1,0:T(8,128)}), f32[16,4,8,128]{3,2,1,0:T(8,128)S(1)}, u32[]{:S(2)}, u32[]{:S(2)}) async-start(f32[16,4,8,128]{3,2,1,0:T(8,128)} %get-tuple-element.44), calls=%async_computation.1 | async-start | bytes 524288 | tf_op jit(solution)/shard_map/all_to_all | solution.py:720
  40.3 11.6 %collective-permute-start.9 = (f32[4,16,256]{2,1,0:T(8,128)S(1)}, f32[4,16,256]{2,1,0:T(8,128)S(1)}, u32[]{:S(2)}, u32[]{:S(2)}) collective-permute-start(f32[4,16,256]{2,1,0:T(8,128)S(1)} %get-tuple-element.45.f2), channel_id=1, source_target_pairs={{0,4},{1,5},{2,6},{3,7},{4,0},{5,1},{6,2},{7,3},{8,16},{9,17},{10,... | collective-permute-start | bytes 196616 | tf_op jit(solution)/shard_map/ppermute | solution.py:666
  40.4 11.5 %collective-permute-start.8 = (f32[4,16,256]{2,1,0:T(8,128)S(1)}, f32[4,16,256]{2,1,0:T(8,128)S(1)}, u32[]{:S(2)}, u32[]{:S(2)}) collective-permute-start(f32[4,16,256]{2,1,0:T(8,128)S(1)} %get-tuple-element.45.f2), channel_id=1, source_target_pairs={{0,8},{1,9},{2,10},{3,11},{4,12},{5,13},{6,14},{7,15},{8,0},{9,1},... | collective-permute-start | bytes 196616 | tf_op jit(solution)/shard_map/ppermute | solution.py:666
  43.7 8.2 %collective-permute-start.10 = (f32[1,16,256]{2,1,0:T(8,128)S(1)}, f32[1,16,256]{2,1,0:T(8,128)S(1)}, u32[]{:S(2)}, u32[]{:S(2)}) collective-permute-start(f32[1,16,256]{2,1,0:T(8,128)S(1)} %get-tuple-element.46), channel_id=1, source_target_pairs={{0,8},{1,9},{2,10},{3,11},{4,16},{5,17},{6,18},{7,19},{8,0},{9,1},... | collective-permute-start | bytes 49160 | tf_op jit(solution)/shard_map/ppermute | solution.py:666

commit v7 on v6

--- a/solution.py
+++ b/solution.py
@@ -144,7 +144,7 @@
             H[x, k] = h[k]
             G[x, k] = 0.5 * (after[k] - before[k])
 
-    each(0, NX, level0, 4)
+    each(0, NX, level0, 8)
 
 
 def masked(G, mask, out):
@@ -583,7 +583,7 @@
             for k in range(nz):
                 new[x, k] = (C0 * u[k] + D * (F0[x, k] + around_u[k])) * m
 
-        each(lo, hi, body, 4)
+        each(lo, hi, body, (hi - lo) // 2)
 
     sweep0(V0, X0, 2, 14)
     sweep0(X0, V0, 3, 13)

time: 56.5 us -> 56.5 us (level)
  transfers between devices with their start and end apart: 14 -> 14, of which waited for: 3 -> 3; matrix products, arithmetic and copies ran while one was open for 0% -> 0% of each run, Pallas kernels for 8% -> 9%
where the time goes in v7:
time: 56.5 us; the launch traced here: 56.2 us
  starting transfers between devices  20.7 us (37%)
  Pallas kernels  12.4 us (22%)
  waiting for transfers between devices  10.2 us (18%)
  blocking collectives  9.95 us (18%)
  local copies, waits for them, and re-layouts  2.09 us (4%)
  between operations  0.79 us (1%)
    pallas_call x11, Pallas kernels, call(): pl.pallas_call(kernel, out_shape=[jax.ShapeDtypeStruct(s, f32) for s in o...  12.4 us
    all_to_all x1, starting transfers between devices, shards(): got = lax.all_to_all(out, AXES, 0, 0, axis_index_groups=group)  11 us
    all_to_all x1, blocking collectives, shards(): got = lax.all_to_all(out, AXES, 0, 0, axis_index_groups=group)  9.95 us
    ppermute x13, starting transfers between devices, shards(): move = lambda v, table: lax.ppermute(v, AXES, table)  9.75 us
    all_to_all x1, waiting for transfers between devices, shards(): got = lax.all_to_all(out, AXES, 0, 0, axis_index_groups=group)  6.15 us
    ppermute x13, waiting for transfers between devices, shards(): move = lambda v, table: lax.ppermute(v, AXES, table)  4.06 us
    unnamed x4, local copies, waits for them, and re-layouts  2.07 us
  transfers between devices with their start and end apart: 14, of which 3 were waited for; matrix products, arithmetic and copies ran while one was open for 0% of the time, Pallas kernels for 9%

profile of v7, /device:TPU:2, one launch (start us, length us, event | category | flops | bytes accessed | tf_op | source)
XLA Modules:
  0.0 56.2 jit_solution(1608237811811024884)
XLA Ops:
  0.6 0.0 copy-start
  0.6 1.0 %copy-done = f32[8,16,1024]{2,1,0:T(8,128)S(1)} copy-done((f32[8,16,1024]{2,1,0:T(8,128)S(1)}, f32[8,16,1024]{2,1,0:T(8,128)}, u32[]{:S(2)}) %copy-start) | copy-done | bytes 524312
  1.7 0.1 shard_map.43
  1.7 0.1 collective-permute-start
  1.8 0.5 collective-permute-start.1
  2.4 1.6 %collective-permute-start.2 = (f32[8,1024]{1,0:T(8,128)S(1)}, f32[8,1024]{1,0:T(8,128)S(1)}, u32[]{:S(2)}, u32[]{:S(2)}) collective-permute-start(f32[8,1024]{1,0:T(8,128)S(1)} %get-tuple-element.32), channel_id=1, source_target_pairs={{0,1},{1,0},{2,3},{3,2},{4,5},{5,4},{6,7},{7,6},{8,9},{9,8},{10,11... | collective-permute-start | bytes 98312 | tf_op jit(solution)/shard_map/ppermute | solution.py:666
  3.9 1.5 %collective-permute-start.3 = (f32[8,1024]{1,0:T(8,128)S(1)}, f32[8,1024]{1,0:T(8,128)S(1)}, u32[]{:S(2)}, u32[]{:S(2)}) collective-permute-start(f32[8,1024]{1,0:T(8,128)S(1)} %get-tuple-element.33), channel_id=1, source_target_pairs={{0,4},{1,2},{2,1},{3,7},{4,0},{5,6},{6,5},{7,3},{8,12},{9,10},{10,... | collective-permute-start | bytes 98312 | tf_op jit(solution)/shard_map/ppermute | solution.py:666
  5.4 1.1 %shard_map.41 = (f32[8,8,16,128]{3,2,1,0:T(8,128)S(1)}, f32[8,8,16,128]{3,2,1,0:T(8,128)S(1)}) custom-call(f32[8,16,1024]{2,1,0:T(8,128)S(1)} %copy-done), custom_call_target="tpu_custom_call" | custom-call | bytes 5400000 | tf_op jit(solution)/shard_map/pallas_call | solution.py:626
  6.6 0.0 copy-start.1
  6.6 1.0 %copy-done.1 = s32[8,16,1024]{2,1,0:T(8,128)S(1)} copy-done((s32[8,16,1024]{2,1,0:T(8,128)S(1)}, s32[8,16,1024]{2,1,0:T(8,128)}, u32[]{:S(2)}) %copy-start.1) | copy-done | bytes 524312
  7.6 0.6 %shard_map.42.G = f32[8,8,16,128]{3,2,1,0:T(8,128)S(1)} custom-call(f32[8,8,16,128]{3,2,1,0:T(8,128)S(1)} %get-tuple-element.29.G, s32[8,16,1024]{2,1,0:T(8,128)S(1)} %copy-done.1), custom_call_target="tpu_custom_call" | custom-call | tf_op jit(solution)/shard_map/pallas_call | solution.py:626
  8.3 0.0 collective-permute-done.2.rs1
  8.3 0.0 collective-permute-done.3.rs2
  8.3 0.0 collective-permute-done.ra
  8.3 0.0 collective-permute-done.1.rb
  8.3 0.7 %shard_map.44.src = f32[8,16,1024]{2,1,0:T(8,128)S(1)} custom-call(f32[8,8,16,128]{3,2,1,0:T(8,128)S(1)} %get-tuple-element.28.H, f32[8,8,16,128]{3,2,1,0:T(8,128)S(1)} %shard_map.42.G, f32[1,16,1024]{2,1,0:T(8,128)S(1)} %collective-permute-done.ra, f32[1,16,1024]{2,1,0:T(8,128)S(1)} %collective-permute-done.1.rb, f32[8,1024]{1,0:T(8,128)S(1)} %collective-permute-done.2.rs1, ...), custom_call_target="tpu_custom_call" | custom-call | tf_op jit(solution)/shard_map/pallas_call | solution.py:626
  9.0 1.3 %shard_map.45 = (f32[8,16,1024]{2,1,0:T(8,128)S(1)}, f32[2,8,256]{2,1,0:T(8,128)S(1)}, f32[2,8,256]{2,1,0:T(8,128)S(1)}) custom-call(f32[8,16,1024]{2,1,0:T(8,128)S(1)} %shard_map.44.src), custom_call_target="tpu_custom_call" | custom-call | tf_op jit(solution)/shard_map/pallas_call | solution.py:626
  10.3 0.4 collective-permute-start.5
  10.7 0.0 collective-permute-start.4
  10.7 3.7 %collective-permute-done.4.r2b = f32[2,8,256]{2,1,0:T(8,128)S(1)} collective-permute-done((f32[2,8,256]{2,1,0:T(8,128)S(1)}, f32[2,8,256]{2,1,0:T(8,128)S(1)}, u32[]{:S(2)}, u32[]{:S(2)}) %collective-permute-start.4) | collective-permute-done | bytes 16416 | tf_op jit(solution)/shard_map/ppermute | solution.py:666
  14.5 0.0 collective-permute-done.5.ra
  14.5 0.1 shard_map.46
  14.5 0.1 collective-permute-start.6
  14.6 10.0 %all_to_all.10.got = f32[8,2,8,256]{3,2,1,0:T(8,128)S(1)} all-to-all(f32[8,2,8,256]{3,2,1,0:T(8,128)S(1)} %get-tuple-element.37), channel_id=1, replica_groups={{0,1,2,3,4,5,6,7},{8,9,10,11,12,13,14,15},{16,17,18,19,20,21,22,23},{24..., dimensions={0} | all-to-all | bytes 262144 | tf_op jit(solution)/shard_map/all_to_all | solution.py:697
  24.6 0.0 collective-permute-done.6.rb
  24.6 0.2 collective-permute-start.7
  24.8 1.0 %shard_map.47 = (f32[4,16,256]{2,1,0:T(8,128)S(1)}, f32[1,16,256]{2,1,0:T(8,128)S(1)}, f32[16,4,8,128]{3,2,1,0:T(8,128)}) custom-call(f32[8,2,8,256]{3,2,1,0:T(8,128)S(1)} %all_to_all.10.got), custom_call_target="tpu_custom_call" | custom-call | tf_op jit(solution)/shard_map/pallas_call | solution.py:626
  25.8 0.3 collective-permute-done.7.far
  26.1 1.2 %shard_map.48 = (f32[14,16,512]{2,1,0:T(8,128)S(1)}, f32[15,8,1024]{2,1,0:T(8,128)}, f32[15,8,1024]{2,1,0:T(8,128)}) custom-call(f32[8,16,1024]{2,1,0:T(8,128)S(1)} %shard_map.44.src, f32[8,16,1024]{2,1,0:T(8,128)S(1)} %get-tuple-element.36.big, f32[8,16,1024]{2,1,0:T(8,128)S(1)} %collective-permute-done.5.ra, f32[7,16,1024]{2,1,0:T(8,128)S(1)} %collective-permute-done.6.rb, ...), custom_call_target="tpu_custom_call" | custom-call | tf_op jit(solution)/shard_map/pallas_call | solution.py:626
  27.3 0.8 %collective-permute-start.11 = (f32[15,8,1024]{2,1,0:T(8,128)}, f32[15,8,1024]{2,1,0:T(8,128)S(1)}, u32[]{:S(2)}, u32[]{:S(2)}) collective-permute-start(f32[15,8,1024]{2,1,0:T(8,128)} %get-tuple-element.48), channel_id=1, source_target_pairs={{0,1},{1,0},{2,3},{3,2},{4,5},{5,4},{6,7},{7,6},{8,9},{9,8},{10,11... | collective-permute-start | bytes 1474568 | tf_op jit(solution)/shard_map/ppermute | solution.py:666
  28.1 1.2 %collective-permute-start.12 = (f32[15,8,1024]{2,1,0:T(8,128)}, f32[15,8,1024]{2,1,0:T(8,128)S(1)}, u32[]{:S(2)}, u32[]{:S(2)}) collective-permute-start(f32[15,8,1024]{2,1,0:T(8,128)} %get-tuple-element.49), channel_id=1, source_target_pairs={{0,4},{1,2},{2,1},{3,7},{4,0},{5,6},{6,5},{7,3},{8,12},{9,10},{10,... | collective-permute-start | bytes 1474568 | tf_op jit(solution)/shard_map/ppermute | solution.py:666
  29.3 11.0 %all-to-all-start.1 = ((f32[16,4,8,128]{3,2,1,0:T(8,128)}), f32[16,4,8,128]{3,2,1,0:T(8,128)S(1)}, u32[]{:S(2)}, u32[]{:S(2)}) async-start(f32[16,4,8,128]{3,2,1,0:T(8,128)} %get-tuple-element.44), calls=%async_computation.1 | async-start | bytes 524288 | tf_op jit(solution)/shard_map/all_to_all | solution.py:720
  40.3 0.1 collective-permute-start.9
  40.4 3.3 %collective-permute-start.8 = (f32[4,16,256]{2,1,0:T(8,128)S(1)}, f32[4,16,256]{2,1,0:T(8,128)S(1)}, u32[]{:S(2)}, u32[]{:S(2)}) collective-permute-start(f32[4,16,256]{2,1,0:T(8,128)S(1)} %get-tuple-element.45.f2), channel_id=1, source_target_pairs={{0,8},{1,9},{2,10},{3,11},{4,12},{5,13},{6,14},{7,15},{8,0},{9,1},... | collective-permute-start | bytes 196616 | tf_op jit(solution)/shard_map/ppermute | solution.py:666
  43.7 0.0 collective-permute-start.10
  43.7 6.1 %all-to-all-done.1.got = f32[16,4,8,128]{3,2,1,0:T(8,128)S(1)} async-done(((f32[16,4,8,128]{3,2,1,0:T(8,128)}), f32[16,4,8,128]{3,2,1,0:T(8,128)S(1)}, u32[]{:S(2)}, u32[]{:S(2)}) %all-to-all-start.1) | async-done | bytes 262176 | tf_op jit(solution)/shard_map/all_to_all | solution.py:720
  49.9 0.6 %shard_map.49.u3 = f32[5,8,128]{2,1,0:T(8,128)S(1)} custom-call(f32[16,4,8,128]{3,2,1,0:T(8,128)S(1)} %all-to-all-done.1.got), custom_call_target="tpu_custom_call" | custom-call | tf_op jit(solution)/shard_map/pallas_call | solution.py:626
  50.5 0.0 collective-permute-done.11.rs1
  50.5 0.0 collective-permute-done.12.rs2
  50.5 1.4 %shard_map.50 = (f32[16,8,24,128]{3,2,1,0:T(8,128)S(1)}, f32[16,8,24,128]{3,2,1,0:T(8,128)S(1)}, f32[14,4,24,128]{3,2,1,0:T(8,128)S(1)}, f32[14,4,24,128]{3,2,1,0:T(8,128)S(1)}) custom-call(f32[8,16,1024]{2,1,0:T(8,128)S(1)} %shard_map.44.src, f32[8,16,1024]{2,1,0:T(8,128)S(1)} %collective-permute-done.5.ra, f32[7,16,1024]{2,1,0:T(8,128)S(1)} %collective-permute-done.6.rb, ...), custom_call_target="tpu_custom_call" | custom-call | tf_op jit(solution)/shard_map/pallas_call | solution.py:626
  51.9 0.0 collective-permute-done.10.r2e
  51.9 0.0 collective-permute-done.9.r2c2
  51.9 0.0 collective-permute-done.8.r2c1
  51.9 4.2 %shard_map.51 = (f32[8,16,1024]{2,1,0:T(8,128)}, f32[8,16,1024]{2,1,0:T(8,128)}) custom-call(f32[5,8,128]{2,1,0:T(8,128)S(1)} %shard_map.49.u3, f32[4,16,256]{2,1,0:T(8,128)S(1)} %get-tuple-element.45.f2, f32[4,16,256]{2,1,0:T(8,128)S(1)} %collective-permute-done.8.r2c1, f32[4,16,256]{2,1,0:T(8,128)S(1)} %collective-permute-done.9.r2c2, ...), custom_call_target="tpu_custom_call" | custom-call | tf_op jit(solution)/shard_map/pallas_call | solution.py:626
  (1 shorter events, 0.0 us)
Async XLA Ops:
  0.6 1.0 %copy-start = (f32[8,16,1024]{2,1,0:T(8,128)S(1)}, f32[8,16,1024]{2,1,0:T(8,128)}, u32[]{:S(2)}) copy-start(f32[8,16,1024]{2,1,0:T(8,128)} %vf.3) | copy-start | bytes 1572868
  1.7 6.6 %collective-permute-start = (f32[1,16,1024]{2,1,0:T(8,128)S(1)}, f32[1,16,1024]{2,1,0:T(8,128)S(1)}, u32[]{:S(2)}, u32[]{:S(2)}) collective-permute-start(f32[1,16,1024]{2,1,0:T(8,128)S(1)} %get-tuple-element.30), channel_id=1, source_target_pairs={{0,4},{1,5},{2,6},{3,7},{4,0},{5,1},{6,2},{7,3},{8,12},{9,13},{10,... | collective-permute-start | bytes 196616 | tf_op jit(solution)/shard_map/ppermute | solution.py:666
  1.8 6.5 %collective-permute-start.1 = (f32[1,16,1024]{2,1,0:T(8,128)S(1)}, f32[1,16,1024]{2,1,0:T(8,128)S(1)}, u32[]{:S(2)}, u32[]{:S(2)}) collective-permute-start(f32[1,16,1024]{2,1,0:T(8,128)S(1)} %get-tuple-element.31), channel_id=1, source_target_pairs={{0,1},{1,0},{2,3},{3,2},{4,8},{5,9},{6,10},{7,11},{8,4},{9,5},{10,... | collective-permute-start | bytes 196616 | tf_op jit(solution)/shard_map/ppermute | solution.py:666
  2.4 5.9 %collective-permute-start.2 = (f32[8,1024]{1,0:T(8,128)S(1)}, f32[8,1024]{1,0:T(8,128)S(1)}, u32[]{:S(2)}, u32[]{:S(2)}) collective-permute-start(f32[8,1024]{1,0:T(8,128)S(1)} %get-tuple-element.32), channel_id=1, source_target_pairs={{0,1},{1,0},{2,3},{3,2},{4,5},{5,4},{6,7},{7,6},{8,9},{9,8},{10,11... | collective-permute-start | bytes 98312 | tf_op jit(solution)/shard_map/ppermute | solution.py:666
  3.9 4.4 %collective-permute-start.3 = (f32[8,1024]{1,0:T(8,128)S(1)}, f32[8,1024]{1,0:T(8,128)S(1)}, u32[]{:S(2)}, u32[]{:S(2)}) collective-permute-start(f32[8,1024]{1,0:T(8,128)S(1)} %get-tuple-element.33), channel_id=1, source_target_pairs={{0,4},{1,2},{2,1},{3,7},{4,0},{5,6},{6,5},{7,3},{8,12},{9,10},{10,... | collective-permute-start | bytes 98312 | tf_op jit(solution)/shard_map/ppermute | solution.py:666
  6.6 1.0 %copy-start.1 = (s32[8,16,1024]{2,1,0:T(8,128)S(1)}, s32[8,16,1024]{2,1,0:T(8,128)}, u32[]{:S(2)}) copy-start(s32[8,16,1024]{2,1,0:T(8,128)} %mask.1) | copy-start | bytes 1572868
  10.3 4.1 %collective-permute-start.5 = (f32[8,16,1024]{2,1,0:T(8,128)S(1)}, f32[8,16,1024]{2,1,0:T(8,128)S(1)}, u32[]{:S(2)}, u32[]{:S(2)}) collective-permute-start(f32[8,16,1024]{2,1,0:T(8,128)S(1)} %get-tuple-element.36.big), channel_id=1, source_target_pairs={{0,4},{1,5},{2,6},{3,7},{4,0},{5,1},{6,2},{7,3},{8,12},{9,13},{10,... | collective-permute-start | bytes 1572872 | tf_op jit(solution)/shard_map/ppermute | solution.py:666
  10.7 3.7 %collective-permute-start.4 = (f32[2,8,256]{2,1,0:T(8,128)S(1)}, f32[2,8,256]{2,1,0:T(8,128)S(1)}, u32[]{:S(2)}, u32[]{:S(2)}) collective-permute-start(f32[2,8,256]{2,1,0:T(8,128)S(1)} %get-tuple-element.35), channel_id=1, source_target_pairs={{0,1},{1,0},{2,3},{3,2},{4,8},{5,9},{6,10},{7,11},{8,4},{9,5},{10,... | collective-permute-start | bytes 49160 | tf_op jit(solution)/shard_map/ppermute | solution.py:666
  14.5 10.0 %collective-permute-start.6 = (f32[7,16,1024]{2,1,0:T(8,128)S(1)}, f32[7,16,1024]{2,1,0:T(8,128)S(1)}, u32[]{:S(2)}, u32[]{:S(2)}) collective-permute-start(f32[7,16,1024]{2,1,0:T(8,128)S(1)} %get-tuple-element.38), channel_id=1, source_target_pairs={{0,1},{1,0},{2,3},{3,2},{4,8},{5,9},{6,10},{7,11},{8,4},{9,5},{10,... | collective-permute-start | bytes 1376264 | tf_op jit(solution)/shard_map/ppermute | solution.py:666
  24.6 1.5 %collective-permute-start.7 = (f32[3,16,1024]{2,1,0:T(8,128)S(1)}, f32[3,16,1024]{2,1,0:T(8,128)S(1)}, u32[]{:S(2)}, u32[]{:S(2)}) collective-permute-start(f32[3,16,1024]{2,1,0:T(8,128)S(1)} %slice.3), channel_id=1, source_target_pairs={{0,4},{1,5},{2,6},{3,7},{4,0},{5,1},{6,2},{7,3},{8,12},{9,13},{10,... | collective-permute-start | bytes 589832 | tf_op jit(solution)/shard_map/ppermute | solution.py:666
  27.3 23.2 %collective-permute-start.11 = (f32[15,8,1024]{2,1,0:T(8,128)}, f32[15,8,1024]{2,1,0:T(8,128)S(1)}, u32[]{:S(2)}, u32[]{:S(2)}) collective-permute-start(f32[15,8,1024]{2,1,0:T(8,128)} %get-tuple-element.48), channel_id=1, source_target_pairs={{0,1},{1,0},{2,3},{3,2},{4,5},{5,4},{6,7},{7,6},{8,9},{9,8},{10,11... | collective-permute-start | bytes 1474568 | tf_op jit(solution)/shard_map/ppermute | solution.py:666
  28.1 22.4 %collective-permute-start.12 = (f32[15,8,1024]{2,1,0:T(8,128)}, f32[15,8,1024]{2,1,0:T(8,128)S(1)}, u32[]{:S(2)}, u32[]{:S(2)}) collective-permute-start(f32[15,8,1024]{2,1,0:T(8,128)} %get-tuple-element.49), channel_id=1, source_target_pairs={{0,4},{1,2},{2,1},{3,7},{4,0},{5,6},{6,5},{7,3},{8,12},{9,10},{10,... | collective-permute-start | bytes 1474568 | tf_op jit(solution)/shard_map/ppermute | solution.py:666
  29.3 20.6 %all-to-all-start.1 = ((f32[16,4,8,128]{3,2,1,0:T(8,128)}), f32[16,4,8,128]{3,2,1,0:T(8,128)S(1)}, u32[]{:S(2)}, u32[]{:S(2)}) async-start(f32[16,4,8,128]{3,2,1,0:T(8,128)} %get-tuple-element.44), calls=%async_computation.1 | async-start | bytes 524288 | tf_op jit(solution)/shard_map/all_to_all | solution.py:720
  40.3 11.6 %collective-permute-start.9 = (f32[4,16,256]{2,1,0:T(8,128)S(1)}, f32[4,16,256]{2,1,0:T(8,128)S(1)}, u32[]{:S(2)}, u32[]{:S(2)}) collective-permute-start(f32[4,16,256]{2,1,0:T(8,128)S(1)} %get-tuple-element.45.f2), channel_id=1, source_target_pairs={{0,4},{1,5},{2,6},{3,7},{4,0},{5,1},{6,2},{7,3},{8,16},{9,17},{10,... | collective-permute-start | bytes 196616 | tf_op jit(solution)/shard_map/ppermute | solution.py:666
  40.4 11.5 %collective-permute-start.8 = (f32[4,16,256]{2,1,0:T(8,128)S(1)}, f32[4,16,256]{2,1,0:T(8,128)S(1)}, u32[]{:S(2)}, u32[]{:S(2)}) collective-permute-start(f32[4,16,256]{2,1,0:T(8,128)S(1)} %get-tuple-element.45.f2), channel_id=1, source_target_pairs={{0,8},{1,9},{2,10},{3,11},{4,12},{5,13},{6,14},{7,15},{8,0},{9,1},... | collective-permute-start | bytes 196616 | tf_op jit(solution)/shard_map/ppermute | solution.py:666
  43.7 8.2 %collective-permute-start.10 = (f32[1,16,256]{2,1,0:T(8,128)S(1)}, f32[1,16,256]{2,1,0:T(8,128)S(1)}, u32[]{:S(2)}, u32[]{:S(2)}) collective-permute-start(f32[1,16,256]{2,1,0:T(8,128)S(1)} %get-tuple-element.46), channel_id=1, source_target_pairs={{0,8},{1,9},{2,10},{3,11},{4,16},{5,17},{6,18},{7,19},{8,0},{9,1},... | collective-permute-start | bytes 49160 | tf_op jit(solution)/shard_map/ppermute | solution.py:666

commit v8 on v6

--- a/solution.py
+++ b/solution.py
@@ -489,7 +489,7 @@
         for k in range(nz):
             P0[x, k] = (C1 * f[k] + C2 * around_f[k]) * m
 
-    each(1, 15, smooth0, 7)
+    each(1, 15, smooth0, 14)
 
 
 def ascent(dims, u3, f2, r2c1, r2c2, r2e, F0, P0, F1, P1, press_out, resid_out, F2, T2, W2, X2, T1, V1, X1, T0, V0, X0, press, resid, done):

time: 56.5 us -> 56.5 us (level)
  no operation moved by 1% of the time
where the time goes in v8:
time: 56.5 us; the launch traced here: 56.2 us
  starting transfers between devices  20.7 us (37%)
  Pallas kernels  12 us (21%)
  blocking collectives  10.3 us (18%)
  waiting for transfers between devices  10.2 us (18%)
  local copies, waits for them, and re-layouts  2.09 us (4%)
  between operations  0.79 us (1%)
    pallas_call x11, Pallas kernels, call(): pl.pallas_call(kernel, out_shape=[jax.ShapeDtypeStruct(s, f32) for s in o...  12 us
    all_to_all x1, starting transfers between devices, shards(): got = lax.all_to_all(out, AXES, 0, 0, axis_index_groups=group)  11.3 us
    all_to_all x1, blocking collectives, shards(): got = lax.all_to_all(out, AXES, 0, 0, axis_index_groups=group)  10.3 us
    ppermute x13, starting transfers between devices, shards(): move = lambda v, table: lax.ppermute(v, AXES, table)  9.39 us
    all_to_all x1, waiting for transfers between devices, shards(): got = lax.all_to_all(out, AXES, 0, 0, axis_index_groups=group)  6.15 us
    ppermute x13, waiting for transfers between devices, shards(): move = lambda v, table: lax.ppermute(v, AXES, table)  4.06 us
    unnamed x4, local copies, waits for them, and re-layouts  2.07 us
  transfers between devices with their start and end apart: 14, of which 3 were waited for; matrix products, arithmetic and copies ran while one was open for 0% of the time, Pallas kernels for 8%

profile of v8, /device:TPU:2, one launch (start us, length us, event | category | flops | bytes accessed | tf_op | source)
XLA Modules:
  0.0 56.2 jit_solution(240324142422441142)
XLA Ops:
  0.6 0.0 copy-start
  0.6 1.0 %copy-done = f32[8,16,1024]{2,1,0:T(8,128)S(1)} copy-done((f32[8,16,1024]{2,1,0:T(8,128)S(1)}, f32[8,16,1024]{2,1,0:T(8,128)}, u32[]{:S(2)}) %copy-start) | copy-done | bytes 524312
  1.7 0.1 shard_map.43
  1.7 0.1 collective-permute-start
  1.8 0.5 collective-permute-start.1
  2.4 1.6 %collective-permute-start.2 = (f32[8,1024]{1,0:T(8,128)S(1)}, f32[8,1024]{1,0:T(8,128)S(1)}, u32[]{:S(2)}, u32[]{:S(2)}) collective-permute-start(f32[8,1024]{1,0:T(8,128)S(1)} %get-tuple-element.32), channel_id=1, source_target_pairs={{0,1},{1,0},{2,3},{3,2},{4,5},{5,4},{6,7},{7,6},{8,9},{9,8},{10,11... | collective-permute-start | bytes 98312 | tf_op jit(solution)/shard_map/ppermute | solution.py:666
  3.9 1.5 %collective-permute-start.3 = (f32[8,1024]{1,0:T(8,128)S(1)}, f32[8,1024]{1,0:T(8,128)S(1)}, u32[]{:S(2)}, u32[]{:S(2)}) collective-permute-start(f32[8,1024]{1,0:T(8,128)S(1)} %get-tuple-element.33), channel_id=1, source_target_pairs={{0,4},{1,2},{2,1},{3,7},{4,0},{5,6},{6,5},{7,3},{8,12},{9,10},{10,... | collective-permute-start | bytes 98312 | tf_op jit(solution)/shard_map/ppermute | solution.py:666
  5.4 0.8 %shard_map.41 = (f32[8,8,16,128]{3,2,1,0:T(8,128)S(1)}, f32[8,8,16,128]{3,2,1,0:T(8,128)S(1)}) custom-call(f32[8,16,1024]{2,1,0:T(8,128)S(1)} %copy-done), custom_call_target="tpu_custom_call" | custom-call | bytes 5400000 | tf_op jit(solution)/shard_map/pallas_call | solution.py:626
  6.2 0.0 copy-start.1
  6.2 1.0 %copy-done.1 = s32[8,16,1024]{2,1,0:T(8,128)S(1)} copy-done((s32[8,16,1024]{2,1,0:T(8,128)S(1)}, s32[8,16,1024]{2,1,0:T(8,128)}, u32[]{:S(2)}) %copy-start.1) | copy-done | bytes 524312
  7.3 0.6 %shard_map.42.G = f32[8,8,16,128]{3,2,1,0:T(8,128)S(1)} custom-call(f32[8,8,16,128]{3,2,1,0:T(8,128)S(1)} %get-tuple-element.29.G, s32[8,16,1024]{2,1,0:T(8,128)S(1)} %copy-done.1), custom_call_target="tpu_custom_call" | custom-call | tf_op jit(solution)/shard_map/pallas_call | solution.py:626
  7.9 0.0 collective-permute-done.2.rs1
  7.9 0.0 collective-permute-done.3.rs2
  7.9 0.0 collective-permute-done.ra
  7.9 0.0 collective-permute-done.1.rb
  8.0 0.7 %shard_map.44.src = f32[8,16,1024]{2,1,0:T(8,128)S(1)} custom-call(f32[8,8,16,128]{3,2,1,0:T(8,128)S(1)} %get-tuple-element.28.H, f32[8,8,16,128]{3,2,1,0:T(8,128)S(1)} %shard_map.42.G, f32[1,16,1024]{2,1,0:T(8,128)S(1)} %collective-permute-done.ra, f32[1,16,1024]{2,1,0:T(8,128)S(1)} %collective-permute-done.1.rb, f32[8,1024]{1,0:T(8,128)S(1)} %collective-permute-done.2.rs1, ...), custom_call_target="tpu_custom_call" | custom-call | tf_op jit(solution)/shard_map/pallas_call | solution.py:626
  8.6 1.3 %shard_map.45 = (f32[8,16,1024]{2,1,0:T(8,128)S(1)}, f32[2,8,256]{2,1,0:T(8,128)S(1)}, f32[2,8,256]{2,1,0:T(8,128)S(1)}) custom-call(f32[8,16,1024]{2,1,0:T(8,128)S(1)} %shard_map.44.src), custom_call_target="tpu_custom_call" | custom-call | tf_op jit(solution)/shard_map/pallas_call | solution.py:626
  10.0 0.4 collective-permute-start.5
  10.4 0.0 collective-permute-start.4
  10.4 3.7 %collective-permute-done.4.r2b = f32[2,8,256]{2,1,0:T(8,128)S(1)} collective-permute-done((f32[2,8,256]{2,1,0:T(8,128)S(1)}, f32[2,8,256]{2,1,0:T(8,128)S(1)}, u32[]{:S(2)}, u32[]{:S(2)}) %collective-permute-start.4) | collective-permute-done | bytes 16416 | tf_op jit(solution)/shard_map/ppermute | solution.py:666
  14.1 0.0 collective-permute-done.5.ra
  14.1 0.1 shard_map.46
  14.2 0.1 collective-permute-start.6
  14.3 10.3 %all_to_all.10.got = f32[8,2,8,256]{3,2,1,0:T(8,128)S(1)} all-to-all(f32[8,2,8,256]{3,2,1,0:T(8,128)S(1)} %get-tuple-element.37), channel_id=1, replica_groups={{0,1,2,3,4,5,6,7},{8,9,10,11,12,13,14,15},{16,17,18,19,20,21,22,23},{24..., dimensions={0} | all-to-all | bytes 262144 | tf_op jit(solution)/shard_map/all_to_all | solution.py:697
  24.6 0.0 collective-permute-done.6.rb
  24.6 0.2 collective-permute-start.7
  24.8 1.0 %shard_map.47 = (f32[4,16,256]{2,1,0:T(8,128)S(1)}, f32[1,16,256]{2,1,0:T(8,128)S(1)}, f32[16,4,8,128]{3,2,1,0:T(8,128)}) custom-call(f32[8,2,8,256]{3,2,1,0:T(8,128)S(1)} %all_to_all.10.got), custom_call_target="tpu_custom_call" | custom-call | tf_op jit(solution)/shard_map/pallas_call | solution.py:626
  25.8 0.3 collective-permute-done.7.far
  26.1 1.2 %shard_map.48 = (f32[14,16,512]{2,1,0:T(8,128)S(1)}, f32[15,8,1024]{2,1,0:T(8,128)}, f32[15,8,1024]{2,1,0:T(8,128)}) custom-call(f32[8,16,1024]{2,1,0:T(8,128)S(1)} %shard_map.44.src, f32[8,16,1024]{2,1,0:T(8,128)S(1)} %get-tuple-element.36.big, f32[8,16,1024]{2,1,0:T(8,128)S(1)} %collective-permute-done.5.ra, f32[7,16,1024]{2,1,0:T(8,128)S(1)} %collective-permute-done.6.rb, ...), custom_call_target="tpu_custom_call" | custom-call | tf_op jit(solution)/shard_map/pallas_call | solution.py:626
  27.3 0.3 collective-permute-start.11
  27.6 1.3 %collective-permute-start.12 = (f32[15,8,1024]{2,1,0:T(8,128)}, f32[15,8,1024]{2,1,0:T(8,128)S(1)}, u32[]{:S(2)}, u32[]{:S(2)}) collective-permute-start(f32[15,8,1024]{2,1,0:T(8,128)} %get-tuple-element.49), channel_id=1, source_target_pairs={{0,4},{1,2},{2,1},{3,7},{4,0},{5,6},{6,5},{7,3},{8,12},{9,10},{10,... | collective-permute-start | bytes 1474568 | tf_op jit(solution)/shard_map/ppermute | solution.py:666
  29.0 11.3 %all-to-all-start.1 = ((f32[16,4,8,128]{3,2,1,0:T(8,128)}), f32[16,4,8,128]{3,2,1,0:T(8,128)S(1)}, u32[]{:S(2)}, u32[]{:S(2)}) async-start(f32[16,4,8,128]{3,2,1,0:T(8,128)} %get-tuple-element.44), calls=%async_computation.1 | async-start | bytes 524288 | tf_op jit(solution)/shard_map/all_to_all | solution.py:720
  40.3 0.1 collective-permute-start.9
  40.4 3.3 %collective-permute-start.8 = (f32[4,16,256]{2,1,0:T(8,128)S(1)}, f32[4,16,256]{2,1,0:T(8,128)S(1)}, u32[]{:S(2)}, u32[]{:S(2)}) collective-permute-start(f32[4,16,256]{2,1,0:T(8,128)S(1)} %get-tuple-element.45.f2), channel_id=1, source_target_pairs={{0,8},{1,9},{2,10},{3,11},{4,12},{5,13},{6,14},{7,15},{8,0},{9,1},... | collective-permute-start | bytes 196616 | tf_op jit(solution)/shard_map/ppermute | solution.py:666
  43.7 0.0 collective-permute-start.10
  43.7 6.1 %all-to-all-done.1.got = f32[16,4,8,128]{3,2,1,0:T(8,128)S(1)} async-done(((f32[16,4,8,128]{3,2,1,0:T(8,128)}), f32[16,4,8,128]{3,2,1,0:T(8,128)S(1)}, u32[]{:S(2)}, u32[]{:S(2)}) %all-to-all-start.1) | async-done | bytes 262176 | tf_op jit(solution)/shard_map/all_to_all | solution.py:720
  49.9 0.6 %shard_map.49.u3 = f32[5,8,128]{2,1,0:T(8,128)S(1)} custom-call(f32[16,4,8,128]{3,2,1,0:T(8,128)S(1)} %all-to-all-done.1.got), custom_call_target="tpu_custom_call" | custom-call | tf_op jit(solution)/shard_map/pallas_call | solution.py:626
  50.5 0.0 collective-permute-done.11.rs1
  50.5 0.0 collective-permute-done.12.rs2
  50.5 1.4 %shard_map.50 = (f32[16,8,24,128]{3,2,1,0:T(8,128)S(1)}, f32[16,8,24,128]{3,2,1,0:T(8,128)S(1)}, f32[14,4,24,128]{3,2,1,0:T(8,128)S(1)}, f32[14,4,24,128]{3,2,1,0:T(8,128)S(1)}) custom-call(f32[8,16,1024]{2,1,0:T(8,128)S(1)} %shard_map.44.src, f32[8,16,1024]{2,1,0:T(8,128)S(1)} %collective-permute-done.5.ra, f32[7,16,1024]{2,1,0:T(8,128)S(1)} %collective-permute-done.6.rb, ...), custom_call_target="tpu_custom_call" | custom-call | tf_op jit(solution)/shard_map/pallas_call | solution.py:626
  51.9 0.0 collective-permute-done.10.r2e
  51.9 0.0 collective-permute-done.9.r2c2
  51.9 0.0 collective-permute-done.8.r2c1
  51.9 4.2 %shard_map.51 = (f32[8,16,1024]{2,1,0:T(8,128)}, f32[8,16,1024]{2,1,0:T(8,128)}) custom-call(f32[5,8,128]{2,1,0:T(8,128)S(1)} %shard_map.49.u3, f32[4,16,256]{2,1,0:T(8,128)S(1)} %get-tuple-element.45.f2, f32[4,16,256]{2,1,0:T(8,128)S(1)} %collective-permute-done.8.r2c1, f32[4,16,256]{2,1,0:T(8,128)S(1)} %collective-permute-done.9.r2c2, ...), custom_call_target="tpu_custom_call" | custom-call | tf_op jit(solution)/shard_map/pallas_call | solution.py:626
  (1 shorter events, 0.0 us)
Async XLA Ops:
  0.6 1.0 %copy-start = (f32[8,16,1024]{2,1,0:T(8,128)S(1)}, f32[8,16,1024]{2,1,0:T(8,128)}, u32[]{:S(2)}) copy-start(f32[8,16,1024]{2,1,0:T(8,128)} %vf.3) | copy-start | bytes 1572868
  1.7 6.2 %collective-permute-start = (f32[1,16,1024]{2,1,0:T(8,128)S(1)}, f32[1,16,1024]{2,1,0:T(8,128)S(1)}, u32[]{:S(2)}, u32[]{:S(2)}) collective-permute-start(f32[1,16,1024]{2,1,0:T(8,128)S(1)} %get-tuple-element.30), channel_id=1, source_target_pairs={{0,4},{1,5},{2,6},{3,7},{4,0},{5,1},{6,2},{7,3},{8,12},{9,13},{10,... | collective-permute-start | bytes 196616 | tf_op jit(solution)/shard_map/ppermute | solution.py:666
  1.8 6.1 %collective-permute-start.1 = (f32[1,16,1024]{2,1,0:T(8,128)S(1)}, f32[1,16,1024]{2,1,0:T(8,128)S(1)}, u32[]{:S(2)}, u32[]{:S(2)}) collective-permute-start(f32[1,16,1024]{2,1,0:T(8,128)S(1)} %get-tuple-element.31), channel_id=1, source_target_pairs={{0,1},{1,0},{2,3},{3,2},{4,8},{5,9},{6,10},{7,11},{8,4},{9,5},{10,... | collective-permute-start | bytes 196616 | tf_op jit(solution)/shard_map/ppermute | solution.py:666
  2.4 5.6 %collective-permute-start.2 = (f32[8,1024]{1,0:T(8,128)S(1)}, f32[8,1024]{1,0:T(8,128)S(1)}, u32[]{:S(2)}, u32[]{:S(2)}) collective-permute-start(f32[8,1024]{1,0:T(8,128)S(1)} %get-tuple-element.32), channel_id=1, source_target_pairs={{0,1},{1,0},{2,3},{3,2},{4,5},{5,4},{6,7},{7,6},{8,9},{9,8},{10,11... | collective-permute-start | bytes 98312 | tf_op jit(solution)/shard_map/ppermute | solution.py:666
  3.9 4.0 %collective-permute-start.3 = (f32[8,1024]{1,0:T(8,128)S(1)}, f32[8,1024]{1,0:T(8,128)S(1)}, u32[]{:S(2)}, u32[]{:S(2)}) collective-permute-start(f32[8,1024]{1,0:T(8,128)S(1)} %get-tuple-element.33), channel_id=1, source_target_pairs={{0,4},{1,2},{2,1},{3,7},{4,0},{5,6},{6,5},{7,3},{8,12},{9,10},{10,... | collective-permute-start | bytes 98312 | tf_op jit(solution)/shard_map/ppermute | solution.py:666
  6.2 1.0 %copy-start.1 = (s32[8,16,1024]{2,1,0:T(8,128)S(1)}, s32[8,16,1024]{2,1,0:T(8,128)}, u32[]{:S(2)}) copy-start(s32[8,16,1024]{2,1,0:T(8,128)} %mask.1) | copy-start | bytes 1572868
  10.0 4.1 %collective-permute-start.5 = (f32[8,16,1024]{2,1,0:T(8,128)S(1)}, f32[8,16,1024]{2,1,0:T(8,128)S(1)}, u32[]{:S(2)}, u32[]{:S(2)}) collective-permute-start(f32[8,16,1024]{2,1,0:T(8,128)S(1)} %get-tuple-element.36.big), channel_id=1, source_target_pairs={{0,4},{1,5},{2,6},{3,7},{4,0},{5,1},{6,2},{7,3},{8,12},{9,13},{10,... | collective-permute-start | bytes 1572872 | tf_op jit(solution)/shard_map/ppermute | solution.py:666
  10.4 3.7 %collective-permute-start.4 = (f32[2,8,256]{2,1,0:T(8,128)S(1)}, f32[2,8,256]{2,1,0:T(8,128)S(1)}, u32[]{:S(2)}, u32[]{:S(2)}) collective-permute-start(f32[2,8,256]{2,1,0:T(8,128)S(1)} %get-tuple-element.35), channel_id=1, source_target_pairs={{0,1},{1,0},{2,3},{3,2},{4,8},{5,9},{6,10},{7,11},{8,4},{9,5},{10,... | collective-permute-start | bytes 49160 | tf_op jit(solution)/shard_map/ppermute | solution.py:666
  14.2 10.4 %collective-permute-start.6 = (f32[7,16,1024]{2,1,0:T(8,128)S(1)}, f32[7,16,1024]{2,1,0:T(8,128)S(1)}, u32[]{:S(2)}, u32[]{:S(2)}) collective-permute-start(f32[7,16,1024]{2,1,0:T(8,128)S(1)} %get-tuple-element.38), channel_id=1, source_target_pairs={{0,1},{1,0},{2,3},{3,2},{4,8},{5,9},{6,10},{7,11},{8,4},{9,5},{10,... | collective-permute-start | bytes 1376264 | tf_op jit(solution)/shard_map/ppermute | solution.py:666
  24.6 1.5 %collective-permute-start.7 = (f32[3,16,1024]{2,1,0:T(8,128)S(1)}, f32[3,16,1024]{2,1,0:T(8,128)S(1)}, u32[]{:S(2)}, u32[]{:S(2)}) collective-permute-start(f32[3,16,1024]{2,1,0:T(8,128)S(1)} %slice.3), channel_id=1, source_target_pairs={{0,4},{1,5},{2,6},{3,7},{4,0},{5,1},{6,2},{7,3},{8,12},{9,13},{10,... | collective-permute-start | bytes 589832 | tf_op jit(solution)/shard_map/ppermute | solution.py:666
  27.3 23.2 %collective-permute-start.11 = (f32[15,8,1024]{2,1,0:T(8,128)}, f32[15,8,1024]{2,1,0:T(8,128)S(1)}, u32[]{:S(2)}, u32[]{:S(2)}) collective-permute-start(f32[15,8,1024]{2,1,0:T(8,128)} %get-tuple-element.48), channel_id=1, source_target_pairs={{0,1},{1,0},{2,3},{3,2},{4,5},{5,4},{6,7},{7,6},{8,9},{9,8},{10,11... | collective-permute-start | bytes 1474568 | tf_op jit(solution)/shard_map/ppermute | solution.py:666
  27.6 22.9 %collective-permute-start.12 = (f32[15,8,1024]{2,1,0:T(8,128)}, f32[15,8,1024]{2,1,0:T(8,128)S(1)}, u32[]{:S(2)}, u32[]{:S(2)}) collective-permute-start(f32[15,8,1024]{2,1,0:T(8,128)} %get-tuple-element.49), channel_id=1, source_target_pairs={{0,4},{1,2},{2,1},{3,7},{4,0},{5,6},{6,5},{7,3},{8,12},{9,10},{10,... | collective-permute-start | bytes 1474568 | tf_op jit(solution)/shard_map/ppermute | solution.py:666
  29.0 20.9 %all-to-all-start.1 = ((f32[16,4,8,128]{3,2,1,0:T(8,128)}), f32[16,4,8,128]{3,2,1,0:T(8,128)S(1)}, u32[]{:S(2)}, u32[]{:S(2)}) async-start(f32[16,4,8,128]{3,2,1,0:T(8,128)} %get-tuple-element.44), calls=%async_computation.1 | async-start | bytes 524288 | tf_op jit(solution)/shard_map/all_to_all | solution.py:720
  40.3 11.6 %collective-permute-start.9 = (f32[4,16,256]{2,1,0:T(8,128)S(1)}, f32[4,16,256]{2,1,0:T(8,128)S(1)}, u32[]{:S(2)}, u32[]{:S(2)}) collective-permute-start(f32[4,16,256]{2,1,0:T(8,128)S(1)} %get-tuple-element.45.f2), channel_id=1, source_target_pairs={{0,4},{1,5},{2,6},{3,7},{4,0},{5,1},{6,2},{7,3},{8,16},{9,17},{10,... | collective-permute-start | bytes 196616 | tf_op jit(solution)/shard_map/ppermute | solution.py:666
  40.4 11.5 %collective-permute-start.8 = (f32[4,16,256]{2,1,0:T(8,128)S(1)}, f32[4,16,256]{2,1,0:T(8,128)S(1)}, u32[]{:S(2)}, u32[]{:S(2)}) collective-permute-start(f32[4,16,256]{2,1,0:T(8,128)S(1)} %get-tuple-element.45.f2), channel_id=1, source_target_pairs={{0,8},{1,9},{2,10},{3,11},{4,12},{5,13},{6,14},{7,15},{8,0},{9,1},... | collective-permute-start | bytes 196616 | tf_op jit(solution)/shard_map/ppermute | solution.py:666
  43.7 8.2 %collective-permute-start.10 = (f32[1,16,256]{2,1,0:T(8,128)S(1)}, f32[1,16,256]{2,1,0:T(8,128)S(1)}, u32[]{:S(2)}, u32[]{:S(2)}) collective-permute-start(f32[1,16,256]{2,1,0:T(8,128)S(1)} %get-tuple-element.46), channel_id=1, source_target_pairs={{0,8},{1,9},{2,10},{3,11},{4,16},{5,17},{6,18},{7,19},{8,0},{9,1},... | collective-permute-start | bytes 49160 | tf_op jit(solution)/shard_map/ppermute | solution.py:666
